TPU v7x, 128 devices: a whole 4x4x4 slice. The times are simulated.
128 devices in a mesh: dev: 128 (over z, y, x, core).
Axes of the slice: x: 4, y: 4, z: 4, core: 2. Of those that a mesh axis runs over, the one named last changes fastest.
Arguments:
- params: float32 [59, 524288], P(None, 'dev'), may hold values from -7000 to 7000, as said below
- cameras: float32 [2, 4, 8], replicated, may hold values from -200 to 3600
- send_lists: int32 [2, 128, 128, 32], P(None, 'dev'), may hold values from 0 to 4095, as said below
- tile_slots: int32 [2, 4096, 256], P(None, 'dev'), may hold values from 0 to 4095, as said below
- tile_ids: int32 [2, 4096], P(None, 'dev'), may hold values from 0 to 129599, as said below
- tile_len: int32 [2, 128, 32], P(None, 'dev'), may hold values from 1 to 256, 4096 in all within a row
- targets: float32 [2, 4096, 3, 256], P(None, 'dev'), may hold values from -4.5 to 5.5
Outputs:
- param_grads: float32 [59, 524288], P(None, 'dev')
- mean_error: float32 [], replicated
Inputs may be any that keep to these rules, and one draw needn't show every extreme that they name: `send_lists`: in each batch, the lists of one owner name each of its 4096 Gaussians exactly once. `tile_slots`: in one batch, the 32 lists of one renderer together name each of its 4096 slots exactly twice, both times in tiles of one view; the first tile_len entries of a list are live. `tile_ids`: the tiles of one batch are distinct. `params`: every Gaussian lies at a depth of 500 or more in front of every camera of both batches; quaternions have a first component of 1 to 2.
All inputs are finite; a program needn't handle non-finite values.
Results may differ from a plain program's by a relative error of at most 0.0003.
Values sent between devices are 32-bit elements; how exact they have to be, the bound alone decides.
No kernel may reach another device: no remote copies, remote signals or barrier semaphores. Data moves between devices by JAX's collectives and lax.ppermute only.
A program may use at most 128 MiB of HBM per device.

v0:
```python
import math

import jax
import jax.numpy as jnp
from jax import lax
from jax.sharding import PartitionSpec as P

BATCHES = 2
TILE = 16
PAIRS = 256
TILE_PX = 256
TILES_X = 240
TILES_VIEW = 32400


SH_ZERO = 0.28209479177387814
SH_ONE = 0.4886025119029199
SH_TWO = (
    1.0925484305920792,
    -1.0925484305920792,
    0.31539156525252005,
    -1.0925484305920792,
    0.5462742152960396,
)
SH_THREE = (
    -0.5900435899266435,
    2.890611442640554,
    -0.4570457994644658,
    0.3731763325901154,
    -0.4570457994644658,
    1.445305721320277,
    -0.5900435899266435,
)


def camera_frame(camera):
    cos_yaw = jnp.cos(camera[0])
    sin_yaw = jnp.sin(camera[0])
    cos_pitch = jnp.cos(camera[1])
    sin_pitch = jnp.sin(camera[1])
    return (
        (cos_yaw, 0.0 * cos_yaw, sin_yaw),
        (sin_pitch * sin_yaw, cos_pitch, -sin_pitch * cos_yaw),
        (-cos_pitch * sin_yaw, sin_pitch, cos_pitch * cos_yaw),
    )


def sh_basis(dir_x, dir_y, dir_z):
    square_x = dir_x * dir_x
    square_y = dir_y * dir_y
    square_z = dir_z * dir_z
    unit_row = jnp.ones_like(dir_x)
    return [
        SH_ZERO * unit_row,
        -SH_ONE * dir_y,
        SH_ONE * dir_z,
        -SH_ONE * dir_x,
        SH_TWO[0] * dir_x * dir_y,
        SH_TWO[1] * dir_y * dir_z,
        SH_TWO[2] * (2.0 * square_z - square_x - square_y),
        SH_TWO[3] * dir_x * dir_z,
        SH_TWO[4] * (square_x - square_y),
        SH_THREE[0] * dir_y * (3.0 * square_x - square_y),
        SH_THREE[1] * dir_x * dir_y * dir_z,
        SH_THREE[2] * dir_y * (4.0 * square_z - square_x - square_y),
        SH_THREE[3] * dir_z * (2.0 * square_z - 3.0 * square_x - 3.0 * square_y),
        SH_THREE[4] * dir_x * (4.0 * square_z - square_x - square_y),
        SH_THREE[5] * dir_z * (square_x - square_y),
        SH_THREE[6] * dir_x * (square_x - 3.0 * square_y),
    ]


def project(columns, camera):
    cam_frame = camera_frame(camera)
    cam_shift = (camera[2], camera[3], camera[4])
    focal_len = camera[5]
    world_pt = (columns[0], columns[1], columns[2])
    viewed = [
        cam_frame[row_i][0] * world_pt[0]
        + cam_frame[row_i][1] * world_pt[1]
        + cam_frame[row_i][2] * world_pt[2]
        + cam_shift[row_i]
        for row_i in range(3)
    ]
    inv_depth = 1.0 / viewed[2]
    screen_u = focal_len * viewed[0] * inv_depth + camera[6]
    screen_v = focal_len * viewed[1] * inv_depth + camera[7]
    quat_len = jnp.sqrt(
        columns[6] * columns[6]
        + columns[7] * columns[7]
        + columns[8] * columns[8]
        + columns[9] * columns[9]
    )
    quat_w = columns[6] / quat_len
    quat_x = columns[7] / quat_len
    quat_y = columns[8] / quat_len
    quat_z = columns[9] / quat_len
    rotation = (
        (
            1.0 - 2.0 * (quat_y * quat_y + quat_z * quat_z),
            2.0 * (quat_x * quat_y - quat_w * quat_z),
            2.0 * (quat_x * quat_z + quat_w * quat_y),
        ),
        (
            2.0 * (quat_x * quat_y + quat_w * quat_z),
            1.0 - 2.0 * (quat_x * quat_x + quat_z * quat_z),
            2.0 * (quat_y * quat_z - quat_w * quat_x),
        ),
        (
            2.0 * (quat_x * quat_z - quat_w * quat_y),
            2.0 * (quat_y * quat_z + quat_w * quat_x),
            1.0 - 2.0 * (quat_x * quat_x + quat_y * quat_y),
        ),
    )
    spread = (jnp.exp(columns[3]), jnp.exp(columns[4]), jnp.exp(columns[5]))
    shaped = [
        [
            (
                cam_frame[row_i][0] * rotation[0][col_j]
                + cam_frame[row_i][1] * rotation[1][col_j]
                + cam_frame[row_i][2] * rotation[2][col_j]
            )
            * spread[col_j]
            for col_j in range(3)
        ]
        for row_i in range(3)
    ]
    jac_main = focal_len * inv_depth
    jac_u = -focal_len * viewed[0] * inv_depth * inv_depth
    jac_v = -focal_len * viewed[1] * inv_depth * inv_depth
    along_u = [jac_main * shaped[0][col_j] + jac_u * shaped[2][col_j] for col_j in range(3)]
    along_v = [jac_main * shaped[1][col_j] + jac_v * shaped[2][col_j] for col_j in range(3)]
    cov_uu = along_u[0] * along_u[0] + along_u[1] * along_u[1] + along_u[2] * along_u[2] + 0.3
    cov_uv = along_u[0] * along_v[0] + along_u[1] * along_v[1] + along_u[2] * along_v[2]
    cov_vv = along_v[0] * along_v[0] + along_v[1] * along_v[1] + along_v[2] * along_v[2] + 0.3
    determinant = cov_uu * cov_vv - cov_uv * cov_uv
    centre = [
        -(
            cam_frame[0][row_i] * cam_shift[0]
            + cam_frame[1][row_i] * cam_shift[1]
            + cam_frame[2][row_i] * cam_shift[2]
        )
        for row_i in range(3)
    ]
    ray_dir = [world_pt[row_i] - centre[row_i] for row_i in range(3)]
    ray_len = jnp.sqrt(ray_dir[0] * ray_dir[0] + ray_dir[1] * ray_dir[1] + ray_dir[2] * ray_dir[2])
    sh_values = sh_basis(ray_dir[0] / ray_len, ray_dir[1] / ray_len, ray_dir[2] / ray_len)
    colors = []
    for channel in range(3):
        shaded = 0.5
        for sh_term in range(16):
            shaded = shaded + sh_values[sh_term] * columns[11 + 16 * channel + sh_term]
        colors.append(shaded)
    return jnp.stack(
        [
            screen_u,
            screen_v,
            cov_vv / determinant,
            -cov_uv / determinant,
            cov_uu / determinant,
            jax.nn.sigmoid(columns[10]),
        ]
        + colors
    )


def tile_pixels(tile_id):
    in_view = tile_id % TILES_VIEW
    row_t = in_view // TILES_X
    col_t = in_view % TILES_X
    pixel_no = jnp.arange(TILE_PX, dtype=jnp.int32)
    pix_u = (col_t * TILE + pixel_no % TILE).astype(jnp.float32) + 0.5
    pix_v = (row_t * TILE + pixel_no // TILE).astype(jnp.float32) + 0.5
    return (pix_u, pix_v)


def tile_error(features, live_mask, pix_u, pix_v, target, upper_ones):
    off_u = pix_u[:, None] - features[0][None, :]
    off_v = pix_v[:, None] - features[1][None, :]
    exponent = (
        -0.5 * (features[2] * off_u * off_u + features[4] * off_v * off_v)
        - features[3] * off_u * off_v
    )
    alphas = features[5] * jnp.exp(exponent) * live_mask
    keep_log = jnp.log1p(-alphas)
    before = jnp.dot(keep_log, upper_ones, precision=lax.Precision.HIGHEST)
    weight = jnp.exp(before) * alphas
    pixel_color = jnp.einsum("cp,xp->cx", features[6:9], weight, precision=lax.Precision.HIGHEST)
    residual = pixel_color - target
    return jnp.sum(residual * residual)


def local(params, cameras, send_lists, tile_slots, tile_ids, tile_len, targets):
    owners = lax.axis_size("dev")
    tiles_dev = tile_ids.shape[1]
    slot_cap = send_lists.shape[3]
    slots_dev = owners * slot_cap
    param_rows = params.shape[0]
    tile_group = math.gcd(tiles_dev, max(1, 512 // TILE_PX))
    block_count = tiles_dev // tile_group
    pair_pos = jnp.arange(PAIRS, dtype=jnp.int32)
    upper_ones = (pair_pos[:, None] < pair_pos[None, :]).astype(jnp.float32)
    grad_sum = jnp.zeros(params.shape, jnp.float32)
    error_sum = jnp.zeros((), jnp.float32)
    for batch_no in range(BATCHES):
        send_picked = send_lists[batch_no, 0].reshape(slots_dev)
        picked_cols = params[:, send_picked]
        send_arrived = lax.all_to_all(
            picked_cols.reshape(param_rows, owners, slot_cap),
            "dev",
            split_axis=1,
            concat_axis=1,
            tiled=True,
        )
        arrived = send_arrived.reshape(param_rows, slots_dev)
        batch_cams = cameras[batch_no]
        arrived_rows = arrived.shape[0]

        def one_tile(tile_items):
            pair_slots, tile_id, length, target = tile_items
            view_no = tile_id // TILES_VIEW
            pix_u, pix_v = tile_pixels(tile_id)
            live_mask = (pair_pos < length).astype(jnp.float32)
            camera = batch_cams[view_no]

            def tile_loss(columns):
                return tile_error(
                    project(columns, camera), live_mask, pix_u, pix_v, target, upper_ones
                )

            return jax.value_and_grad(tile_loss)(arrived[:, pair_slots])

        def tile_block(tile_items):
            return jax.vmap(one_tile)(tile_items)

        tile_items = (
            tile_slots[batch_no].reshape(block_count, tile_group, PAIRS),
            tile_ids[batch_no].reshape(block_count, tile_group),
            tile_len[batch_no, 0].reshape(block_count, tile_group),
            targets[batch_no].reshape(block_count, tile_group, 3, TILE_PX),
        )
        errors, col_grads = lax.map(tile_block, tile_items)
        col_grads = col_grads.reshape(tiles_dev, arrived_rows, PAIRS)
        flat_grads = jnp.transpose(col_grads, (1, 0, 2)).reshape(arrived_rows, tiles_dev * PAIRS)
        render_slot_grads = (
            jnp.zeros((arrived_rows, slots_dev), jnp.float32)
            .at[:, tile_slots[batch_no].reshape(tiles_dev * PAIRS)]
            .add(flat_grads)
        )
        batch_error = jnp.sum(errors)
        error_sum = error_sum + batch_error
        returned = lax.all_to_all(
            render_slot_grads.reshape(param_rows, owners, slot_cap),
            "dev",
            split_axis=1,
            concat_axis=1,
            tiled=True,
        )
        row_grads = returned.reshape(param_rows, slots_dev)
        grad_sum = grad_sum.at[:, send_picked].add(row_grads)
    every_error = lax.psum(error_sum, "dev")
    mean_error = every_error / (BATCHES * owners * tiles_dev * 3 * TILE_PX)
    return (grad_sum, mean_error)


def solution(mesh):
    placed = (
        P(None, "dev"),
        P(),
        P(None, "dev", None, None),
        P(None, "dev", None),
        P(None, "dev"),
        P(None, "dev", None),
        P(None, "dev", None, None),
    )
    return jax.shard_map(
        local, mesh=mesh, in_specs=placed, out_specs=(P(None, "dev"), P()), check_vma=False
    )
```

profile of v0, /device:TPU:1, one launch (start us, length us, event | category | flops | bytes accessed | tf_op | source)
XLA Modules:
  0.0 877.7 jit_solution(12152047439159508131)
XLA Ops:
  3.5 14.1 %gather_fusion.4 = f32[4096,59]{1,0:T(8,128)} fusion(f32[59,4096]{0,1:T(8,128)S(1)} %copy.21, s32[4096]{0:T(1024)S(1)} %broadcast_clamp_fusion.1), kind=kCustom, calls=%fused_computation.4 | custom fusion | bytes 1949696 | tf_op jit(solution)/shard_map/gather | solution.py:207
  17.6 5.5 reshape.17436
  23.1 11.5 %all-to-all-start = ((f32[128,1,1888]{2,1,0:T(1,128)}), f32[128,1,1888]{2,1,0:T(1,128)S(1)}, u32[]{:S(2)}, u32[]{:S(2)}) async-start(f32[128,1,1888]{2,1,0:T(1,128)} %reshape.17436), calls=%async_computation | async-start | bytes 1966080 | tf_op jit(solution)/shard_map/all_to_all | solution.py:208
  39.6 14.1 %gather_fusion.5 = f32[4096,59]{1,0:T(8,128)} fusion(f32[59,4096]{0,1:T(8,128)S(1)} %copy.21, s32[4096]{0:T(1024)S(1)} %broadcast_clamp_fusion), kind=kCustom, calls=%fused_computation.5 | custom fusion | bytes 1949696 | tf_op jit(solution)/shard_map/gather | solution.py:207
  53.7 5.4 reshape.17440
  62.1 10.3 %all-to-all-start.2 = ((f32[128,1,1888]{2,1,0:T(1,128)}), f32[128,1,1888]{2,1,0:T(1,128)S(1)}, u32[]{:S(2)}, u32[]{:S(2)}) async-start(f32[128,1,1888]{2,1,0:T(1,128)} %reshape.17440), calls=%async_computation.2 | async-start | bytes 1966080 | tf_op jit(solution)/shard_map/all_to_all | solution.py:208
  73.1 5.2 reduce.92
  78.2 4.2 reshape.17437
  84.0 247.1 %while.34 = (s32[]{:T(128)}, f32[16,2]{1,0:T(8,128)S(1)}, f32[16,2,59,256]{3,2,1,0:T(8,128)}, s32[16,2,256]{2,1,0:T(2,128)}, f32[59,4096]{0,1:T(8,128)S(1)}, /*i...) while((s32[]{:T(128)}, f32[16,2]{1,0:T(8,128)S(1)}, ...), condition=%wide.region_8.9_spmd.clone.clone, body=%wide.region_0.8_spmd.clone.clone.sunk | while | flops 835955328 | bytes 9399585 | solution.py:242
  335.2 44.8 %scatter_custom_fusion = f32[59,4096]{0,1:T(8,128)S(1)} fusion(s32[8192]{0:T(1024)} %bitcast.1245, f32[8192,59]{1,0:T(8,128)} %bitcast.1183, f32[]{:T(128)} %constant.496.clone.1), kind=kCustom, calls=%fused_computation.998 | custom fusion | flops 483328 | bytes 967168 | tf_op jit(solution)/shard_map/scatter-add | solution.py:248
  380.0 4.3 reshape.17438
  385.3 9.8 %all-to-all-start.1 = ((f32[128,1,1888]{2,1,0:T(1,128)}), f32[128,1,1888]{2,1,0:T(1,128)S(1)}, u32[]{:S(2)}, u32[]{:S(2)}) async-start(f32[128,1,1888]{2,1,0:T(1,128)} %reshape.17438), calls=%async_computation.1 | async-start | bytes 1966080 | tf_op jit(solution)/shard_map/all_to_all | solution.py:252
  395.0 5.2 reduce.94
  400.2 4.2 reshape.17441
  406.6 272.5 %while.35 = (s32[]{:T(128)}, f32[16,2]{1,0:T(8,128)}, f32[16,2,59,256]{3,2,1,0:T(8,128)}, s32[16,2,256]{2,1,0:T(2,128)}, f32[59,4096]{0,1:T(8,128)S(1)}, /*index...) while((s32[]{:T(128)}, f32[16,2]{1,0:T(8,128)}, ...), condition=%wide.region_19.20_spmd.clone.clone, body=%wide.region_11.19_spmd.clone.clone.sunk | while | flops 835955328 | bytes 9399585 | solution.py:242
  679.1 4.2 copy.27
  683.3 44.8 %scatter_custom_fusion.2 = f32[59,4096]{0,1:T(8,128)S(1)} fusion(s32[8192]{0:T(1024)} %bitcast.1244, f32[8192,59]{1,0:T(8,128)} %bitcast.1184, f32[]{:T(128)} %constant.496.clone.1), kind=kCustom, calls=%fused_computation.994 | custom fusion | flops 483328 | bytes 967168 | tf_op jit(solution)/shard_map/scatter-add | solution.py:248
  728.2 4.3 reshape.17442
  732.5 9.8 %all-to-all-start.3 = ((f32[128,1,1888]{2,1,0:T(1,128)}), f32[128,1,1888]{2,1,0:T(1,128)S(1)}, u32[]{:S(2)}, u32[]{:S(2)}) async-start(f32[128,1,1888]{2,1,0:T(1,128)} %reshape.17442), calls=%async_computation.3 | async-start | bytes 1966080 | tf_op jit(solution)/shard_map/all_to_all | solution.py:252
  744.8 67.8 %psum.7 = f32[]{:T(128)} all-reduce(f32[]{:T(128)S(6)} %add.6849), channel_id=1, replica_groups=mesh['dev'=128] {'dev'}, use_global_device_ids=true, to_apply=%region_24.25 | all-reduce | flops 1 | bytes 8 | tf_op jit(solution)/shard_map/psum | solution.py:261
  816.2 4.5 reshape.17439
  823.7 4.4 reshape.17443
  828.2 23.2 %scatter_custom_fusion.1 = f32[59,4096]{0,1:T(8,128)S(1)} fusion(s32[4096]{0:T(1024)} %bitcast.1195, f32[4096,59]{1,0:T(8,128)} %bitcast.1185, f32[]{:T(128)} %constant.496.clone.1), kind=kCustom, calls=%fused_computation.996 | custom fusion | flops 241664 | bytes 967168 | tf_op jit(solution)/shard_map/scatter-add | solution.py:260
  851.3 23.4 %scatter_fusion = f32[59,4096]{0,1:T(8,128)S(1)} fusion(f32[59,4096]{0,1:T(8,128)S(1)} %scatter_custom_fusion.1, s32[4096]{0:T(1024)S(1)} %bitcast.1189, f32[4096,59]{1,0:T(8,128)} %bitcast.1180), kind=kCustom, calls=%fused_computation.9 | custom fusion | flops 241664 | bytes 2916352 | tf_op jit(solution)/shard_map/scatter-add | solution.py:260
  (2268 shorter events, 538.7 us)
Async XLA Ops:
  1.6 16.0 %copy-start.4 = (s32[4096,1]{0,1:T(1,128)}, s32[4096,1]{0,1:T(1,128)S(1)}, u32[]{:S(2)}) copy-start(s32[4096,1]{0,1:T(1,128)S(1)} %compare_select_fusion.7) | copy-start | bytes 49156
  17.6 17.0 %copy-start.3 = (s32[2,32,256]{2,1,0:T(8,128)S(1)}, s32[2,32,256]{2,1,0:T(8,128)}, u32[]{:S(2)}) copy-start(s32[2,32,256]{2,1,0:T(8,128)} %param.14) | copy-start | bytes 196612
  17.6 18.3 %copy-start.7 = (s32[2,32]{1,0:T(2,128)S(1)}, s32[2,32]{1,0:T(2,128)}, u32[]{:S(2)}) copy-start(s32[2,32]{1,0:T(2,128)} %param.15) | copy-start | bytes 772
  17.6 19.0 %copy-start.8 = (s32[2,1,32]{2,1,0:T(1,128)S(1)}, s32[2,1,32]{2,1,0:T(1,128)}, u32[]{:S(2)}) copy-start(s32[2,1,32]{2,1,0:T(1,128)} %param.16) | copy-start | bytes 772
  17.6 19.7 %copy-start.2 = (f32[2,32,3,256]{3,1,2,0:T(8,128)S(1)}, f32[2,32,3,256]{3,1,2,0:T(8,128)}, u32[]{:S(2)}) copy-start(f32[2,32,3,256]{3,1,2,0:T(8,128)} %param.17) | copy-start | bytes 589828
  23.1 38.1 %all-to-all-start = ((f32[128,1,1888]{2,1,0:T(1,128)}), f32[128,1,1888]{2,1,0:T(1,128)S(1)}, u32[]{:S(2)}, u32[]{:S(2)}) async-start(f32[128,1,1888]{2,1,0:T(1,128)} %reshape.17436), calls=%async_computation | async-start | bytes 1966080 | tf_op jit(solution)/shard_map/all_to_all | solution.py:208
  53.7 7.5 copy-start.6
  62.1 322.1 %all-to-all-start.2 = ((f32[128,1,1888]{2,1,0:T(1,128)}), f32[128,1,1888]{2,1,0:T(1,128)S(1)}, u32[]{:S(2)}, u32[]{:S(2)}) async-start(f32[128,1,1888]{2,1,0:T(1,128)} %reshape.17440), calls=%async_computation.2 | async-start | bytes 1966080 | tf_op jit(solution)/shard_map/all_to_all | solution.py:208
  93.6 3.0 copy-start.10
  109.0 3.0 copy-start.10
  124.4 3.0 copy-start.10
  139.9 3.0 copy-start.10
  155.3 3.0 copy-start.10
  170.8 3.0 copy-start.10
  186.2 3.0 copy-start.10
  201.7 3.0 copy-start.10
  217.1 3.0 copy-start.10
  232.5 3.0 copy-start.10
  248.0 3.0 copy-start.10
  278.9 3.0 copy-start.10
  325.2 3.0 copy-start.10
  385.3 347.3 %all-to-all-start.1 = ((f32[128,1,1888]{2,1,0:T(1,128)}), f32[128,1,1888]{2,1,0:T(1,128)S(1)}, u32[]{:S(2)}, u32[]{:S(2)}) async-start(f32[128,1,1888]{2,1,0:T(1,128)} %reshape.17438), calls=%async_computation.1 | async-start | bytes 1966080 | tf_op jit(solution)/shard_map/all_to_all | solution.py:252
  728.1 14.7 %copy-start.5 = (f32[16,2]{1,0:T(8,128)S(1)}, f32[16,2]{1,0:T(8,128)}, u32[]{:S(2)}) copy-start(f32[16,2]{1,0:T(8,128)} %get-tuple-element.397) | copy-start | bytes 388
  732.5 88.2 %all-to-all-start.3 = ((f32[128,1,1888]{2,1,0:T(1,128)}), f32[128,1,1888]{2,1,0:T(1,128)S(1)}, u32[]{:S(2)}, u32[]{:S(2)}) async-start(f32[128,1,1888]{2,1,0:T(1,128)} %reshape.17442), calls=%async_computation.3 | async-start | bytes 1966080 | tf_op jit(solution)/shard_map/all_to_all | solution.py:252
  (53 other events, 105.0 us)
where the time goes:
time: 892 us; the launch traced here: 878 us
  other arithmetic  339 us (38%)
  matrix products  220 us (25%)
  local copies, waits for them, and re-layouts  195 us (22%)
  blocking collectives  67.8 us (8%)
  starting transfers between devices  41.4 us (5%)
  loops' own time  9.9 us (1%)
    dot_general x64, matrix products, tile_error(): before = jnp.dot(keep_log, upper_ones, precision=lax.Precision.HIGHEST)  124 us
    dot_general x96, matrix products, tile_error(): jnp.einsum('cp,xp->cx', features[6:9], weight, precision=lax.Precision.HI...  96 us
    scatter-add x2, other arithmetic, local(): render_slot_grads = jnp.zeros((arrived_rows, slots_dev), jnp.float32).at[...  89.6 us
    psum x1, blocking collectives, local(): every_error = lax.psum(error_sum, 'dev')  67.8 us
    scatter-add x2, other arithmetic, local(): grad_sum = grad_sum.at[:, send_picked].add(row_grads)  46.6 us
    unnamed x30, local copies, waits for them, and re-layouts  42.3 us
    gather x64, local copies, waits for them, and re-layouts, one_tile(): return jax.value_and_grad(tile_loss)(arrived[:, pair_slots])  37.2 us
    dynamic_update_slice x32, other arithmetic, local(): errors, col_grads = lax.map(tile_block, tile_items)  33.7 us
  transfers between devices with their start and end apart: 4, of which 0 were waited for; matrix products, arithmetic and copies ran while one was open for 76% of the time, Pallas kernels for 0%

commit v1 on v0

v1 whole, which is shorter than its diff:
```python
import functools

import jax
import jax.numpy as jnp
from jax import lax
from jax.experimental import pallas as pl
from jax.experimental.pallas import tpu as pltpu
from jax.sharding import PartitionSpec as P

BATCHES = 2
TILE = 16
PAIRS = 256
TILE_PX = 256
TILES_X = 240
TILES_VIEW = 32400
VIEWS = 4
PARAMS = 59
TILES_DEV = 32
OWNERS = 128
CAP = 32
SLOTS = 4096
GROUPS = 4
LOG2_E = 1.4426950408889634
VMEM_BYTES = 56 * 1024 * 1024

SH_ZERO = 0.28209479177387814
SH_ONE = 0.4886025119029199
SH_TWO = (
    1.0925484305920792,
    -1.0925484305920792,
    0.31539156525252005,
    -1.0925484305920792,
    0.5462742152960396,
)
SH_THREE = (
    -0.5900435899266435,
    2.890611442640554,
    -0.4570457994644658,
    0.3731763325901154,
    -0.4570457994644658,
    1.445305721320277,
    -0.5900435899266435,
)

F32 = jnp.float32
BF16 = jnp.bfloat16
NN = (((1,), (0,)), ((), ()))
NT = (((1,), (1,)), ((), ()))
TN = (((0,), (0,)), ((), ()))


def dot(lhs, rhs, dims):
    return lax.dot_general(lhs, rhs, dims, preferred_element_type=F32)


def split2(value):
    high = value.astype(BF16).astype(F32)
    return high, value - high


def camera_table(cameras):
    cos_yaw = jnp.cos(cameras[:, :, 0])
    sin_yaw = jnp.sin(cameras[:, :, 0])
    cos_pitch = jnp.cos(cameras[:, :, 1])
    sin_pitch = jnp.sin(cameras[:, :, 1])
    frame = [
        cos_yaw,
        sin_yaw,
        sin_pitch * sin_yaw,
        cos_pitch,
        -sin_pitch * cos_yaw,
        -cos_pitch * sin_yaw,
        sin_pitch,
        cos_pitch * cos_yaw,
    ]
    shift = [cameras[:, :, 2], cameras[:, :, 3], cameras[:, :, 4]]
    centre = [
        -(frame[0] * shift[0] + frame[2] * shift[1] + frame[5] * shift[2]),
        -(frame[3] * shift[1] + frame[6] * shift[2]),
        -(frame[1] * shift[0] + frame[4] * shift[1] + frame[7] * shift[2]),
    ]
    rest = [cameras[:, :, 5], cameras[:, :, 6], cameras[:, :, 7]]
    return jnp.stack(frame + shift + centre + rest)


CAM_ROWS = 17


def sh_basis(dir_x, dir_y, dir_z):
    square_x = dir_x * dir_x
    square_y = dir_y * dir_y
    square_z = dir_z * dir_z
    return [
        SH_ZERO * jnp.ones_like(dir_x),
        -SH_ONE * dir_y,
        SH_ONE * dir_z,
        -SH_ONE * dir_x,
        SH_TWO[0] * dir_x * dir_y,
        SH_TWO[1] * dir_y * dir_z,
        SH_TWO[2] * (2.0 * square_z - square_x - square_y),
        SH_TWO[3] * dir_x * dir_z,
        SH_TWO[4] * (square_x - square_y),
        SH_THREE[0] * dir_y * (3.0 * square_x - square_y),
        SH_THREE[1] * dir_x * dir_y * dir_z,
        SH_THREE[2] * dir_y * (4.0 * square_z - square_x - square_y),
        SH_THREE[3] * dir_z * (2.0 * square_z - 3.0 * square_x - 3.0 * square_y),
        SH_THREE[4] * dir_x * (4.0 * square_z - square_x - square_y),
        SH_THREE[5] * dir_z * (square_x - square_y),
        SH_THREE[6] * dir_x * (square_x - 3.0 * square_y),
    ]


def project_geometry(cols, cam):
    zero = jnp.zeros_like(cam[0])
    frame = ((cam[0], zero, cam[1]), (cam[2], cam[3], cam[4]), (cam[5], cam[6], cam[7]))
    shift = cam[8:11]
    focal = cam[14]
    viewed = [
        frame[0][0] * cols[0] + frame[0][2] * cols[2] + shift[0],
        frame[1][0] * cols[0] + frame[1][1] * cols[1] + frame[1][2] * cols[2] + shift[1],
        frame[2][0] * cols[0] + frame[2][1] * cols[1] + frame[2][2] * cols[2] + shift[2],
    ]
    inv_depth = 1.0 / viewed[2]
    screen_u = focal * viewed[0] * inv_depth + cam[15]
    screen_v = focal * viewed[1] * inv_depth + cam[16]
    inv_quat = 1.0 / jnp.sqrt(
        cols[6] * cols[6] + cols[7] * cols[7] + cols[8] * cols[8] + cols[9] * cols[9]
    )
    quat_w, quat_x, quat_y, quat_z = [cols[6 + i] * inv_quat for i in range(4)]
    rotation = (
        (
            1.0 - 2.0 * (quat_y * quat_y + quat_z * quat_z),
            2.0 * (quat_x * quat_y - quat_w * quat_z),
            2.0 * (quat_x * quat_z + quat_w * quat_y),
        ),
        (
            2.0 * (quat_x * quat_y + quat_w * quat_z),
            1.0 - 2.0 * (quat_x * quat_x + quat_z * quat_z),
            2.0 * (quat_y * quat_z - quat_w * quat_x),
        ),
        (
            2.0 * (quat_x * quat_z - quat_w * quat_y),
            2.0 * (quat_y * quat_z + quat_w * quat_x),
            1.0 - 2.0 * (quat_x * quat_x + quat_y * quat_y),
        ),
    )
    spread = [jnp.exp(cols[3 + i]) for i in range(3)]
    jac_main = focal * inv_depth
    jac_u = -jac_main * viewed[0] * inv_depth
    jac_v = -jac_main * viewed[1] * inv_depth
    row_u = [
        jac_main * frame[0][0] + jac_u * frame[2][0],
        jac_u * frame[2][1],
        jac_main * frame[0][2] + jac_u * frame[2][2],
    ]
    row_v = [jac_main * frame[1][i] + jac_v * frame[2][i] for i in range(3)]
    along_u = [
        (row_u[0] * rotation[0][j] + row_u[1] * rotation[1][j] + row_u[2] * rotation[2][j])
        * spread[j]
        for j in range(3)
    ]
    along_v = [
        (row_v[0] * rotation[0][j] + row_v[1] * rotation[1][j] + row_v[2] * rotation[2][j])
        * spread[j]
        for j in range(3)
    ]
    cov_uu = along_u[0] * along_u[0] + along_u[1] * along_u[1] + along_u[2] * along_u[2] + 0.3
    cov_uv = along_u[0] * along_v[0] + along_u[1] * along_v[1] + along_u[2] * along_v[2]
    cov_vv = along_v[0] * along_v[0] + along_v[1] * along_v[1] + along_v[2] * along_v[2] + 0.3
    inv_det = 1.0 / (cov_uu * cov_vv - cov_uv * cov_uv)
    return screen_u, screen_v, cov_vv * inv_det, -cov_uv * inv_det, cov_uu * inv_det


def ray_basis(position, cam):
    ray = [position[i] - cam[11 + i] for i in range(3)]
    inv_len = 1.0 / jnp.sqrt(ray[0] * ray[0] + ray[1] * ray[1] + ray[2] * ray[2])
    return sh_basis(ray[0] * inv_len, ray[1] * inv_len, ray[2] * inv_len)


def pick_camera(cam_ref, batch_no, view):
    picked = []
    for row in range(CAM_ROWS):
        value = jnp.full(view.shape, cam_ref[row, batch_no, VIEWS - 1], F32)
        for view_no in range(VIEWS - 2, -1, -1):
            value = jnp.where(view == view_no, cam_ref[row, batch_no, view_no], value)
        picked.append(value)
    return picked


def view_kernel(ids_ref, slots_ref, out_ref):
    row_own = lax.broadcasted_iota(jnp.int32, (OWNERS, PAIRS), 0)
    row_cap = lax.broadcasted_iota(jnp.int32, (CAP, PAIRS), 0)

    def step(tile_no, sums):
        out = []
        for batch_no in range(BATCHES):
            view = (ids_ref[batch_no, tile_no] // TILES_VIEW).astype(F32) * 0.5
            slots = slots_ref[batch_no, pl.ds(tile_no, 1), :]
            lhs = jnp.where(row_own == (slots >> 5), view, 0.0).astype(BF16)
            rhs = jnp.where(row_cap == (slots & 31), 1.0, 0.0).astype(BF16)
            out.append(sums[batch_no] + dot(lhs, rhs, NT))
        return tuple(out)

    zero = jnp.zeros((OWNERS, CAP), F32)
    sums = lax.fori_loop(0, TILES_DEV, step, (zero, zero))
    for batch_no in range(BATCHES):
        out_ref[:, batch_no * CAP : (batch_no + 1) * CAP] = sums[batch_no]


def scatter_rhs(index):
    row = lax.broadcasted_iota(jnp.int32, (256, index.shape[1]), 0)
    return jnp.where(row == (index & 255), 1.0, 0.0).astype(BF16)


def project_kernel(cam_ref, params_ref, view_ref, send_ref, out_ref, vg_ref, tab_ref):
    row_a = lax.broadcasted_iota(jnp.int32, (16, 256), 0)

    for batch_no in range(BATCHES):

        def place(chunk, total, batch_no=batch_no):
            index = send_ref[batch_no, pl.ds(chunk, 1), :]
            view = view_ref[batch_no, pl.ds(chunk, 1), :]
            lhs = jnp.where(row_a == (index >> 8), view, 0.0).astype(BF16)
            return total + dot(lhs, scatter_rhs(index), NT)

        vg_ref[batch_no] = lax.fori_loop(0, 16, place, jnp.zeros((16, 256), F32))

    def block(block_no, carry):
        row0 = pl.multiple_of((block_no // 2) * 8, 8)
        half = block_no % 2
        lane0 = pl.multiple_of(half * 128, 128)
        cols = [params_ref[p, pl.ds(row0, 8), pl.ds(lane0, 128)] for p in range(PARAMS)]
        opac = -(jnp.maximum(-cols[10], 0.0) + jnp.log1p(jnp.exp(-jnp.abs(cols[10]))))
        for batch_no in range(BATCHES):
            view = vg_ref[batch_no, pl.ds(row0, 8), pl.ds(lane0, 128)]
            cam = pick_camera(cam_ref, batch_no, view)
            feats = list(project_geometry(cols, cam)) + [opac]
            basis = ray_basis(cols[0:3], cam)
            for channel in range(3):
                shade = 0.5
                for term in range(16):
                    shade = shade + basis[term] * cols[11 + 16 * channel + term]
                feats.append(shade)
            for f, value in enumerate(feats):
                start = (2 * row0 + half) * 16 + f
                tab_ref[batch_no, pl.ds(start, 8, stride=32), :] = value
        return carry

    lax.fori_loop(0, 4, block, 0)

    for batch_no in range(BATCHES):

        def pick(chunk, carry, batch_no=batch_no):
            both = send_ref[batch_no, pl.ds(chunk, 1), :]
            for half in range(2):
                index = jnp.broadcast_to(both[:, half * 128 : half * 128 + 128], (8, 128))
                low = index & 127
                high = index >> 7
                acc0 = jnp.zeros((8, 128), F32)
                acc1 = jnp.zeros((8, 128), F32)
                for h in range(32):
                    hit = high == h
                    got0 = jnp.take_along_axis(
                        tab_ref[batch_no, h * 16 : h * 16 + 8, :], low, axis=1,
                        mode="promise_in_bounds",
                    )
                    got1 = jnp.take_along_axis(
                        tab_ref[batch_no, h * 16 + 8 : h * 16 + 16, :], low, axis=1,
                        mode="promise_in_bounds",
                    )
                    acc0 = jnp.where(hit, got0, acc0)
                    acc1 = jnp.where(hit, got1, acc1)
                lane = pl.multiple_of(chunk * 256 + half * 128, 128)
                out_ref[batch_no, 0:8, pl.ds(lane, 128)] = acc0
                out_ref[batch_no, 8:9, pl.ds(lane, 128)] = acc1[0:1]
            return carry

        lax.fori_loop(0, 16, pick, 0)


def blend_kernel(
    order_ref, ids_ref, len_ref, feat_ref, slots_ref, target_ref, out_ref,
    sl_ref, tg_ref, fe_ref, cm_ref, ix_ref, al_ref, w_ref, wh_ref, wl_ref,
):
    lane = lax.broadcasted_iota(jnp.int32, (8, 128), 1)
    sub = lax.broadcasted_iota(jnp.int32, (8, 128), 0)
    diag = sub == (lane & 7)
    lane_k = lane >> 3
    row_a = lax.broadcasted_iota(jnp.int32, (16, 128), 0)
    pix = lax.broadcasted_iota(jnp.int32, (8, 256), 1)
    term = lax.broadcasted_iota(jnp.int32, (8, 256), 0)
    px = (pix & 15).astype(F32) - 7.5
    py = (pix >> 4).astype(F32) - 7.5
    basis = jnp.where(
        term == 0, px * px,
        jnp.where(
            term == 1, px * py,
            jnp.where(
                term == 2, py * py,
                jnp.where(term == 3, px, jnp.where(term == 4, py, jnp.where(term == 5, 1.0, 0.0))),
            ),
        ),
    )
    basis_b = jnp.concatenate([basis] * 4, axis=0).astype(BF16)
    basis_2 = jnp.concatenate([jnp.concatenate([basis, basis], axis=1)] * 2, axis=0).astype(BF16)
    zero8 = jnp.zeros((8, 128), F32)

    for batch_no in range(BATCHES):
        out_ref[batch_no] = jnp.zeros((160, 256), F32)

        def group(group_no, err, batch_no=batch_no):
            longest = jnp.int32(0)
            cx = zero8
            cy = zero8
            length = jnp.zeros((8, 128), jnp.int32)
            for t in range(8):
                tile = order_ref[batch_no, group_no * 8 + t]
                in_view = lax.rem(ids_ref[batch_no, tile], TILES_VIEW)
                row_t = lax.div(in_view, TILES_X)
                col_t = in_view - row_t * TILES_X
                tile_len = len_ref[batch_no, tile]
                longest = jnp.maximum(longest, tile_len)
                here = (lane & 7) == t
                cx = jnp.where(here, (col_t * TILE + 8).astype(F32), cx)
                cy = jnp.where(here, (row_t * TILE + 8).astype(F32), cy)
                length = jnp.where(here, tile_len, length)
                sl_ref[t : t + 1, :] = slots_ref[batch_no, pl.ds(tile, 1), :]
                for channel in range(3):
                    tg_ref[channel * 8 + t : channel * 8 + t + 1, :] = target_ref[
                        batch_no, pl.ds(tile, 1), channel, :
                    ]
            chunks = (longest + 15) // 16

            def forward(j, carry):
                through, colour = carry
                half = pl.multiple_of((j // 8) * 128, 128)
                picked = jnp.take_along_axis(
                    sl_ref[:, pl.ds(half, 128)], lane_k + (j % 8) * 16, axis=1,
                    mode="promise_in_bounds",
                )
                picked = jnp.sum(jnp.where(diag, picked.astype(F32), 0.0), axis=0, keepdims=True)
                index = jnp.broadcast_to(picked.astype(jnp.int32), (8, 128))
                low = index & 127
                high = index >> 7
                acc0 = zero8
                acc1 = zero8
                for h in range(32):
                    hit = high == h
                    got0 = jnp.take_along_axis(
                        feat_ref[batch_no, 0:8, h * 128 : h * 128 + 128], low, axis=1,
                        mode="promise_in_bounds",
                    )
                    got1 = jnp.take_along_axis(
                        feat_ref[batch_no, 8:16, h * 128 : h * 128 + 128], low, axis=1,
                        mode="promise_in_bounds",
                    )
                    acc0 = jnp.where(hit, got0, acc0)
                    acc1 = jnp.where(hit, got1, acc1)
                ix_ref[pl.ds(j, 1), :] = index[0:1]
                u = acc0[0:1] - cx[0:1]
                v = acc0[1:2] - cy[0:1]
                con_a = acc0[2:3]
                con_b = acc0[3:4]
                con_c = acc0[4:5]
                live = (lane_k[0:1] + j * 16) < length[0:1]
                coefs = [
                    con_a * (-0.5 * LOG2_E),
                    con_b * -LOG2_E,
                    con_c * (-0.5 * LOG2_E),
                    (con_a * u + con_b * v) * LOG2_E,
                    (con_b * u + con_c * v) * LOG2_E,
                    jnp.where(
                        live,
                        (acc0[5:6] - 0.5 * (con_a * u * u + con_c * v * v) - con_b * u * v) * LOG2_E,
                        -1e30,
                    ),
                ]
                fe_ref[j] = jnp.concatenate(
                    [u, v, con_a, con_b, con_c, acc0[5:6], jnp.zeros((2, 128), F32)], axis=0
                )
                coef = jnp.concatenate(coefs + [jnp.zeros((2, 128), F32)], axis=0)
                hi, rest = split2(coef)
                mid, lo = split2(rest)
                lhs = jnp.concatenate([hi, mid, lo, zero8], axis=0).astype(BF16)
                alphas = jnp.exp2(dot(lhs, basis_b, TN))
                row0 = pl.multiple_of(j * 128, 128)
                al_ref[pl.ds(row0, 128), :] = alphas
                weights = []
                for k in range(16):
                    weight = through * alphas[k * 8 : k * 8 + 8]
                    through = through - weight
                    weights.append(weight)
                weight = jnp.concatenate(weights, axis=0)
                w_ref[pl.ds(row0, 128), :] = weight
                w_hi, w_lo = split2(weight)
                w_hi = w_hi.astype(BF16)
                w_lo = w_lo.astype(BF16)
                wh_ref[pl.ds(row0, 128), :] = w_hi
                wl_ref[pl.ds(row0, 128), :] = w_lo
                cmat = jnp.concatenate(
                    [
                        jnp.where(diag, acc0[6:7], 0.0),
                        jnp.where(diag, acc0[7:8], 0.0),
                        jnp.where(diag, acc1[0:1], 0.0),
                    ],
                    axis=0,
                )
                c_hi, c_lo = split2(cmat)
                c_two = jnp.concatenate([c_hi, c_lo], axis=0).astype(BF16)
                cm_ref[j] = c_two
                prod = dot(c_two, w_hi, NN)
                prod_lo = dot(c_two, w_lo, NN)
                colour = colour + prod[0:24] + prod[24:48] + prod_lo[0:24] + prod_lo[24:48]
                return through, colour

            _, colour = lax.fori_loop(
                0, chunks, forward, (jnp.ones((8, 256), F32), jnp.zeros((24, 256), F32))
            )
            resid = colour - tg_ref[...]
            err = err + jnp.sum(resid * resid, axis=0, keepdims=True)
            r_hi, r_lo = split2(2.0 * resid)
            r_two = jnp.concatenate([r_hi, r_lo], axis=0).astype(BF16)
            r_four = jnp.concatenate([r_hi, r_hi, r_lo, r_lo], axis=0).astype(BF16)

            def backward(i, behind):
                j = chunks - 1 - i
                row0 = pl.multiple_of(j * 128, 128)
                c_two = cm_ref[j]
                pull = dot(jnp.concatenate([c_two, c_two], axis=0), r_four, TN)
                alphas = al_ref[pl.ds(row0, 128), :]
                weight = w_ref[pl.ds(row0, 128), :]
                parts = []
                for k in range(15, -1, -1):
                    diff = pull[k * 8 : k * 8 + 8] - behind
                    parts.append(weight[k * 8 : k * 8 + 8] * diff)
                    behind = behind + alphas[k * 8 : k * 8 + 8] * diff
                d_exp = jnp.concatenate(parts[::-1], axis=0)
                d_hi, d_lo = split2(d_exp)
                d_two = jnp.concatenate([d_hi.astype(BF16), d_lo.astype(BF16)], axis=1)
                mom = dot(basis_2, d_two, NT)
                shade_hi = dot(r_two, wh_ref[pl.ds(row0, 128), :], NT)
                shade_lo = dot(r_two, wl_ref[pl.ds(row0, 128), :], NT)
                shade = shade_hi[0:24] + shade_hi[24:48] + shade_lo[0:24] + shade_lo[24:48]
                d_col = [
                    jnp.sum(
                        jnp.where(diag, shade[h * 8 : h * 8 + 8], 0.0), axis=0, keepdims=True
                    )
                    for h in range(3)
                ]
                feats = fe_ref[j]
                u = feats[0:1]
                v = feats[1:2]
                con_a = feats[2:3]
                con_b = feats[3:4]
                con_c = feats[4:5]
                m_xx = mom[0:1]
                m_xy = mom[1:2]
                m_yy = mom[2:3]
                m_x = mom[3:4]
                m_y = mom[4:5]
                m_1 = mom[5:6]
                s_x = m_x - u * m_1
                s_y = m_y - v * m_1
                grads = [
                    con_a * s_x + con_b * s_y,
                    con_b * s_x + con_c * s_y,
                    -0.5 * (m_xx - u * (m_x + s_x)),
                    -(m_xy - u * m_y - v * s_x),
                    -0.5 * (m_yy - v * (m_y + s_y)),
                    m_1,
                ] + d_col
                index = ix_ref[pl.ds(j, 1), :]
                hit = row_a == (index >> 8)
                rhs = scatter_rhs(index)
                rows = []
                for value in grads:
                    g_hi, g_lo = split2(value)
                    rows.append(
                        jnp.concatenate(
                            [jnp.where(hit, g_hi, 0.0), jnp.where(hit, g_lo, 0.0)], axis=1
                        )
                    )
                lhs = jnp.concatenate(rows, axis=0).astype(BF16)
                out_ref[batch_no, 0:144, :] += dot(
                    lhs, jnp.concatenate([rhs, rhs], axis=1), NT
                )
                return behind

            lax.fori_loop(0, chunks, backward, jnp.zeros((8, 256), F32))
            return err

        err = lax.fori_loop(0, GROUPS, group, jnp.zeros((1, 256), F32))
        out_ref[batch_no, 144:160, :] = jnp.broadcast_to(
            jnp.sum(err, axis=1, keepdims=True), (16, 256)
        )


def grads_kernel(cam_ref, params_ref, view_ref, send_ref, grad_ref, out_ref, err_ref, vg_ref, gg_ref):
    row_a = lax.broadcasted_iota(jnp.int32, (16, 256), 0)

    for batch_no in range(BATCHES):
        gg_ref[batch_no] = jnp.zeros((160, 256), F32)

        def place(chunk, carry, batch_no=batch_no):
            index = send_ref[batch_no, pl.ds(chunk, 1), :]
            view = view_ref[batch_no, pl.ds(chunk, 1), :]
            hit = row_a == (index >> 8)
            rhs = scatter_rhs(index)
            high = []
            low = []
            for f in range(9):
                g_hi, g_lo = split2(grad_ref[batch_no, f, pl.ds(chunk, 1), :])
                high.append(jnp.where(hit, g_hi, 0.0))
                low.append(jnp.where(hit, g_lo, 0.0))
            high.append(jnp.where(hit, view, 0.0))
            low.append(jnp.zeros((16, 256), F32))
            gg_ref[batch_no] += dot(jnp.concatenate(high, axis=0).astype(BF16), rhs, NT) + dot(
                jnp.concatenate(low, axis=0).astype(BF16), rhs, NT
            )
            return carry

        lax.fori_loop(0, 16, place, 0)

    def block(block_no, carry):
        row0 = pl.multiple_of((block_no // 2) * 8, 8)
        lane0 = pl.multiple_of((block_no % 2) * 128, 128)
        cols = [params_ref[p, pl.ds(row0, 8), pl.ds(lane0, 128)] for p in range(PARAMS)]
        geo = [0.0] * 10
        opac = 0.0
        shade = [0.0] * 48
        for batch_no in range(BATCHES):

            def feat(f, batch_no=batch_no):
                return gg_ref[batch_no, pl.ds(f * 16 + row0, 8), pl.ds(lane0, 128)]

            cam = pick_camera(cam_ref, batch_no, feat(9))
            _, pull_geo = jax.vjp(lambda c: project_geometry(c, cam), cols[0:10])
            (d_geo,) = pull_geo(tuple(feat(f) for f in range(5)))
            basis, pull_ray = jax.vjp(lambda c: ray_basis(c, cam), cols[0:3])
            d_col = [feat(6 + h) for h in range(3)]
            (d_ray,) = pull_ray(
                [
                    d_col[0] * cols[11 + k] + d_col[1] * cols[27 + k] + d_col[2] * cols[43 + k]
                    for k in range(16)
                ]
            )
            for i in range(10):
                geo[i] = geo[i] + d_geo[i]
            for i in range(3):
                geo[i] = geo[i] + d_ray[i]
            opac = opac + feat(5)
            for h in range(3):
                for k in range(16):
                    shade[16 * h + k] = shade[16 * h + k] + d_col[h] * basis[k]
        opac = opac / (1.0 + jnp.exp(cols[10]))
        for p, value in enumerate(geo + [opac] + shade):
            out_ref[p, pl.ds(row0, 8), pl.ds(lane0, 128)] = value
        return carry

    lax.fori_loop(0, 4, block, 0)
    total = grad_ref[0, 9] + grad_ref[1, 9]
    total = jnp.sum(jnp.sum(total, axis=0, keepdims=True), axis=1, keepdims=True)
    err_ref[...] = total * (1.0 / (CAP * BATCHES * OWNERS * TILES_DEV * 3 * TILE_PX))


def exchange(values):
    return lax.all_to_all(values, "dev", split_axis=1, concat_axis=1, tiled=True)


SMEM = pl.BlockSpec(memory_space=pltpu.SMEM)
VMEM = pl.BlockSpec(memory_space=pltpu.VMEM)
CALL = pltpu.CompilerParams(vmem_limit_bytes=VMEM_BYTES)


def local(params, cameras, send_lists, tile_slots, tile_ids, tile_len, targets):
    cams = camera_table(cameras)
    lengths = tile_len[:, 0]
    tile_no = jnp.arange(TILES_DEV, dtype=jnp.int32)
    ahead = (lengths[:, None, :] > lengths[:, :, None]) | (
        (lengths[:, None, :] == lengths[:, :, None]) & (tile_no[None, None, :] < tile_no[None, :, None])
    )
    rank = jnp.sum(ahead.astype(jnp.int32), axis=2)
    order = jnp.sum(
        jnp.where(rank[:, None, :] == tile_no[None, :, None], tile_no[None, None, :], 0), axis=2
    )
    send = send_lists[:, 0].reshape(BATCHES, 16, 256)
    blocks = params.reshape(PARAMS, 16, 256)

    views = pl.pallas_call(
        view_kernel,
        out_shape=jax.ShapeDtypeStruct((OWNERS, BATCHES * CAP), F32),
        in_specs=[SMEM, VMEM],
        out_specs=VMEM,
        compiler_params=CALL,
        name="slot_views",
    )(tile_ids, tile_slots)
    views = lax.all_to_all(views, "dev", split_axis=0, concat_axis=0, tiled=True)
    views = jnp.transpose(views.reshape(OWNERS, BATCHES, CAP), (1, 0, 2)).reshape(BATCHES, 16, 256)

    feats = pl.pallas_call(
        project_kernel,
        out_shape=jax.ShapeDtypeStruct((BATCHES, 9, SLOTS), F32),
        in_specs=[SMEM, VMEM, VMEM, VMEM],
        out_specs=VMEM,
        scratch_shapes=[
            pltpu.VMEM((BATCHES, 16, 256), F32),
            pltpu.VMEM((BATCHES, 512, 128), F32),
        ],
        compiler_params=CALL,
        name="project",
    )(cams, blocks, views, send)
    feats = exchange(feats.reshape(BATCHES * 9, OWNERS, CAP)).reshape(BATCHES, 9, SLOTS)
    feats = jnp.pad(feats, ((0, 0), (0, 7), (0, 0)))

    rows = TILES_DEV // GROUPS * PAIRS
    slot_grads = pl.pallas_call(
        blend_kernel,
        out_shape=jax.ShapeDtypeStruct((BATCHES, 160, 256), F32),
        in_specs=[SMEM, SMEM, SMEM, VMEM, VMEM, VMEM],
        out_specs=VMEM,
        scratch_shapes=[
            pltpu.VMEM((8, 256), jnp.int32),
            pltpu.VMEM((24, 256), F32),
            pltpu.VMEM((16, 8, 128), F32),
            pltpu.VMEM((16, 48, 128), BF16),
            pltpu.VMEM((16, 128), jnp.int32),
            pltpu.VMEM((rows, 256), F32),
            pltpu.VMEM((rows, 256), F32),
            pltpu.VMEM((rows, 256), BF16),
            pltpu.VMEM((rows, 256), BF16),
        ],
        compiler_params=CALL,
        name="blend",
    )(order, tile_ids, lengths, feats, tile_slots, targets)
    slot_grads = exchange(slot_grads.reshape(BATCHES * 10, OWNERS, CAP)).reshape(
        BATCHES, 10, 16, 256
    )

    grads, err = pl.pallas_call(
        grads_kernel,
        out_shape=(
            jax.ShapeDtypeStruct((PARAMS, 16, 256), F32),
            jax.ShapeDtypeStruct((1, 1), F32),
        ),
        in_specs=[SMEM, VMEM, VMEM, VMEM, VMEM],
        out_specs=(VMEM, VMEM),
        scratch_shapes=[
            pltpu.VMEM((BATCHES, 16, 256), F32),
            pltpu.VMEM((BATCHES, 160, 256), F32),
        ],
        compiler_params=CALL,
        name="param_grads",
    )(cams, blocks, views, send, slot_grads)
    return (grads.reshape(PARAMS, 4096), err[0, 0])


def solution(mesh):
    placed = (
        P(None, "dev"),
        P(),
        P(None, "dev", None, None),
        P(None, "dev", None),
        P(None, "dev"),
        P(None, "dev", None),
        P(None, "dev", None, None),
    )
    return jax.shard_map(
        local, mesh=mesh, in_specs=placed, out_specs=(P(None, "dev"), P()), check_vma=False
    )
```

time: 892 us -> 208 us (0.23); the launches traced: 878 us -> 207 us
  other arithmetic: 339 us -> 3.82 us
  matrix products: 220 us -> 0 us
  local copies, waits for them, and re-layouts: 195 us -> 19.8 us
  Pallas kernels: 0 us -> 136 us
  blocking collectives: 67.8 us -> 14.9 us
  starting transfers between devices: 41.4 us -> 17.3 us
  waiting for transfers between devices: 0.01 us -> 14.8 us
  loops' own time: 9.9 us -> 0 us
    dot_general x160 -> x0, matrix products: 220 us -> none  [the longest x64 124 us: tile_error(): before = jnp.dot(keep_log, upper_ones, precision=lax.Precision.HIGHEST)]
    scatter-add x4 -> x0, other arithmetic: 136 us -> none  [the longest x2 89.6 us: local(): render_slot_grads = jnp.zeros((arrived_rows, slots_dev), jnp.float32).at[...]
    pallas_call x0 -> x4, Pallas kernels: none -> 136 us  [the longest x1 102 us: local(): pl.pallas_call(blend_kernel, out_shape=jax.ShapeDtypeStruct((BATCHES, 160...]
    gather x98 -> x0, local copies, waits for them, and re-layouts: 83.6 us -> none  [the longest x64 37.2 us: one_tile(): return jax.value_and_grad(tile_loss)(arrived[:, pair_slots])]
    psum x1 -> x0, blocking collectives: 67.8 us -> none  [local(): every_error = lax.psum(error_sum, 'dev')]
    mul x512 -> x0, other arithmetic: 36.6 us -> none  [the longest x32 22.8 us: tile_pixels(): pix_u = (col_t * TILE + pixel_no % TILE).astype(jnp.float32) + 0.5]
    unnamed x30 -> x26, local copies, waits for them, and re-layouts: 42.3 us -> 8.28 us
    dynamic_update_slice x32 -> x0, other arithmetic: 33.7 us -> none  [local(): errors, col_grads = lax.map(tile_block, tile_items)]
  transfers between devices with their start and end apart: 4 -> 2, of which waited for: 0 -> 2; matrix products, arithmetic and copies ran while one was open for 76% -> 3% of each run, Pallas kernels for 0% -> 0%
where the time goes in v1:
time: 208 us; the launch traced here: 207 us
  Pallas kernels  136 us (65%)
  local copies, waits for them, and re-layouts  19.8 us (10%)
  starting transfers between devices  17.3 us (8%)
  blocking collectives  14.9 us (7%)
  waiting for transfers between devices  14.8 us (7%)
  other arithmetic  3.82 us (2%)
    pallas_call x1, Pallas kernels, local(): pl.pallas_call(blend_kernel, out_shape=jax.ShapeDtypeStruct((BATCHES, 160...  102 us
    pallas_call x1, Pallas kernels, local(): pl.pallas_call(project_kernel, out_shape=jax.ShapeDtypeStruct((BATCHES, 9...  15.4 us
    all_to_all x1, blocking collectives, exchange(): lax.all_to_all(values, 'dev', split_axis=1, concat_axis=1, tiled=True)  14.9 us
    all_to_all x1, starting transfers between devices, local(): lax.all_to_all(views, 'dev', split_axis=0, concat_axis=0, tiled=True)  11.5 us
    pallas_call x1, Pallas kernels, local(): pl.pallas_call(grads_kernel, out_shape=(jax.ShapeDtypeStruct((PARAMS, 16,...  11 us
    all_to_all x1, waiting for transfers between devices, exchange(): lax.all_to_all(values, 'dev', split_axis=1, concat_axis=1, tiled=True)  10.8 us
    unnamed x26, local copies, waits for them, and re-layouts  8.28 us
    pallas_call x1, Pallas kernels, local(): pl.pallas_call(view_kernel, out_shape=jax.ShapeDtypeStruct((OWNERS, BATCH...  7.11 us
  transfers between devices with their start and end apart: 2, of which 2 were waited for; matrix products, arithmetic and copies ran while one was open for 3% of the time, Pallas kernels for 0%

profile of v1, /device:TPU:1, one launch (start us, length us, event | category | flops | bytes accessed | tf_op | source)
XLA Modules:
  0.0 207.0 jit_solution(10401514655716826359)
XLA Ops:
  0.6 7.1 %slot_views.1 = f32[128,64]{1,0:T(8,128)} custom-call(s32[2,32]{1,0:T(2,128)} %ids_ref.3, s32[2,32,256]{2,1,0:T(8,128)} %slots_ref.3), custom_call_target="tpu_custom_call" | custom-call | tf_op jit(solution)/shard_map/slot_views/pallas_call | solution.py:589
  7.7 11.5 %all-to-all-start = ((f32[128,1,64]{2,1,0:T(1,128)}), f32[128,1,64]{2,1,0:T(1,128)S(1)}, u32[]{:S(2)}, u32[]{:S(2)}) async-start(f32[128,1,64]{2,1,0:T(1,128)} %bitcast.142), calls=%async_computation | async-start | bytes 131072 | tf_op jit(solution)/shard_map/all_to_all | solution.py:597
  19.2 1.2 slice_reduce_fusion
  20.7 1.5 copy.53
  22.2 1.0 slice.34.params_ref
  24.1 0.8 copy.50.target_ref
  24.9 4.0 %all-to-all-done = f32[128,1,64]{2,1,0:T(1,128)S(1)} async-done(((f32[128,1,64]{2,1,0:T(1,128)}), f32[128,1,64]{2,1,0:T(1,128)S(1)}, u32[]{:S(2)}, u32[]{:S(2)}) %all-to-all-start) | async-done | bytes 32800 | tf_op jit(solution)/shard_map/all_to_all | solution.py:597
  29.7 15.4 %project.1 = f32[2,9,4096]{2,1,0:T(8,128)} custom-call(f32[17,2,4]{2,1,0:T(2,128)} %copy-done.1, f32[59,16,256]{2,1,0:T(8,128)} %slice.34.params_ref, f32[2,16,256]{2,1,0:T(8,128)} %reshape.283.view_ref, s32[2,16,256]{2,1,0:T(8,128)} %reshape_squeeze.3.send_ref), custom_call_target="tpu_custom_call" | custom-call | tf_op jit(solution)/shard_map/project/pallas_call | solution.py:600
  45.2 1.4 reshape.284
  46.6 0.7 copy.58
  47.3 1.3 reshape.299
  48.6 5.8 %all-to-all-start.1 = ((f32[128,1,576]{2,1,0:T(1,128)}), f32[128,1,576]{2,1,0:T(1,128)S(1)}, u32[]{:S(2)}, u32[]{:S(2)}) async-start(f32[128,1,576]{2,1,0:T(1,128)} %reshape.299), calls=%async_computation.1 | async-start | bytes 655360 | tf_op jit(solution)/shard_map/all_to_all | solution.py:567
  55.3 10.8 %all-to-all-done.1 = f32[128,1,576]{2,1,0:T(1,128)S(1)} async-done(((f32[128,1,576]{2,1,0:T(1,128)}), f32[128,1,576]{2,1,0:T(1,128)S(1)}, u32[]{:S(2)}, u32[]{:S(2)}) %all-to-all-start.1) | async-done | bytes 294944 | tf_op jit(solution)/shard_map/all_to_all | solution.py:567
  66.7 1.4 reduce.20
  69.3 0.8 pad.4.feat_ref
  70.1 102.0 %blend.1 = f32[2,160,256]{2,1,0:T(8,128)} custom-call(s32[2,32]{1,0:T(2,128)} %select_reduce_fusion.order_ref, s32[2,32]{1,0:T(2,128)} %ids_ref.3, s32[2,32]{1,0:T(2,128)} %bitcast.144, f32[2,16,4096]{2,1,0:T(8,128)} %pad.4.feat_ref, s32[2,32,256]{2,1,0:T(8,128)} %slots_ref.3, f32[2,32,3,256]{3,2,1,0:T(4,128)} %copy.50.target_ref), custom_call_target="tpu_custom_call" | custom-call | tf_op jit(solution)/shard_map/blend/pallas_call | solution.py:616
  172.1 1.3 reshape.286
  173.4 0.8 copy.57
  174.9 14.9 %all_to_all.19 = f32[128,1,640]{2,1,0:T(1,128)S(1)} all-to-all(f32[128,1,640]{2,1,0:T(1,128)S(1)} %reshape.301), channel_id=1, replica_groups=mesh['dev'=128] {'dev'}, dimensions={0} | all-to-all | bytes 655360 | tf_op jit(solution)/shard_map/all_to_all | solution.py:567
  189.7 1.4 reduce.21
  191.9 1.1 reshape.287.grad_ref
  193.1 11.0 %param_grads.1 = (f32[59,16,256]{2,1,0:T(8,128)}, f32[1,1]{1,0:T(1,128)}) custom-call(f32[17,2,4]{2,1,0:T(2,128)} %copy-done.1, f32[59,16,256]{2,1,0:T(8,128)} %slice.34.params_ref, f32[2,16,256]{2,1,0:T(8,128)} %reshape.283.view_ref, s32[2,16,256]{2,1,0:T(8,128)} %reshape_squeeze.3.send_ref, f32[2,10,16,256]{3,2,1,0:T(8,128)} %reshape.287.grad_ref), custom_call_target="tpu_custom_call" | custom-call | tf_op jit(solution)/shard_map/param_grads/pallas_call | solution.py:639
  204.1 1.3 pad.5
  205.4 1.6 copy.54
  (40 shorter events, 5.9 us)
Async XLA Ops:
  7.7 21.1 %all-to-all-start = ((f32[128,1,64]{2,1,0:T(1,128)}), f32[128,1,64]{2,1,0:T(1,128)S(1)}, u32[]{:S(2)}, u32[]{:S(2)}) async-start(f32[128,1,64]{2,1,0:T(1,128)} %bitcast.142), calls=%async_computation | async-start | bytes 131072 | tf_op jit(solution)/shard_map/all_to_all | solution.py:597
  20.7 2.6 %copy-start.1 = (f32[17,2,4]{2,1,0:T(2,128)}, f32[17,2,4]{2,1,0:T(2,128)S(1)}, u32[]{:S(2)}) copy-start(f32[17,2,4]{2,1,0:T(2,128)S(1)} %constant_dynamic-update-slice_fusion.cam_ref) | copy-start | bytes 1636
  20.7 2.6 %copy-start.2 = (s32[2,1,128,32]{2,3,1,0:T(8,128)S(1)}, s32[2,1,128,32]{2,3,1,0:T(8,128)}, u32[]{:S(2)}) copy-start(s32[2,1,128,32]{2,3,1,0:T(8,128)} %param.9) | copy-start | bytes 98308
  22.2 1.8 copy-start
  47.3 7.2 %copy-start.3 = (s32[2,1,32]{2,1,0:T(1,128)S(1)}, s32[2,1,32]{2,1,0:T(1,128)}, u32[]{:S(2)}) copy-start(s32[2,1,32]{2,1,0:T(1,128)} %param.12) | copy-start | bytes 772
  48.6 17.6 %all-to-all-start.1 = ((f32[128,1,576]{2,1,0:T(1,128)}), f32[128,1,576]{2,1,0:T(1,128)S(1)}, u32[]{:S(2)}, u32[]{:S(2)}) async-start(f32[128,1,576]{2,1,0:T(1,128)} %reshape.299), calls=%async_computation.1 | async-start | bytes 655360 | tf_op jit(solution)/shard_map/all_to_all | solution.py:567

commit v2 on v1

v2 whole, which is shorter than its diff:
```python
import jax
import jax.numpy as jnp
from jax import lax
from jax.experimental import pallas as pl
from jax.experimental.pallas import tpu as pltpu
from jax.sharding import PartitionSpec as P

BATCHES = 2
TILE = 16
PAIRS = 256
TILE_PX = 256
TILES_X = 240
TILES_VIEW = 32400
VIEWS = 4
PARAMS = 59
TILES_DEV = 32
OWNERS = 128
CAP = 32
SLOTS = 4096
GROUPS = 4
UNROLL = 2
LOG2_E = 1.4426950408889634
VMEM_BYTES = 56 * 1024 * 1024

SH_ZERO = 0.28209479177387814
SH_ONE = 0.4886025119029199
SH_TWO = (
    1.0925484305920792,
    -1.0925484305920792,
    0.31539156525252005,
    -1.0925484305920792,
    0.5462742152960396,
)
SH_THREE = (
    -0.5900435899266435,
    2.890611442640554,
    -0.4570457994644658,
    0.3731763325901154,
    -0.4570457994644658,
    1.445305721320277,
    -0.5900435899266435,
)

F32 = jnp.float32
BF16 = jnp.bfloat16
NN = (((1,), (0,)), ((), ()))
NT = (((1,), (1,)), ((), ()))
TN = (((0,), (0,)), ((), ()))


def dot(lhs, rhs, dims):
    return lax.dot_general(lhs, rhs, dims, preferred_element_type=F32)


def split2(value):
    high = value.astype(BF16).astype(F32)
    return high, value - high


def camera_table(cameras):
    cos_yaw = jnp.cos(cameras[:, :, 0])
    sin_yaw = jnp.sin(cameras[:, :, 0])
    cos_pitch = jnp.cos(cameras[:, :, 1])
    sin_pitch = jnp.sin(cameras[:, :, 1])
    frame = [
        cos_yaw,
        sin_yaw,
        sin_pitch * sin_yaw,
        cos_pitch,
        -sin_pitch * cos_yaw,
        -cos_pitch * sin_yaw,
        sin_pitch,
        cos_pitch * cos_yaw,
    ]
    shift = [cameras[:, :, 2], cameras[:, :, 3], cameras[:, :, 4]]
    centre = [
        -(frame[0] * shift[0] + frame[2] * shift[1] + frame[5] * shift[2]),
        -(frame[3] * shift[1] + frame[6] * shift[2]),
        -(frame[1] * shift[0] + frame[4] * shift[1] + frame[7] * shift[2]),
    ]
    rest = [cameras[:, :, 5], cameras[:, :, 6], cameras[:, :, 7]]
    return jnp.stack(frame + shift + centre + rest)


CAM_ROWS = 17


def sh_basis(dir_x, dir_y, dir_z):
    square_x = dir_x * dir_x
    square_y = dir_y * dir_y
    square_z = dir_z * dir_z
    return [
        SH_ZERO * jnp.ones_like(dir_x),
        -SH_ONE * dir_y,
        SH_ONE * dir_z,
        -SH_ONE * dir_x,
        SH_TWO[0] * dir_x * dir_y,
        SH_TWO[1] * dir_y * dir_z,
        SH_TWO[2] * (2.0 * square_z - square_x - square_y),
        SH_TWO[3] * dir_x * dir_z,
        SH_TWO[4] * (square_x - square_y),
        SH_THREE[0] * dir_y * (3.0 * square_x - square_y),
        SH_THREE[1] * dir_x * dir_y * dir_z,
        SH_THREE[2] * dir_y * (4.0 * square_z - square_x - square_y),
        SH_THREE[3] * dir_z * (2.0 * square_z - 3.0 * square_x - 3.0 * square_y),
        SH_THREE[4] * dir_x * (4.0 * square_z - square_x - square_y),
        SH_THREE[5] * dir_z * (square_x - square_y),
        SH_THREE[6] * dir_x * (square_x - 3.0 * square_y),
    ]


def shape_terms(cols):
    inv_quat = 1.0 / jnp.sqrt(
        cols[6] * cols[6] + cols[7] * cols[7] + cols[8] * cols[8] + cols[9] * cols[9]
    )
    return [jnp.exp(cols[3 + i]) for i in range(3)] + [cols[6 + i] * inv_quat for i in range(4)]


def screen_terms(position, shape, cam):
    spread = shape[0:3]
    quat_w, quat_x, quat_y, quat_z = shape[3:7]
    frame = ((cam[0], None, cam[1]), (cam[2], cam[3], cam[4]), (cam[5], cam[6], cam[7]))
    shift = cam[8:11]
    focal = cam[14]
    viewed = [
        frame[0][0] * position[0] + frame[0][2] * position[2] + shift[0],
        frame[1][0] * position[0]
        + frame[1][1] * position[1]
        + frame[1][2] * position[2]
        + shift[1],
        frame[2][0] * position[0]
        + frame[2][1] * position[1]
        + frame[2][2] * position[2]
        + shift[2],
    ]
    inv_depth = 1.0 / viewed[2]
    screen_u = focal * viewed[0] * inv_depth + cam[15]
    screen_v = focal * viewed[1] * inv_depth + cam[16]
    rotation = (
        (
            1.0 - 2.0 * (quat_y * quat_y + quat_z * quat_z),
            2.0 * (quat_x * quat_y - quat_w * quat_z),
            2.0 * (quat_x * quat_z + quat_w * quat_y),
        ),
        (
            2.0 * (quat_x * quat_y + quat_w * quat_z),
            1.0 - 2.0 * (quat_x * quat_x + quat_z * quat_z),
            2.0 * (quat_y * quat_z - quat_w * quat_x),
        ),
        (
            2.0 * (quat_x * quat_z - quat_w * quat_y),
            2.0 * (quat_y * quat_z + quat_w * quat_x),
            1.0 - 2.0 * (quat_x * quat_x + quat_y * quat_y),
        ),
    )
    jac_main = focal * inv_depth
    jac_u = -jac_main * viewed[0] * inv_depth
    jac_v = -jac_main * viewed[1] * inv_depth
    row_u = [
        jac_main * frame[0][0] + jac_u * frame[2][0],
        jac_u * frame[2][1],
        jac_main * frame[0][2] + jac_u * frame[2][2],
    ]
    row_v = [jac_main * frame[1][i] + jac_v * frame[2][i] for i in range(3)]
    along_u = [
        (row_u[0] * rotation[0][j] + row_u[1] * rotation[1][j] + row_u[2] * rotation[2][j])
        * spread[j]
        for j in range(3)
    ]
    along_v = [
        (row_v[0] * rotation[0][j] + row_v[1] * rotation[1][j] + row_v[2] * rotation[2][j])
        * spread[j]
        for j in range(3)
    ]
    cov_uu = along_u[0] * along_u[0] + along_u[1] * along_u[1] + along_u[2] * along_u[2] + 0.3
    cov_uv = along_u[0] * along_v[0] + along_u[1] * along_v[1] + along_u[2] * along_v[2]
    cov_vv = along_v[0] * along_v[0] + along_v[1] * along_v[1] + along_v[2] * along_v[2] + 0.3
    inv_det = 1.0 / (cov_uu * cov_vv - cov_uv * cov_uv)
    return screen_u, screen_v, cov_vv * inv_det, -cov_uv * inv_det, cov_uu * inv_det


def ray_basis(position, cam):
    ray = [position[i] - cam[11 + i] for i in range(3)]
    inv_len = 1.0 / jnp.sqrt(ray[0] * ray[0] + ray[1] * ray[1] + ray[2] * ray[2])
    return sh_basis(ray[0] * inv_len, ray[1] * inv_len, ray[2] * inv_len)


def pick_camera(cam_ref, batch_no, view):
    picked = []
    for row in range(CAM_ROWS):
        value = jnp.full(view.shape, cam_ref[row, batch_no, VIEWS - 1], F32)
        for view_no in range(VIEWS - 2, -1, -1):
            value = jnp.where(view == view_no, cam_ref[row, batch_no, view_no], value)
        picked.append(value)
    return picked


def take_lanes(table, index):
    return jnp.take_along_axis(table, index, axis=1, mode="promise_in_bounds")


def by_quarter(quarter, values):
    out = values[0]
    for q in range(1, len(values)):
        out = jnp.where(quarter == q, values[q], out)
    return out


def turn(value, quarters):
    quarters = quarters % 4
    return value if quarters == 0 else pltpu.roll(value, 32 * quarters, 1)


def scatter_rhs(index):
    row = lax.broadcasted_iota(jnp.int32, (256, index.shape[1]), 0)
    return jnp.where(row == (index & 255), 1.0, 0.0).astype(BF16)


def offer_kernel(cam_ref, params_ref, send_ref, out_ref, tab_ref):
    quarter = lax.broadcasted_iota(jnp.int32, (8, 128), 1) >> 5

    def block(block_no, carry):
        row0 = pl.multiple_of((block_no // 2) * 8, 8)
        half = block_no % 2
        lane0 = pl.multiple_of(half * 128, 128)
        cols = [params_ref[p, pl.ds(row0, 8), pl.ds(lane0, 128)] for p in range(PARAMS)]
        opac = -(jnp.maximum(-cols[10], 0.0) + jnp.log1p(jnp.exp(-jnp.abs(cols[10]))))
        shared = cols[0:3] + shape_terms(cols) + [opac]
        for batch_no in range(BATCHES):
            feats = list(shared)
            for view_no in range(VIEWS):
                cam = [cam_ref[row, batch_no, view_no] for row in range(CAM_ROWS)]
                basis = ray_basis(cols[0:3], cam)
                for channel in range(3):
                    shade = 0.5
                    for term in range(16):
                        shade = shade + basis[term] * cols[11 + 16 * channel + term]
                    feats.append(shade)
            for f, value in enumerate(feats):
                start = (2 * row0 + half) * 24 + f
                tab_ref[batch_no, pl.ds(start, 8, stride=48), :] = value
            tab_ref[batch_no, pl.ds((2 * row0 + half) * 24 + 23, 8, stride=48), :] = cols[0]
        return carry

    lax.fori_loop(0, 4, block, 0)

    def pick(chunk, carry):
        for batch_no in range(BATCHES):
            both = send_ref[batch_no, pl.ds(chunk, 1), :]
            for half in range(2):
                index = jnp.broadcast_to(both[:, half * 128 : half * 128 + 128], (8, 128))
                low = index & 127
                high = index >> 7
                acc = [jnp.zeros((8, 128), F32)] * 3
                for h in range(32):
                    hit = high == h
                    for q in range(3):
                        row = h * 24 + q * 8
                        got = take_lanes(tab_ref[batch_no, row : row + 8, :], low)
                        acc[q] = jnp.where(hit, got, acc[q])
                for r in range(4):
                    out_ref[(chunk * 2 + half) * 4 + r, batch_no * 8 : batch_no * 8 + 8, :] = (
                        by_quarter(quarter, [turn(acc[q], q - r) for q in range(3)])
                    )
        return carry

    lax.fori_loop(0, 16, pick, 0)


def blend_kernel(
    order_ref, ids_ref, len_ref, cam_ref, feat_ref, slots_ref, target_ref, out_ref,
    tab_ref, sl_ref, tg_ref, fr_ref, ix_ref, ft_ref, co_ref, cc_ref,
    al_ref, w_ref, wh_ref, wl_ref, mo_ref, gr_ref, sg_ref, err_ref,
):
    lane = lax.broadcasted_iota(jnp.int32, (8, 128), 1)
    sub = lax.broadcasted_iota(jnp.int32, (8, 128), 0)
    quarter = lane >> 5
    diag = sub == (lane & 7)
    lane_k = lane >> 3
    row_a = lax.broadcasted_iota(jnp.int32, (16, 128), 0)
    pix = lax.broadcasted_iota(jnp.int32, (8, 256), 1)
    term = lax.broadcasted_iota(jnp.int32, (8, 256), 0)
    px = (pix & 15).astype(F32) - 7.5
    py = (pix >> 4).astype(F32) - 7.5
    basis = jnp.where(
        term == 0, px * px,
        jnp.where(
            term == 1, px * py,
            jnp.where(
                term == 2, py * py,
                jnp.where(term == 3, px, jnp.where(term == 4, py, jnp.where(term == 5, 1.0, 0.0))),
            ),
        ),
    )
    basis_b = jnp.concatenate([basis] * 4, axis=0).astype(BF16)
    basis_2 = jnp.concatenate([jnp.concatenate([basis, basis], axis=1)] * 2, axis=0).astype(BF16)
    zero8 = jnp.zeros((8, 128), F32)
    both = range(BATCHES)

    sg_ref[...] = jnp.zeros(sg_ref.shape, F32)
    co_ref[...] = jnp.zeros(co_ref.shape, F32)
    err_ref[...] = jnp.zeros(err_ref.shape, F32)

    def table(high, carry):
        for b in both:
            tiles = [feat_ref[high * 4 + i, b * 8 : b * 8 + 8, :] for i in range(4)]
            for q in range(3):
                row = pl.multiple_of(high * 8, 8)
                tab_ref[b, q, pl.ds(row, 8), :] = by_quarter(
                    quarter, [turn(tiles[i], i - q) for i in range(4)]
                )
        return carry

    lax.fori_loop(0, 32, table, 0)

    def group(group_no, carry):
        longest = jnp.int32(0)
        centre = []
        lengths = []
        views = []
        for b in both:
            cx = zero8
            cy = zero8
            length = jnp.zeros((8, 128), jnp.int32)
            view = jnp.zeros((8, 128), jnp.int32)
            for t in range(8):
                tile = order_ref[b, group_no * 8 + t]
                tile_id = ids_ref[b, tile]
                view_t = lax.div(tile_id, TILES_VIEW)
                in_view = tile_id - view_t * TILES_VIEW
                row_t = lax.div(in_view, TILES_X)
                col_t = in_view - row_t * TILES_X
                tile_len = len_ref[b, tile]
                longest = jnp.maximum(longest, tile_len)
                here = (lane & 7) == t
                cx = jnp.where(here, (col_t * TILE + 8).astype(F32), cx)
                cy = jnp.where(here, (row_t * TILE + 8).astype(F32), cy)
                length = jnp.where(here, tile_len, length)
                view = jnp.where(here, view_t, view)
                sl_ref[b, t : t + 1, :] = slots_ref[b, pl.ds(tile, 1), :]
                for channel in range(3):
                    tg_ref[b, channel * 8 + t : channel * 8 + t + 1, :] = target_ref[
                        b, pl.ds(tile, 1), channel, :
                    ]
            centre.append((cx, cy))
            lengths.append(length)
            views.append(view)
        chunks = lax.div(longest + (16 * UNROLL - 1), 16 * UNROLL)

        def gather(i, carry):
            for b in both:
                for n in range(UNROLL):
                    j = i * UNROLL + n
                    half = pl.multiple_of(lax.div(j, 8) * 128, 128)
                    picked = take_lanes(
                        sl_ref[b, :, pl.ds(half, 128)], lane_k + lax.rem(j, 8) * 16
                    )
                    picked = jnp.sum(
                        jnp.where(diag, picked.astype(F32), 0.0), axis=0, keepdims=True
                    )
                    index = jnp.broadcast_to(picked.astype(jnp.int32), (8, 128))
                    low = index & 127
                    high = index >> 7
                    acc = [zero8] * 3
                    for h in range(32):
                        hit = high == h
                        for q in range(3):
                            got = take_lanes(tab_ref[b, q, h * 8 : h * 8 + 8, :], low)
                            acc[q] = jnp.where(hit, got, acc[q])
                    ix_ref[b, pl.ds(j, 1), :] = index[0:1]
                    for q in range(3):
                        fr_ref[b, pl.ds(q * 128 + j, 8, stride=16), :] = acc[q]
            return carry

        lax.fori_loop(0, chunks, gather, 0)

        for b in both:
            cx, cy = centre[b]
            packed = [take_lanes(cam_ref[b, r * 8 : r * 8 + 8, :], views[b]) for r in range(3)]
            cam = [packed[r // 8][r % 8 : r % 8 + 1] for r in range(CAM_ROWS)]
            cam = [jnp.broadcast_to(c, (8, 128)) for c in cam]
            for part in range(2):
                c0 = part * 8

                def raw(f, b=b, c0=c0):
                    return fr_ref[b, f * 16 + c0 : f * 16 + c0 + 8, :]

                u, v, con_a, con_b, con_c = screen_terms(
                    [raw(f) for f in range(3)], [raw(f) for f in range(3, 10)], cam
                )
                u = u - cx
                v = v - cy
                for f, value in enumerate((u, v, con_a, con_b, con_c)):
                    ft_ref[b, f * 16 + c0 : f * 16 + c0 + 8, :] = value
                live = (lane_k + (sub + c0) * 16) < lengths[b]
                coefs = [
                    con_a * (-0.5 * LOG2_E),
                    con_b * -LOG2_E,
                    con_c * (-0.5 * LOG2_E),
                    (con_a * u + con_b * v) * LOG2_E,
                    (con_b * u + con_c * v) * LOG2_E,
                    jnp.where(
                        live,
                        (raw(10) - 0.5 * (con_a * u * u + con_c * v * v) - con_b * u * v) * LOG2_E,
                        -1e30,
                    ),
                ]
                for f, value in enumerate(coefs):
                    hi, rest = split2(value)
                    mid, lo = split2(rest)
                    for p, piece in enumerate((hi, mid, lo)):
                        co_ref[b, pl.ds(c0 * 32 + p * 8 + f, 8, stride=32), :] = piece
                for channel in range(3):
                    shade = raw(11 + channel)
                    for view_no in range(1, VIEWS):
                        shade = jnp.where(
                            views[b] == view_no, raw(11 + 3 * view_no + channel), shade
                        )
                    hi, lo = split2(shade)
                    cc_ref[b, pl.ds(c0 * 8 + channel, 8, stride=8), :] = hi
                    cc_ref[b, pl.ds(c0 * 8 + 3 + channel, 8, stride=8), :] = lo

        def colours_of(b, j):
            rows = cc_ref[b, pl.ds(pl.multiple_of(j * 8, 8), 8), :]
            return jnp.concatenate(
                [jnp.where(diag, rows[r : r + 1], 0.0) for r in range(6)], axis=0
            ).astype(BF16)

        def forward(i, carry):
            carry = list(carry)
            for b in both:
                through, colour = carry[b]
                for n in range(UNROLL):
                    j = i * UNROLL + n
                    lhs = co_ref[b, pl.ds(pl.multiple_of(j * 32, 32), 32), :].astype(BF16)
                    alphas = jnp.exp2(dot(lhs, basis_b, TN))
                    row0 = pl.multiple_of(j * 128, 128)
                    al_ref[b, pl.ds(row0, 128), :] = alphas
                    weights = []
                    for k in range(16):
                        weight = through * alphas[k * 8 : k * 8 + 8]
                        through = through - weight
                        weights.append(weight)
                    weight = jnp.concatenate(weights, axis=0)
                    w_ref[b, pl.ds(row0, 128), :] = weight
                    w_hi, w_lo = split2(weight)
                    w_hi = w_hi.astype(BF16)
                    w_lo = w_lo.astype(BF16)
                    wh_ref[b, pl.ds(row0, 128), :] = w_hi
                    wl_ref[b, pl.ds(row0, 128), :] = w_lo
                    c_two = colours_of(b, j)
                    prod = dot(c_two, w_hi, NN)
                    prod_lo = dot(c_two, w_lo, NN)
                    colour = colour + prod[0:24] + prod[24:48] + prod_lo[0:24] + prod_lo[24:48]
                carry[b] = (through, colour)
            return tuple(carry)

        start = (jnp.ones((8, 256), F32), jnp.zeros((24, 256), F32))
        done = lax.fori_loop(0, chunks, forward, (start, start))
        r_two = []
        r_four = []
        for b in both:
            resid = done[b][1] - tg_ref[b]
            err_ref[b] += resid * resid
            r_hi, r_lo = split2(2.0 * resid)
            r_two.append(jnp.concatenate([r_hi, r_lo], axis=0).astype(BF16))
            r_four.append(jnp.concatenate([r_hi, r_hi, r_lo, r_lo], axis=0).astype(BF16))

        def backward(i, carry):
            carry = list(carry)
            for b in both:
                behind = carry[b]
                for n in range(UNROLL):
                    j = (chunks - 1 - i) * UNROLL + (UNROLL - 1 - n)
                    row0 = pl.multiple_of(j * 128, 128)
                    c_two = colours_of(b, j)
                    pull = dot(jnp.concatenate([c_two, c_two], axis=0), r_four[b], TN)
                    alphas = al_ref[b, pl.ds(row0, 128), :]
                    weight = w_ref[b, pl.ds(row0, 128), :]
                    parts = []
                    for k in range(15, -1, -1):
                        diff = pull[k * 8 : k * 8 + 8] - behind
                        parts.append(weight[k * 8 : k * 8 + 8] * diff)
                        behind = behind + alphas[k * 8 : k * 8 + 8] * diff
                    d_exp = jnp.concatenate(parts[::-1], axis=0)
                    d_hi, d_lo = split2(d_exp)
                    d_two = jnp.concatenate([d_hi.astype(BF16), d_lo.astype(BF16)], axis=1)
                    mom = dot(basis_2, d_two, NT)
                    shade_hi = dot(r_two[b], wh_ref[b, pl.ds(row0, 128), :], NT)
                    shade_lo = dot(r_two[b], wl_ref[b, pl.ds(row0, 128), :], NT)
                    shade = shade_hi[0:24] + shade_hi[24:48] + shade_lo[0:24] + shade_lo[24:48]
                    mo_ref[b, pl.ds(j, 8, stride=16), :] = mom[0:8]
                    for h in range(3):
                        mo_ref[b, pl.ds((8 + h) * 16 + j, 1), :] = jnp.sum(
                            jnp.where(diag, shade[h * 8 : h * 8 + 8], 0.0), axis=0, keepdims=True
                        )
                carry[b] = behind
            return tuple(carry)

        zero = jnp.zeros((8, 256), F32)
        lax.fori_loop(0, chunks, backward, (zero, zero))

        for b in both:
            for part in range(2):
                c0 = part * 8

                def moment(f, b=b, c0=c0):
                    return mo_ref[b, f * 16 + c0 : f * 16 + c0 + 8, :]

                u, v, con_a, con_b, con_c = [
                    ft_ref[b, f * 16 + c0 : f * 16 + c0 + 8, :] for f in range(5)
                ]
                m_xx, m_xy, m_yy, m_x, m_y, m_1 = [moment(f) for f in range(6)]
                s_x = m_x - u * m_1
                s_y = m_y - v * m_1
                live = (lane_k + (sub + c0) * 16) < lengths[b]
                code = jnp.where(live, 8.0 + views[b].astype(F32), 0.0)
                grads = [
                    con_a * s_x + con_b * s_y,
                    con_b * s_x + con_c * s_y,
                    -0.5 * (m_xx - u * (m_x + s_x)),
                    -(m_xy - u * m_y - v * s_x),
                    -0.5 * (m_yy - v * (m_y + s_y)),
                    m_1,
                    moment(8),
                    moment(9),
                    moment(10),
                    code,
                ]
                for f, value in enumerate(grads):
                    hi, lo = split2(value)
                    gr_ref[b, f * 16 + c0 : f * 16 + c0 + 8, :] = hi
                    gr_ref[b, 160 + f * 16 + c0 : 160 + f * 16 + c0 + 8, :] = lo

        def scatter(i, carry):
            for b in both:
                for n in range(UNROLL):
                    j = i * UNROLL + n
                    index = ix_ref[b, pl.ds(j, 1), :]
                    hit = row_a == (index >> 8)
                    rhs = scatter_rhs(index)
                    rows = []
                    for f in range(10):
                        g_hi = gr_ref[b, pl.ds(f * 16 + j, 1), :]
                        g_lo = gr_ref[b, pl.ds(160 + f * 16 + j, 1), :]
                        rows.append(
                            jnp.concatenate(
                                [jnp.where(hit, g_hi, 0.0), jnp.where(hit, g_lo, 0.0)], axis=1
                            )
                        )
                    lhs = jnp.concatenate(rows, axis=0).astype(BF16)
                    add = dot(lhs, jnp.concatenate([rhs, rhs], axis=1), NT)
                    for half in range(2):
                        sg_ref[b, half, 0:160, :] += add[:, half * 128 : half * 128 + 128]
            return carry

        lax.fori_loop(0, chunks, scatter, 0)
        return carry

    lax.fori_loop(0, GROUPS, group, 0)
    for b in both:
        total = jnp.sum(jnp.sum(err_ref[b], axis=0, keepdims=True), axis=1, keepdims=True)
        for half in range(2):
            sg_ref[b, half, 240:256, :] = jnp.broadcast_to(total, (16, 128))

    for a in range(16):
        for half in range(2):
            parts = [
                sg_ref[b, half, pl.ds(q * 128 + a, 8, stride=16), :]
                for b in both
                for q in range(2)
            ]
            for r in range(4):
                out_ref[(a * 2 + half) * 4 + r] = by_quarter(
                    quarter, [turn(parts[q], q - r) for q in range(4)]
                )


def grads_kernel(cam_ref, params_ref, send_ref, grad_ref, out_ref, err_ref, gg_ref):
    row_a = lax.broadcasted_iota(jnp.int32, (16, 256), 0)
    quarter = lax.broadcasted_iota(jnp.int32, (8, 128), 1) >> 5
    gg_ref[...] = jnp.zeros(gg_ref.shape, F32)

    def place(chunk, total):
        tiles = [grad_ref[chunk * 8 + i] for i in range(8)]
        for tile in tiles:
            total = total + tile
        for batch_no in range(BATCHES):
            index = send_ref[batch_no, pl.ds(chunk, 1), :]
            hit = row_a == (index >> 8)
            rhs = scatter_rhs(index)
            high = []
            low = []
            for q in range(2):
                values = jnp.concatenate(
                    [
                        by_quarter(
                            quarter,
                            [turn(tiles[4 * n + i], i - 2 * batch_no - q) for i in range(4)],
                        )
                        for n in range(2)
                    ],
                    axis=1,
                )
                g_hi, g_lo = split2(values)
                for f in range(8 if q == 0 else 2):
                    high.append(jnp.where(hit, g_hi[f : f + 1], 0.0))
                    low.append(jnp.where(hit, g_lo[f : f + 1], 0.0))
            gg_ref[batch_no] += dot(jnp.concatenate(high, axis=0).astype(BF16), rhs, NT) + dot(
                jnp.concatenate(low, axis=0).astype(BF16), rhs, NT
            )
        return total

    total = lax.fori_loop(0, 16, place, jnp.zeros((8, 128), F32))

    def block(block_no, carry):
        row0 = pl.multiple_of((block_no // 2) * 8, 8)
        lane0 = pl.multiple_of((block_no % 2) * 128, 128)
        cols = [params_ref[p, pl.ds(row0, 8), pl.ds(lane0, 128)] for p in range(PARAMS)]
        geo = [0.0] * 10
        opac = 0.0
        shade = [0.0] * 48
        for batch_no in range(BATCHES):

            def feat(f, batch_no=batch_no):
                return gg_ref[batch_no, pl.ds(f * 16 + row0, 8), pl.ds(lane0, 128)]

            code = feat(9)
            view = jnp.where(code >= 12.0, (code - 16.0) * 0.5, code - 8.0)
            view = jnp.maximum(view, 0.0)
            cam = pick_camera(cam_ref, batch_no, view)
            _, pull_geo = jax.vjp(
                lambda c: screen_terms(c[0:3], shape_terms(c), cam), cols[0:10]
            )
            (d_geo,) = pull_geo(tuple(feat(f) for f in range(5)))
            basis, pull_ray = jax.vjp(lambda c: ray_basis(c, cam), cols[0:3])
            d_col = [feat(6 + h) for h in range(3)]
            (d_ray,) = pull_ray(
                [
                    d_col[0] * cols[11 + k] + d_col[1] * cols[27 + k] + d_col[2] * cols[43 + k]
                    for k in range(16)
                ]
            )
            for i in range(10):
                geo[i] = geo[i] + d_geo[i]
            for i in range(3):
                geo[i] = geo[i] + d_ray[i]
            opac = opac + feat(5)
            for h in range(3):
                for k in range(16):
                    shade[16 * h + k] = shade[16 * h + k] + d_col[h] * basis[k]
        opac = opac / (1.0 + jnp.exp(cols[10]))
        for p, value in enumerate(geo + [opac] + shade):
            out_ref[p, pl.ds(row0, 8), pl.ds(lane0, 128)] = value
        return carry

    lax.fori_loop(0, 4, block, 0)
    lane = lax.broadcasted_iota(jnp.int32, (1, 128), 1)
    errors = jnp.sum(
        jnp.where((lane == 32) | (lane == 96), total[7:8], 0.0), axis=1, keepdims=True
    )
    err_ref[...] = errors * (1.0 / (BATCHES * OWNERS * TILES_DEV * 3 * TILE_PX))


def exchange(values):
    return lax.all_to_all(values, "dev", split_axis=0, concat_axis=0, tiled=True)


SMEM = pl.BlockSpec(memory_space=pltpu.SMEM)
VMEM = pl.BlockSpec(memory_space=pltpu.VMEM)
CALL = pltpu.CompilerParams(vmem_limit_bytes=VMEM_BYTES)


def local(params, cameras, send_lists, tile_slots, tile_ids, tile_len, targets):
    cams = camera_table(cameras)
    lengths = tile_len[:, 0]
    tile_no = jnp.arange(TILES_DEV, dtype=jnp.int32)
    ahead = (lengths[:, None, :] > lengths[:, :, None]) | (
        (lengths[:, None, :] == lengths[:, :, None]) & (tile_no[None, None, :] < tile_no[None, :, None])
    )
    rank = jnp.sum(ahead.astype(jnp.int32), axis=2)
    order = jnp.sum(
        jnp.where(rank[:, None, :] == tile_no[None, :, None], tile_no[None, None, :], 0), axis=2
    )
    send = send_lists[:, 0].reshape(BATCHES, 16, 256)
    blocks = params.reshape(PARAMS, 16, 256)
    cam_lanes = jnp.pad(
        jnp.transpose(cams, (1, 0, 2)), ((0, 0), (0, 24 - CAM_ROWS), (0, 128 - VIEWS))
    )

    feats = pl.pallas_call(
        offer_kernel,
        out_shape=jax.ShapeDtypeStruct((OWNERS, 16, 128), F32),
        in_specs=[SMEM, VMEM, VMEM],
        out_specs=VMEM,
        scratch_shapes=[pltpu.VMEM((BATCHES, 768, 128), F32)],
        compiler_params=CALL,
        name="offer",
    )(cams, blocks, send)
    feats = exchange(feats)

    rows = TILES_DEV // GROUPS * PAIRS
    slot_grads = pl.pallas_call(
        blend_kernel,
        out_shape=jax.ShapeDtypeStruct((OWNERS, 8, 128), F32),
        in_specs=[SMEM, SMEM, SMEM, VMEM, VMEM, VMEM, VMEM],
        out_specs=VMEM,
        scratch_shapes=[
            pltpu.VMEM((BATCHES, 3, 256, 128), F32),
            pltpu.VMEM((BATCHES, 8, 256), jnp.int32),
            pltpu.VMEM((BATCHES, 24, 256), F32),
            pltpu.VMEM((BATCHES, 384, 128), F32),
            pltpu.VMEM((BATCHES, 16, 128), jnp.int32),
            pltpu.VMEM((BATCHES, 80, 128), F32),
            pltpu.VMEM((BATCHES, 512, 128), F32),
            pltpu.VMEM((BATCHES, 128, 128), F32),
            pltpu.VMEM((BATCHES, rows, 256), F32),
            pltpu.VMEM((BATCHES, rows, 256), F32),
            pltpu.VMEM((BATCHES, rows, 256), BF16),
            pltpu.VMEM((BATCHES, rows, 256), BF16),
            pltpu.VMEM((BATCHES, 176, 128), F32),
            pltpu.VMEM((BATCHES, 320, 128), F32),
            pltpu.VMEM((BATCHES, 2, 256, 128), F32),
            pltpu.VMEM((BATCHES, 24, 256), F32),
        ],
        compiler_params=CALL,
        name="blend",
    )(order, tile_ids, lengths, cam_lanes, feats, tile_slots, targets)
    slot_grads = exchange(slot_grads)

    grads, err = pl.pallas_call(
        grads_kernel,
        out_shape=(
            jax.ShapeDtypeStruct((PARAMS, 16, 256), F32),
            jax.ShapeDtypeStruct((1, 1), F32),
        ),
        in_specs=[SMEM, VMEM, VMEM, VMEM],
        out_specs=(VMEM, VMEM),
        scratch_shapes=[pltpu.VMEM((BATCHES, 160, 256), F32)],
        compiler_params=CALL,
        name="param_grads",
    )(cams, blocks, send, slot_grads)
    return (grads.reshape(PARAMS, 4096), err[0, 0])


def solution(mesh):
    placed = (
        P(None, "dev"),
        P(),
        P(None, "dev", None, None),
        P(None, "dev", None),
        P(None, "dev"),
        P(None, "dev", None),
        P(None, "dev", None, None),
    )
    return jax.shard_map(
        local, mesh=mesh, in_specs=placed, out_specs=(P(None, "dev"), P()), check_vma=False
    )
```

time: 208 us -> 156 us (0.75)
  Pallas kernels: 136 us -> 93.1 us
  local copies, waits for them, and re-layouts: 19.8 us -> 11.2 us
  blocking collectives: 14.9 us -> 21.1 us
  starting transfers between devices: 17.3 us -> 11.5 us
  other arithmetic: 3.82 us -> 0.95 us
    pallas_call x3 -> x2, Pallas kernels: 125 us -> 84.3 us  [the longest x1 68.8 us: local(): pl.pallas_call(blend_kernel, out_shape=jax.ShapeDtypeStruct((OWNERS, 8, 1...]
    reshape x7 -> x0, local copies, waits for them, and re-layouts: 6.58 us -> none  [the longest x2 2.13 us: local(): feats.reshape(BATCHES * 9, OWNERS, CAP)]
    all_to_all x1, blocking collectives: 14.9 us -> 21.1 us  [exchange(): lax.all_to_all(values, 'dev', split_axis=0, concat_axis=0, tiled=True)]
    all_to_all x2 -> x1, starting transfers between devices: 17.3 us -> 11.5 us  [exchange(): lax.all_to_all(values, 'dev', split_axis=0, concat_axis=0, tiled=True)]
    all_to_all x2 -> x0, other arithmetic: 2.84 us -> none  [exchange(): lax.all_to_all(values, 'dev', split_axis=1, concat_axis=1, tiled=True)]
    pallas_call x1, Pallas kernels: 11 us -> 8.78 us  [local(): pl.pallas_call(grads_kernel, out_shape=(jax.ShapeDtypeStruct((PARAMS, 16,...]
    all_to_all x2 -> x1, waiting for transfers between devices: 14.8 us -> 16.3 us  [exchange(): lax.all_to_all(values, 'dev', split_axis=0, concat_axis=0, tiled=True)]
    unnamed x26 -> x27, local copies, waits for them, and re-layouts: 8.28 us -> 7.68 us
  transfers between devices with their start and end apart: 2 -> 1, of which waited for: 2 -> 1; matrix products, arithmetic and copies ran while one was open for 3% -> 2% of each run, Pallas kernels for 0% -> 0%
where the time goes in v2:
time: 156 us; the launch traced here: 155 us
  Pallas kernels  93.1 us (60%)
  blocking collectives  21.1 us (14%)
  waiting for transfers between devices  16.3 us (10%)
  starting transfers between devices  11.5 us (7%)
  local copies, waits for them, and re-layouts  11.2 us (7%)
    pallas_call x1, Pallas kernels, local(): pl.pallas_call(blend_kernel, out_shape=jax.ShapeDtypeStruct((OWNERS, 8, 1...  68.8 us
    all_to_all x1, blocking collectives, exchange(): lax.all_to_all(values, 'dev', split_axis=0, concat_axis=0, tiled=True)  21.1 us
    all_to_all x1, waiting for transfers between devices, exchange(): lax.all_to_all(values, 'dev', split_axis=0, concat_axis=0, tiled=True)  16.3 us
    pallas_call x1, Pallas kernels, local(): pl.pallas_call(offer_kernel, out_shape=jax.ShapeDtypeStruct((OWNERS, 16,...  15.6 us
    all_to_all x1, starting transfers between devices, exchange(): lax.all_to_all(values, 'dev', split_axis=0, concat_axis=0, tiled=True)  11.5 us
    pallas_call x1, Pallas kernels, local(): pl.pallas_call(grads_kernel, out_shape=(jax.ShapeDtypeStruct((PARAMS, 16,...  8.78 us
    unnamed x27, local copies, waits for them, and re-layouts  7.68 us
  transfers between devices with their start and end apart: 1, of which 1 were waited for; matrix products, arithmetic and copies ran while one was open for 2% of the time, Pallas kernels for 0%

profile of v2, /device:TPU:1, one launch (start us, length us, event | category | flops | bytes accessed | tf_op | source)
XLA Modules:
  0.0 154.9 jit_solution(2214038463402656456)
XLA Ops:
  0.6 1.2 slice_reduce_fusion
  2.0 1.5 copy.41
  3.6 0.0 copy-start.4
  3.6 1.0 slice.34.params_ref
  4.6 0.0 copy-done.4
  4.6 0.1 copy.37
  4.7 0.7 reshape_squeeze.3.send_ref
  5.4 0.6 copy-done.2
  6.0 15.6 %offer.1 = f32[128,16,128]{2,1,0:T(8,128)} custom-call(f32[17,2,4]{2,1,0:T(2,128)} %copy-done.2, f32[59,16,256]{2,1,0:T(8,128)} %slice.34.params_ref, s32[2,16,256]{2,1,0:T(8,128)} %reshape_squeeze.3.send_ref), custom_call_target="tpu_custom_call" | custom-call | tf_op jit(solution)/shard_map/offer/pallas_call | solution.py:691
  21.6 11.5 %all-to-all-start = ((f32[128,16,128]{2,1,0:T(8,128)}), f32[128,16,128]{2,1,0:T(8,128)S(1)}, u32[]{:S(2)}, u32[]{:S(2)}) async-start(f32[128,16,128]{2,1,0:T(8,128)} %offer.1), calls=%async_computation | async-start | bytes 2097152 | tf_op jit(solution)/shard_map/all_to_all | solution.py:666
  33.1 0.0 copy-done.3
  33.1 0.0 copy-done.1
  33.1 0.8 copy.39.target_ref
  34.0 0.6 pad.4.clone.cam_ref
  34.6 0.7 copy-done.5
  35.3 0.2 convert_reduce_fusion
  35.4 0.7 select_reduce_fusion.order_ref
  36.1 16.3 %all-to-all-done.feat_ref = f32[128,16,128]{2,1,0:T(8,128)S(1)} async-done(((f32[128,16,128]{2,1,0:T(8,128)}), f32[128,16,128]{2,1,0:T(8,128)S(1)}, u32[]{:S(2)}, u32[]{:S(2)}) %all-to-all-start) | async-done | bytes 1048608 | tf_op jit(solution)/shard_map/all_to_all | solution.py:666
  52.4 1.0 copy-done
  53.4 68.8 %blend.1 = f32[128,8,128]{2,1,0:T(8,128)} custom-call(s32[2,32]{1,0:T(2,128)} %select_reduce_fusion.order_ref, s32[2,32]{1,0:T(2,128)} %ids_ref.1, s32[2,32]{1,0:T(2,128)} %bitcast.126, f32[2,24,128]{2,1,0:T(8,128)} %pad.4.clone.cam_ref, f32[128,16,128]{2,1,0:T(8,128)} %copy-done, s32[2,32,256]{2,1,0:T(8,128)} %slots_ref.1, f32[2,32,3,256]{3,2,1,0:T(4,128)} %copy.39.target_ref), custom_call_target="tpu_custom_call" | custom-call | tf_op jit(solution)/shard_map/blend/pallas_call | solution.py:703
  122.2 21.1 %all_to_all.10.grad_ref = f32[128,8,128]{2,1,0:T(8,128)} all-to-all(f32[128,8,128]{2,1,0:T(8,128)} %blend.1), channel_id=1, replica_groups=mesh['dev'=128] {'dev'}, dimensions={0} | all-to-all | bytes 1048576 | tf_op jit(solution)/shard_map/all_to_all | solution.py:666
  143.2 8.8 %param_grads.1 = (f32[59,16,256]{2,1,0:T(8,128)}, f32[1,1]{1,0:T(1,128)}) custom-call(f32[17,2,4]{2,1,0:T(2,128)} %copy-done.2, f32[59,16,256]{2,1,0:T(8,128)} %slice.34.params_ref, s32[2,16,256]{2,1,0:T(8,128)} %reshape_squeeze.3.send_ref, f32[128,8,128]{2,1,0:T(8,128)} %all_to_all.10.grad_ref), custom_call_target="tpu_custom_call" | custom-call | tf_op jit(solution)/shard_map/param_grads/pallas_call | solution.py:731
  152.0 1.3 pad.5
  153.3 1.6 %copy.42 = f32[8,8,16,256]{3,1,2,0:T(8,128)} copy(f32[8,8,16,256]{3,2,1,0:T(8,128)S(1)} %bitcast.121) | data formatting | bytes 2097152
  (24 shorter events, 0.2 us)
Async XLA Ops:
  3.6 1.0 copy-start.4
  5.4 0.6 copy-start.2
  21.6 11.5 %copy-start.3 = (f32[17,2,4]{2,1,0:T(2,128)S(1)}, f32[17,2,4]{2,1,0:T(2,128)}, u32[]{:S(2)}) copy-start(f32[17,2,4]{2,1,0:T(2,128)} %copy-done.2) | copy-start | bytes 1636
  21.6 11.5 %copy-start.1 = (f32[2,32,3,256]{3,1,2,0:T(8,128)S(1)}, f32[2,32,3,256]{3,1,2,0:T(8,128)}, u32[]{:S(2)}) copy-start(f32[2,32,3,256]{3,1,2,0:T(8,128)} %param.13) | copy-start | bytes 589828
  21.6 30.8 %all-to-all-start = ((f32[128,16,128]{2,1,0:T(8,128)}), f32[128,16,128]{2,1,0:T(8,128)S(1)}, u32[]{:S(2)}, u32[]{:S(2)}) async-start(f32[128,16,128]{2,1,0:T(8,128)} %offer.1), calls=%async_computation | async-start | bytes 2097152 | tf_op jit(solution)/shard_map/all_to_all | solution.py:666
  34.6 0.7 copy-start.5
  52.4 1.0 copy-start

commit v3 on v2

v3 whole, which is shorter than its diff:
```python
import jax
import jax.numpy as jnp
from jax import lax
from jax.experimental import pallas as pl
from jax.experimental.pallas import tpu as pltpu
from jax.sharding import PartitionSpec as P

BATCHES = 2
TILE = 16
PAIRS = 256
TILE_PX = 256
TILES_X = 240
TILES_VIEW = 32400
VIEWS = 4
PARAMS = 59
TILES_DEV = 32
OWNERS = 128
CAP = 32
SLOTS = 4096
GROUPS = 4
UNROLL = 2
PITCH = 72
LOG2_E = 1.4426950408889634
VMEM_BYTES = 56 * 1024 * 1024

SH_ZERO = 0.28209479177387814
SH_ONE = 0.4886025119029199
SH_TWO = (
    1.0925484305920792,
    -1.0925484305920792,
    0.31539156525252005,
    -1.0925484305920792,
    0.5462742152960396,
)
SH_THREE = (
    -0.5900435899266435,
    2.890611442640554,
    -0.4570457994644658,
    0.3731763325901154,
    -0.4570457994644658,
    1.445305721320277,
    -0.5900435899266435,
)

F32 = jnp.float32
BF16 = jnp.bfloat16
NN = (((1,), (0,)), ((), ()))
NT = (((1,), (1,)), ((), ()))
TN = (((0,), (0,)), ((), ()))


def dot(lhs, rhs, dims):
    return lax.dot_general(lhs, rhs, dims, preferred_element_type=F32)


def split2(value):
    high = value.astype(BF16).astype(F32)
    return high, value - high


def camera_table(cameras):
    cos_yaw = jnp.cos(cameras[:, :, 0])
    sin_yaw = jnp.sin(cameras[:, :, 0])
    cos_pitch = jnp.cos(cameras[:, :, 1])
    sin_pitch = jnp.sin(cameras[:, :, 1])
    frame = [
        cos_yaw,
        sin_yaw,
        sin_pitch * sin_yaw,
        cos_pitch,
        -sin_pitch * cos_yaw,
        -cos_pitch * sin_yaw,
        sin_pitch,
        cos_pitch * cos_yaw,
    ]
    shift = [cameras[:, :, 2], cameras[:, :, 3], cameras[:, :, 4]]
    centre = [
        -(frame[0] * shift[0] + frame[2] * shift[1] + frame[5] * shift[2]),
        -(frame[3] * shift[1] + frame[6] * shift[2]),
        -(frame[1] * shift[0] + frame[4] * shift[1] + frame[7] * shift[2]),
    ]
    rest = [cameras[:, :, 5], cameras[:, :, 6], cameras[:, :, 7]]
    return jnp.stack(frame + shift + centre + rest)


CAM_ROWS = 17


def sh_basis(dir_x, dir_y, dir_z):
    square_x = dir_x * dir_x
    square_y = dir_y * dir_y
    square_z = dir_z * dir_z
    return [
        SH_ZERO * jnp.ones_like(dir_x),
        -SH_ONE * dir_y,
        SH_ONE * dir_z,
        -SH_ONE * dir_x,
        SH_TWO[0] * dir_x * dir_y,
        SH_TWO[1] * dir_y * dir_z,
        SH_TWO[2] * (2.0 * square_z - square_x - square_y),
        SH_TWO[3] * dir_x * dir_z,
        SH_TWO[4] * (square_x - square_y),
        SH_THREE[0] * dir_y * (3.0 * square_x - square_y),
        SH_THREE[1] * dir_x * dir_y * dir_z,
        SH_THREE[2] * dir_y * (4.0 * square_z - square_x - square_y),
        SH_THREE[3] * dir_z * (2.0 * square_z - 3.0 * square_x - 3.0 * square_y),
        SH_THREE[4] * dir_x * (4.0 * square_z - square_x - square_y),
        SH_THREE[5] * dir_z * (square_x - square_y),
        SH_THREE[6] * dir_x * (square_x - 3.0 * square_y),
    ]


def shape_terms(cols):
    inv_quat = 1.0 / jnp.sqrt(
        cols[6] * cols[6] + cols[7] * cols[7] + cols[8] * cols[8] + cols[9] * cols[9]
    )
    return [jnp.exp(cols[3 + i]) for i in range(3)] + [cols[6 + i] * inv_quat for i in range(4)]


def screen_terms(position, shape, cam):
    spread = shape[0:3]
    quat_w, quat_x, quat_y, quat_z = shape[3:7]
    frame = ((cam[0], None, cam[1]), (cam[2], cam[3], cam[4]), (cam[5], cam[6], cam[7]))
    shift = cam[8:11]
    focal = cam[14]
    viewed = [
        frame[0][0] * position[0] + frame[0][2] * position[2] + shift[0],
        frame[1][0] * position[0]
        + frame[1][1] * position[1]
        + frame[1][2] * position[2]
        + shift[1],
        frame[2][0] * position[0]
        + frame[2][1] * position[1]
        + frame[2][2] * position[2]
        + shift[2],
    ]
    inv_depth = 1.0 / viewed[2]
    screen_u = focal * viewed[0] * inv_depth + cam[15]
    screen_v = focal * viewed[1] * inv_depth + cam[16]
    rotation = (
        (
            1.0 - 2.0 * (quat_y * quat_y + quat_z * quat_z),
            2.0 * (quat_x * quat_y - quat_w * quat_z),
            2.0 * (quat_x * quat_z + quat_w * quat_y),
        ),
        (
            2.0 * (quat_x * quat_y + quat_w * quat_z),
            1.0 - 2.0 * (quat_x * quat_x + quat_z * quat_z),
            2.0 * (quat_y * quat_z - quat_w * quat_x),
        ),
        (
            2.0 * (quat_x * quat_z - quat_w * quat_y),
            2.0 * (quat_y * quat_z + quat_w * quat_x),
            1.0 - 2.0 * (quat_x * quat_x + quat_y * quat_y),
        ),
    )
    jac_main = focal * inv_depth
    jac_u = -jac_main * viewed[0] * inv_depth
    jac_v = -jac_main * viewed[1] * inv_depth
    row_u = [
        jac_main * frame[0][0] + jac_u * frame[2][0],
        jac_u * frame[2][1],
        jac_main * frame[0][2] + jac_u * frame[2][2],
    ]
    row_v = [jac_main * frame[1][i] + jac_v * frame[2][i] for i in range(3)]
    along_u = [
        (row_u[0] * rotation[0][j] + row_u[1] * rotation[1][j] + row_u[2] * rotation[2][j])
        * spread[j]
        for j in range(3)
    ]
    along_v = [
        (row_v[0] * rotation[0][j] + row_v[1] * rotation[1][j] + row_v[2] * rotation[2][j])
        * spread[j]
        for j in range(3)
    ]
    cov_uu = along_u[0] * along_u[0] + along_u[1] * along_u[1] + along_u[2] * along_u[2] + 0.3
    cov_uv = along_u[0] * along_v[0] + along_u[1] * along_v[1] + along_u[2] * along_v[2]
    cov_vv = along_v[0] * along_v[0] + along_v[1] * along_v[1] + along_v[2] * along_v[2] + 0.3
    inv_det = 1.0 / (cov_uu * cov_vv - cov_uv * cov_uv)
    return screen_u, screen_v, cov_vv * inv_det, -cov_uv * inv_det, cov_uu * inv_det


def ray_basis(position, cam):
    ray = [position[i] - cam[11 + i] for i in range(3)]
    inv_len = 1.0 / jnp.sqrt(ray[0] * ray[0] + ray[1] * ray[1] + ray[2] * ray[2])
    return sh_basis(ray[0] * inv_len, ray[1] * inv_len, ray[2] * inv_len)


def pick_camera(cam_ref, batch_no, view):
    picked = []
    for row in range(CAM_ROWS):
        value = jnp.full(view.shape, cam_ref[row, batch_no, VIEWS - 1], F32)
        for view_no in range(VIEWS - 2, -1, -1):
            value = jnp.where(view == view_no, cam_ref[row, batch_no, view_no], value)
        picked.append(value)
    return picked


def take_lanes(table, index):
    return jnp.take_along_axis(table, index, axis=1, mode="promise_in_bounds")


def by_quarter(quarter, values):
    out = values[0]
    for q in range(1, len(values)):
        out = jnp.where(quarter == q, values[q], out)
    return out


def turn(value, quarters):
    quarters = quarters % 4
    return value if quarters == 0 else pltpu.roll(value, 32 * quarters, 1)


def scatter_rhs(index):
    row = lax.broadcasted_iota(jnp.int32, (256, index.shape[1]), 0)
    return jnp.where(row == (index & 255), 1.0, 0.0).astype(BF16)


def fetch_params(params_ref, flat_ref, sems):
    copies = [
        pltpu.make_async_copy(
            params_ref.at[:, pl.ds(j * 128, 128)],
            flat_ref.at[pl.ds(j * PITCH, PARAMS), :],
            sems.at[j],
        )
        for j in range(32)
    ]
    for copy in copies:
        copy.start()
    return copies


def param_rows(flat_ref, row0, half, param):
    return flat_ref[pl.ds((2 * row0 + half) * PITCH + param, 8, stride=2 * PITCH), :]


def offer_kernel(
    cam_ref, params_ref, send_ref, out_ref, flat_ref, tab_ref, two_ref, third_ref, sems
):
    copies = fetch_params(params_ref, flat_ref, sems)
    quarter = lax.broadcasted_iota(jnp.int32, (8, 128), 1) >> 5
    row_low = lax.broadcasted_iota(jnp.int32, (128, 256), 0)
    is_place = lax.broadcasted_iota(jnp.int32, (8, 128), 0) < 3
    for copy in copies:
        copy.wait()

    def block(block_no, carry):
        row0 = (block_no // 2) * 8
        half = block_no % 2
        cols = [param_rows(flat_ref, row0, half, p) for p in range(PARAMS)]
        opac = -(jnp.maximum(-cols[10], 0.0) + jnp.log1p(jnp.exp(-jnp.abs(cols[10]))))
        shared = cols[0:3] + shape_terms(cols) + [opac]
        for batch_no in range(BATCHES):
            feats = list(shared)
            for view_no in range(VIEWS):
                cam = [cam_ref[row, batch_no, view_no] for row in range(CAM_ROWS)]
                basis = ray_basis(cols[0:3], cam)
                for channel in range(3):
                    shade = 0.5
                    for term in range(16):
                        shade = shade + basis[term] * cols[11 + 16 * channel + term]
                    feats.append(shade)
            feats.append(jnp.zeros((8, 128), F32))
            for f, value in enumerate(feats):
                start = (2 * row0 + half) * 24 + f
                tab_ref[batch_no, pl.ds(start, 8, stride=48), :] = value
        return carry

    lax.fori_loop(0, 4, block, 0)

    def pieces(step, carry):
        for batch_no in range(BATCHES):
            row0 = pl.multiple_of(step * 192, 192)
            value = tab_ref[batch_no, pl.ds(row0, 192), :]
            hi, rest = split2(value)
            mid, lo = split2(rest)
            two_ref[batch_no, pl.ds(row0, 192), 0:128] = hi.astype(BF16)
            two_ref[batch_no, pl.ds(row0, 192), 128:256] = mid.astype(BF16)
            low = jnp.concatenate(
                [jnp.where(is_place, lo[n * 24 : n * 24 + 8], 0.0) for n in range(8)], axis=0
            )
            row1 = pl.multiple_of(step * 64, 64)
            third_ref[batch_no, pl.ds(row1, 64), 0:128] = low.astype(BF16)
            third_ref[batch_no, pl.ds(row1, 64), 128:256] = jnp.zeros((64, 128), BF16)
        return carry

    lax.fori_loop(0, 4, pieces, 0)

    def pick(chunk, carry):
        for batch_no in range(BATCHES):
            index = send_ref[batch_no, pl.ds(chunk, 1), :]
            high = jnp.broadcast_to(index >> 7, (8, 256))
            one = jnp.where(row_low == (index & 127), 1.0, 0.0).astype(BF16)
            one = jnp.concatenate([one, one], axis=0)
            acc = [jnp.zeros((8, 256), F32)] * 4
            for part in range(4):
                got = dot(two_ref[batch_no, part * 192 : part * 192 + 192, :], one, NN)
                low = dot(third_ref[batch_no, part * 64 : part * 64 + 64, :], one, NN)
                for h in range(8):
                    hit = high == part * 8 + h
                    for q in range(3):
                        row = h * 24 + q * 8
                        acc[q] = jnp.where(hit, got[row : row + 8], acc[q])
                    acc[3] = jnp.where(hit, low[h * 8 : h * 8 + 8], acc[3])
            acc[0] = acc[0] + acc[3]
            for half in range(2):
                cut = [acc[q][:, half * 128 : half * 128 + 128] for q in range(3)]
                for r in range(4):
                    out_ref[(chunk * 2 + half) * 4 + r, batch_no * 8 : batch_no * 8 + 8, :] = (
                        by_quarter(quarter, [turn(cut[q], q - r) for q in range(3)])
                    )
        return carry

    lax.fori_loop(0, 16, pick, 0)


def views_kernel(ids_ref, slots_ref, out_ref):
    row_high = lax.broadcasted_iota(jnp.int32, (32, PAIRS), 0)
    row_low = lax.broadcasted_iota(jnp.int32, (128, PAIRS), 0)

    def step(tile_no, sums):
        out = []
        for b in range(BATCHES):
            view = lax.div(ids_ref[b, tile_no], TILES_VIEW).astype(F32) * 0.5
            slots = slots_ref[b, pl.ds(tile_no, 1), :]
            lhs = jnp.where(row_high == (slots >> 7), view, 0.0).astype(BF16)
            rhs = jnp.where(row_low == (slots & 127), 1.0, 0.0).astype(BF16)
            out.append(sums[b] + dot(lhs, rhs, NT))
        return tuple(out)

    zero = jnp.zeros((32, 128), F32)
    sums = lax.fori_loop(0, TILES_DEV, step, (zero, zero))
    for b in range(BATCHES):
        out_ref[b] = sums[b]


def blend_kernel(
    order_ref, ids_ref, len_ref, cam_ref, feat_ref, view_ref, slots_ref, target_ref, out_ref,
    sf_ref, tab_ref, last_ref, sl_ref, tg_ref, fr_ref, ix_ref, co_ref, cc_ref,
    al_ref, w_ref, ww_ref, pl_ref, dd_ref, rt_ref, mo_ref, gr_ref, sg_ref, err_ref,
):
    lane = lax.broadcasted_iota(jnp.int32, (8, 128), 1)
    sub = lax.broadcasted_iota(jnp.int32, (8, 128), 0)
    quarter = lane >> 5
    diag = sub == (lane & 7)
    lane_k = lane >> 3
    row_a = lax.broadcasted_iota(jnp.int32, (16, 256), 0)
    pix = lax.broadcasted_iota(jnp.int32, (8, 256), 1)
    term = lax.broadcasted_iota(jnp.int32, (8, 256), 0)
    px = (pix & 15).astype(F32) - 7.5
    py = (pix >> 4).astype(F32) - 7.5
    basis = jnp.where(
        term == 0, px * px,
        jnp.where(
            term == 1, px * py,
            jnp.where(
                term == 2, py * py,
                jnp.where(term == 3, px, jnp.where(term == 4, py, jnp.where(term == 5, 1.0, 0.0))),
            ),
        ),
    )
    basis_b = jnp.concatenate([basis] * 4, axis=0).astype(BF16)
    basis_t = jnp.transpose(
        jnp.concatenate([basis, jnp.zeros((120, 256), F32)], axis=0)
    ).astype(BF16)
    row_t = lax.broadcasted_iota(jnp.int32, (256, 128), 0) & 7
    lane_t = lax.broadcasted_iota(jnp.int32, (256, 128), 1)
    own = (lane_t < 8) | ((lane_t & 7) == row_t)
    zero8 = jnp.zeros((8, 128), F32)
    both = range(BATCHES)

    sg_ref[...] = jnp.zeros(sg_ref.shape, F32)
    co_ref[...] = jnp.zeros(co_ref.shape, F32)
    err_ref[...] = jnp.zeros(err_ref.shape, F32)
    for b in both:
        rt_ref[b, 0:256, :] = basis_t
        rt_ref[b, 256:512, :] = basis_t

    def table(step, carry):
        for n in range(4):
            high = step * 4 + n
            for b in both:
                tiles = [feat_ref[high * 4 + i, b * 8 : b * 8 + 8, :] for i in range(4)]
                for q in range(3):
                    sf_ref[b, pl.ds(q * 256 + high, 8, stride=32), :] = by_quarter(
                        quarter, [turn(tiles[i], i - q) for i in range(4)]
                    )
        return carry

    lax.fori_loop(0, 8, table, 0)

    def screen(block, carry):
        row0 = pl.multiple_of(block * 8, 8)
        for b in both:

            def raw(f, b=b):
                return sf_ref[b, pl.ds(f * 32 + row0, 8), :]

            view = view_ref[b, pl.ds(row0, 8), :]
            cam = pick_camera(cam_ref, b, view)
            feats = list(
                screen_terms([raw(f) for f in range(3)], [raw(f) for f in range(3, 10)], cam)
            ) + [raw(10)]
            for channel in range(3):
                shade = raw(11 + channel)
                for view_no in range(1, VIEWS):
                    shade = jnp.where(view == view_no, raw(11 + 3 * view_no + channel), shade)
                feats.append(shade)
            for f in range(8):
                tab_ref[b, pl.ds(row0 * 8 + f, 8, stride=8), :] = feats[f]
            last_ref[b, pl.ds(row0, 8), :] = feats[8]
        return carry

    lax.fori_loop(0, 4, screen, 0)

    def group(group_no, carry):
        longest = jnp.int32(0)
        centre = []
        lengths = []
        for b in both:
            cx = zero8
            cy = zero8
            length = jnp.zeros((8, 128), jnp.int32)
            for t in range(8):
                tile = order_ref[b, group_no * 8 + t]
                tile_id = ids_ref[b, tile]
                in_view = lax.rem(tile_id, TILES_VIEW)
                row_t = lax.div(in_view, TILES_X)
                col_t = in_view - row_t * TILES_X
                tile_len = len_ref[b, tile]
                longest = jnp.maximum(longest, tile_len)
                here = (lane & 7) == t
                cx = jnp.where(here, (col_t * TILE + 8).astype(F32), cx)
                cy = jnp.where(here, (row_t * TILE + 8).astype(F32), cy)
                length = jnp.where(here, tile_len, length)
                sl_ref[b, t : t + 1, :] = slots_ref[b, pl.ds(tile, 1), :]
                for channel in range(3):
                    tg_ref[b, channel * 8 + t : channel * 8 + t + 1, :] = target_ref[
                        b, pl.ds(tile, 1), channel, :
                    ]
            centre.append((cx, cy))
            lengths.append(length)
        chunks = lax.div(longest + (16 * UNROLL - 1), 16 * UNROLL)

        def gather(i, carry):
            for b in both:
                for n in range(UNROLL):
                    j = i * UNROLL + n
                    half = pl.multiple_of(lax.div(j, 8) * 128, 128)
                    picked = take_lanes(
                        sl_ref[b, :, pl.ds(half, 128)], lane_k + lax.rem(j, 8) * 16
                    )
                    picked = jnp.sum(
                        jnp.where(diag, picked.astype(F32), 0.0), axis=0, keepdims=True
                    )
                    index = jnp.broadcast_to(picked.astype(jnp.int32), (8, 128))
                    low = index & 127
                    high = index >> 7
                    acc = zero8
                    for h in range(32):
                        got = take_lanes(tab_ref[b, h * 8 : h * 8 + 8, :], low)
                        acc = jnp.where(high == h, got, acc)
                    ix_ref[b, pl.ds(j, 1), :] = index[0:1]
                    fr_ref[b, pl.ds(j, 8, stride=16), :] = acc
            return carry

        lax.fori_loop(0, chunks, gather, 0)

        for b in both:
            cx, cy = centre[b]
            for part in range(2):
                c0 = part * 8

                def got(f, b=b, c0=c0):
                    return fr_ref[b, f * 16 + c0 : f * 16 + c0 + 8, :]

                index = ix_ref[b, c0 : c0 + 8, :]
                low = index & 127
                high = index >> 7
                last = zero8
                for h in range(32):
                    row = jnp.broadcast_to(last_ref[b, h : h + 1, :], (8, 128))
                    last = jnp.where(high == h, take_lanes(row, low), last)
                u = got(0) - cx
                v = got(1) - cy
                con_a, con_b, con_c = [got(f) for f in range(2, 5)]
                fr_ref[b, c0 : c0 + 8, :] = u
                fr_ref[b, 16 + c0 : 16 + c0 + 8, :] = v
                live = (lane_k + (sub + c0) * 16) < lengths[b]
                coefs = [
                    con_a * (-0.5 * LOG2_E),
                    con_b * -LOG2_E,
                    con_c * (-0.5 * LOG2_E),
                    (con_a * u + con_b * v) * LOG2_E,
                    (con_b * u + con_c * v) * LOG2_E,
                    jnp.where(
                        live,
                        (got(5) - 0.5 * (con_a * u * u + con_c * v * v) - con_b * u * v) * LOG2_E,
                        -1e30,
                    ),
                ]
                for f, value in enumerate(coefs):
                    hi, rest = split2(value)
                    mid, lo = split2(rest)
                    for p, piece in enumerate((hi, mid, lo)):
                        co_ref[b, pl.ds(c0 * 32 + p * 8 + f, 8, stride=32), :] = piece
                for channel, shade in enumerate((got(6), got(7), last)):
                    hi, lo = split2(shade)
                    cc_ref[b, pl.ds(c0 * 8 + channel, 8, stride=8), :] = hi
                    cc_ref[b, pl.ds(c0 * 8 + 3 + channel, 8, stride=8), :] = lo

        def colours_of(b, i):
            rows = cc_ref[b, pl.ds(pl.multiple_of(i * 16, 16), 16), :]
            return jnp.concatenate(
                [
                    jnp.concatenate(
                        [jnp.where(diag, rows[n * 8 + r : n * 8 + r + 1], 0.0) for r in range(6)],
                        axis=0,
                    )
                    for n in range(2)
                ],
                axis=1,
            ).astype(BF16)

        def fade(b, i):
            row0 = pl.multiple_of(i * 256, 256)
            pair = co_ref[b, pl.ds(pl.multiple_of(i * 64, 64), 64), :].astype(BF16)
            lhs = jnp.concatenate([pair[0:32], pair[32:64]], axis=1)
            al_ref[b, pl.ds(row0, 256), :] = jnp.exp2(dot(lhs, basis_b, TN))

        def weigh(b, i, through):
            row0 = pl.multiple_of(i * 256, 256)
            alphas = al_ref[b, pl.ds(row0, 256), :]
            weights = []
            for k in range(32):
                weight = through * alphas[k * 8 : k * 8 + 8]
                through = through - weight
                weights.append(weight)
            weight = jnp.concatenate(weights, axis=0)
            w_hi, w_lo = split2(weight)
            w_ref[b, pl.ds(row0, 256), :] = weight
            ww_ref[b, pl.ds(row0, 256), 0:256] = w_hi.astype(BF16)
            ww_ref[b, pl.ds(row0, 256), 256:512] = w_lo.astype(BF16)
            return through

        def shade(b, i, colour):
            row0 = pl.multiple_of(i * 256, 256)
            c_two = colours_of(b, i)
            prod = dot(c_two, ww_ref[b, pl.ds(row0, 256), 0:256], NN)
            prod_lo = dot(c_two, ww_ref[b, pl.ds(row0, 256), 256:512], NN)
            return colour + prod[0:24] + prod[24:48] + prod_lo[0:24] + prod_lo[24:48]

        def forward(i, carry):
            carry = list(carry)
            colours = [shade(b, i - 1, carry[b][1]) for b in both]
            through = [weigh(b, i, carry[b][0]) for b in both]
            for b in both:
                fade(b, i + 1)
            return tuple((through[b], colours[b]) for b in both)

        for b in both:
            fade(b, 0)
        start = [weigh(b, 0, jnp.ones((8, 256), F32)) for b in both]
        for b in both:
            fade(b, 1)
        dark = jnp.zeros((24, 256), F32)
        done = lax.fori_loop(1, chunks, forward, tuple((start[b], dark) for b in both))
        done = [(None, shade(b, chunks - 1, done[b][1])) for b in both]
        r_four = []
        for b in both:
            resid = done[b][1] - tg_ref[b]
            err_ref[b] += resid * resid
            r_hi, r_lo = split2(2.0 * resid)
            r_four.append(jnp.concatenate([r_hi, r_hi, r_lo, r_lo], axis=0).astype(BF16))
            r_t = jnp.transpose(
                jnp.concatenate(
                    [jnp.zeros((8, 256), F32), r_hi, r_lo, jnp.zeros((72, 256), F32)], axis=0
                )
            ).astype(BF16)
            rt_ref[b, 512:768, :] = r_t
            rt_ref[b, 768:1024, :] = r_t

        def pull(b, i):
            c_two = colours_of(b, i)
            pl_ref[b] = dot(jnp.concatenate([c_two, c_two], axis=0), r_four[b], TN)

        def slope(b, i, behind):
            row0 = pl.multiple_of(i * 256, 256)
            pulls = pl_ref[b]
            alphas = al_ref[b, pl.ds(row0, 256), :]
            weight = w_ref[b, pl.ds(row0, 256), :]
            parts = []
            for k in range(31, -1, -1):
                diff = pulls[k * 8 : k * 8 + 8] - behind
                parts.append(weight[k * 8 : k * 8 + 8] * diff)
                behind = behind + alphas[k * 8 : k * 8 + 8] * diff
            d_hi, d_lo = split2(jnp.concatenate(parts[::-1], axis=0))
            dd_ref[b, :, 0:256] = d_hi.astype(BF16)
            dd_ref[b, :, 256:512] = d_lo.astype(BF16)
            return behind

        def collect(b, i):
            row0 = pl.multiple_of(i * 256, 256)
            lhs = jnp.concatenate([dd_ref[b], ww_ref[b, pl.ds(row0, 256), :]], axis=1)
            sums = jnp.where(own, dot(lhs, rt_ref[b], NN), 0.0)
            for n in range(2):
                flip = jnp.transpose(sums[n * 128 : n * 128 + 128])
                j = i * 2 + n
                mo_ref[b, pl.ds(j, 8, stride=16), :] = flip[0:8]
                for h in range(3):
                    mo_ref[b, pl.ds((8 + h) * 16 + j, 1), :] = jnp.sum(
                        flip[8 + h * 8 : 16 + h * 8] + flip[32 + h * 8 : 40 + h * 8],
                        axis=0,
                        keepdims=True,
                    )

        def backward(step, carry):
            i = chunks - 1 - step
            for b in both:
                collect(b, i + 1)
            carry = tuple(slope(b, i, carry[b]) for b in both)
            for b in both:
                pull(b, jnp.maximum(i - 1, 0))
            return carry

        for b in both:
            pull(b, chunks - 1)
        start = tuple(slope(b, chunks - 1, jnp.zeros((8, 256), F32)) for b in both)
        for b in both:
            pull(b, jnp.maximum(chunks - 2, 0))
        lax.fori_loop(1, chunks, backward, start)
        for b in both:
            collect(b, 0)

        for b in both:
            for part in range(2):
                c0 = part * 8

                def moment(f, b=b, c0=c0):
                    return mo_ref[b, f * 16 + c0 : f * 16 + c0 + 8, :]

                u, v, con_a, con_b, con_c = [
                    fr_ref[b, f * 16 + c0 : f * 16 + c0 + 8, :] for f in range(5)
                ]
                m_xx, m_xy, m_yy, m_x, m_y, m_1 = [moment(f) for f in range(6)]
                s_x = m_x - u * m_1
                s_y = m_y - v * m_1
                grads = [
                    con_a * s_x + con_b * s_y,
                    con_b * s_x + con_c * s_y,
                    -0.5 * (m_xx - u * (m_x + s_x)),
                    -(m_xy - u * m_y - v * s_x),
                    -0.5 * (m_yy - v * (m_y + s_y)),
                    m_1,
                    moment(8),
                    moment(9),
                    moment(10),
                ]
                for f, value in enumerate(grads):
                    hi, lo = split2(value)
                    gr_ref[b, f * 16 + c0 : f * 16 + c0 + 8, :] = hi
                    gr_ref[b, 144 + f * 16 + c0 : 144 + f * 16 + c0 + 8, :] = lo

        def scatter(i, carry):
            j = i * 2
            for b in both:
                index = jnp.concatenate(
                    [ix_ref[b, pl.ds(j, 1), :], ix_ref[b, pl.ds(j + 1, 1), :]], axis=1
                )
                hit = row_a == (index >> 8)
                rows = []
                for f in range(18):
                    row = f * 16 + j
                    value = jnp.concatenate(
                        [gr_ref[b, pl.ds(row, 1), :], gr_ref[b, pl.ds(row + 1, 1), :]], axis=1
                    )
                    rows.append(jnp.where(hit, value, 0.0))
                add = dot(jnp.concatenate(rows, axis=0).astype(BF16), scatter_rhs(index), NT)
                add = add[0:144] + add[144:288]
                for half in range(2):
                    sg_ref[b, half, 0:144, :] += add[:, half * 128 : half * 128 + 128]
            return carry

        lax.fori_loop(0, chunks, scatter, 0)
        return carry

    lax.fori_loop(0, GROUPS, group, 0)
    for b in both:
        total = jnp.sum(jnp.sum(err_ref[b], axis=0, keepdims=True), axis=1, keepdims=True)
        for half in range(2):
            sg_ref[b, half, 144:160, :] = view_ref[b, pl.ds(half, 16, stride=2), :]
            sg_ref[b, half, 240:256, :] = jnp.broadcast_to(total, (16, 128))

    for a in range(16):
        for half in range(2):
            parts = [
                sg_ref[b, half, pl.ds(q * 128 + a, 8, stride=16), :]
                for b in both
                for q in range(2)
            ]
            for r in range(4):
                out_ref[(a * 2 + half) * 4 + r] = by_quarter(
                    quarter, [turn(parts[q], q - r) for q in range(4)]
                )


def grads_kernel(
    cam_ref, params_ref, send_ref, grad_ref, out_ref, err_ref, flat_ref, res_ref, gg_ref, sems
):
    copies = fetch_params(params_ref, flat_ref, sems)
    row_a = lax.broadcasted_iota(jnp.int32, (16, 256), 0)
    quarter = lax.broadcasted_iota(jnp.int32, (8, 128), 1) >> 5
    gg_ref[...] = jnp.zeros(gg_ref.shape, F32)

    def place(chunk, total):
        tiles = [grad_ref[chunk * 8 + i] for i in range(8)]
        for tile in tiles:
            total = total + tile
        for batch_no in range(BATCHES):
            index = send_ref[batch_no, pl.ds(chunk, 1), :]
            hit = row_a == (index >> 8)
            rhs = scatter_rhs(index)
            high = []
            low = []
            for q in range(2):
                values = jnp.concatenate(
                    [
                        by_quarter(
                            quarter,
                            [turn(tiles[4 * n + i], i - 2 * batch_no - q) for i in range(4)],
                        )
                        for n in range(2)
                    ],
                    axis=1,
                )
                g_hi, g_lo = split2(values)
                for f in range(8 if q == 0 else 2):
                    high.append(jnp.where(hit, g_hi[f : f + 1], 0.0))
                    low.append(jnp.where(hit, g_lo[f : f + 1], 0.0))
            add = dot(jnp.concatenate(high + low, axis=0).astype(BF16), rhs, NT)
            gg_ref[batch_no] += add[0:160] + add[160:320]
        return total

    total = lax.fori_loop(0, 16, place, jnp.zeros((8, 128), F32))
    for copy in copies:
        copy.wait()

    def block(block_no, carry):
        row0 = pl.multiple_of((block_no // 2) * 8, 8)
        half = block_no % 2
        lane0 = pl.multiple_of(half * 128, 128)
        cols = [param_rows(flat_ref, row0, half, p) for p in range(PARAMS)]
        geo = [0.0] * 10
        opac = 0.0
        shade = [0.0] * 48
        for batch_no in range(BATCHES):

            def feat(f, batch_no=batch_no):
                return gg_ref[batch_no, pl.ds(f * 16 + row0, 8), pl.ds(lane0, 128)]

            cam = pick_camera(cam_ref, batch_no, feat(9))
            _, pull_geo = jax.vjp(
                lambda c: screen_terms(c[0:3], shape_terms(c), cam), cols[0:10]
            )
            (d_geo,) = pull_geo(tuple(feat(f) for f in range(5)))
            basis, pull_ray = jax.vjp(lambda c: ray_basis(c, cam), cols[0:3])
            d_col = [feat(6 + h) for h in range(3)]
            (d_ray,) = pull_ray(
                [
                    d_col[0] * cols[11 + k] + d_col[1] * cols[27 + k] + d_col[2] * cols[43 + k]
                    for k in range(16)
                ]
            )
            for i in range(10):
                geo[i] = geo[i] + d_geo[i]
            for i in range(3):
                geo[i] = geo[i] + d_ray[i]
            opac = opac + feat(5)
            for h in range(3):
                for k in range(16):
                    shade[16 * h + k] = shade[16 * h + k] + d_col[h] * basis[k]
        opac = opac / (1.0 + jnp.exp(cols[10]))
        for p, value in enumerate(geo + [opac] + shade):
            res_ref[pl.ds((2 * row0 + half) * PITCH + p, 8, stride=2 * PITCH), :] = value
        return carry

    lax.fori_loop(0, 4, block, 0)
    copies = [
        pltpu.make_async_copy(
            res_ref.at[pl.ds(j * PITCH, PARAMS), :],
            out_ref.at[:, pl.ds(j * 128, 128)],
            sems.at[j],
        )
        for j in range(32)
    ]
    for copy in copies:
        copy.start()
    lane = lax.broadcasted_iota(jnp.int32, (1, 128), 1)
    errors = jnp.sum(
        jnp.where((lane == 32) | (lane == 96), total[7:8], 0.0), axis=1, keepdims=True
    )
    err_ref[...] = errors * (1.0 / (BATCHES * OWNERS * TILES_DEV * 3 * TILE_PX))
    for copy in copies:
        copy.wait()


def exchange(values):
    return lax.all_to_all(values, "dev", split_axis=0, concat_axis=0, tiled=True)


SMEM = pl.BlockSpec(memory_space=pltpu.SMEM)
VMEM = pl.BlockSpec(memory_space=pltpu.VMEM)
HBM = pl.BlockSpec(memory_space=pl.ANY)
CALL = pltpu.CompilerParams(vmem_limit_bytes=VMEM_BYTES)


def local(params, cameras, send_lists, tile_slots, tile_ids, tile_len, targets):
    cams = camera_table(cameras)
    lengths = tile_len[:, 0]
    tile_no = jnp.arange(TILES_DEV, dtype=jnp.int32)
    ahead = (lengths[:, None, :] > lengths[:, :, None]) | (
        (lengths[:, None, :] == lengths[:, :, None]) & (tile_no[None, None, :] < tile_no[None, :, None])
    )
    rank = jnp.sum(ahead.astype(jnp.int32), axis=2)
    order = jnp.sum(
        jnp.where(rank[:, None, :] == tile_no[None, :, None], tile_no[None, None, :], 0), axis=2
    )
    send = send_lists[:, 0].reshape(BATCHES, 16, 256)

    feats = pl.pallas_call(
        offer_kernel,
        out_shape=jax.ShapeDtypeStruct((OWNERS, 16, 128), F32),
        in_specs=[SMEM, HBM, VMEM],
        out_specs=VMEM,
        scratch_shapes=[
            pltpu.VMEM((32 * PITCH, 128), F32),
            pltpu.VMEM((BATCHES, 768, 128), F32),
            pltpu.VMEM((BATCHES, 768, 256), BF16),
            pltpu.VMEM((BATCHES, 256, 256), BF16),
            pltpu.SemaphoreType.DMA((32,)),
        ],
        compiler_params=CALL,
        name="offer",
    )(cams, params, send)
    feats = exchange(feats)

    views = pl.pallas_call(
        views_kernel,
        out_shape=jax.ShapeDtypeStruct((BATCHES, 32, 128), F32),
        in_specs=[SMEM, VMEM],
        out_specs=VMEM,
        compiler_params=CALL,
        name="slot_views",
    )(tile_ids, tile_slots)

    rows = TILES_DEV // GROUPS * PAIRS
    slot_grads = pl.pallas_call(
        blend_kernel,
        out_shape=jax.ShapeDtypeStruct((OWNERS, 8, 128), F32),
        in_specs=[SMEM, SMEM, SMEM, SMEM, VMEM, VMEM, VMEM, VMEM],
        out_specs=VMEM,
        scratch_shapes=[
            pltpu.VMEM((BATCHES, 768, 128), F32),
            pltpu.VMEM((BATCHES, 256, 128), F32),
            pltpu.VMEM((BATCHES, 32, 128), F32),
            pltpu.VMEM((BATCHES, 8, 256), jnp.int32),
            pltpu.VMEM((BATCHES, 24, 256), F32),
            pltpu.VMEM((BATCHES, 128, 128), F32),
            pltpu.VMEM((BATCHES, 16, 128), jnp.int32),
            pltpu.VMEM((BATCHES, 576, 128), F32),
            pltpu.VMEM((BATCHES, 128, 128), F32),
            pltpu.VMEM((BATCHES, rows + 256, 256), F32),
            pltpu.VMEM((BATCHES, rows, 256), F32),
            pltpu.VMEM((BATCHES, rows, 512), BF16),
            pltpu.VMEM((BATCHES, 256, 256), F32),
            pltpu.VMEM((BATCHES, 256, 512), BF16),
            pltpu.VMEM((BATCHES, 1024, 128), BF16),
            pltpu.VMEM((BATCHES, 176, 128), F32),
            pltpu.VMEM((BATCHES, 288, 128), F32),
            pltpu.VMEM((BATCHES, 2, 256, 128), F32),
            pltpu.VMEM((BATCHES, 24, 256), F32),
        ],
        compiler_params=CALL,
        name="blend",
    )(order, tile_ids, lengths, cams, feats, views, tile_slots, targets)
    slot_grads = exchange(slot_grads)

    grads, err = pl.pallas_call(
        grads_kernel,
        out_shape=(
            jax.ShapeDtypeStruct((PARAMS, 4096), F32),
            jax.ShapeDtypeStruct((1, 1), F32),
        ),
        in_specs=[SMEM, HBM, VMEM, VMEM],
        out_specs=(HBM, VMEM),
        scratch_shapes=[
            pltpu.VMEM((32 * PITCH, 128), F32),
            pltpu.VMEM((32 * PITCH, 128), F32),
            pltpu.VMEM((BATCHES, 160, 256), F32),
            pltpu.SemaphoreType.DMA((32,)),
        ],
        compiler_params=CALL,
        name="param_grads",
    )(cams, params, send, slot_grads)
    return (grads, err[0, 0])


def solution(mesh):
    placed = (
        P(None, "dev"),
        P(),
        P(None, "dev", None, None),
        P(None, "dev", None),
        P(None, "dev"),
        P(None, "dev", None),
        P(None, "dev", None, None),
    )
    return jax.shard_map(
        local, mesh=mesh, in_specs=placed, out_specs=(P(None, "dev"), P()), check_vma=False
    )
```

time: 156 us -> 123 us (0.79)
  Pallas kernels: 93.1 us -> 71.8 us
  waiting for transfers between devices: 16.3 us -> 10.4 us
  local copies, waits for them, and re-layouts: 11.2 us -> 5.71 us
    pallas_call x1, Pallas kernels: 68.8 us -> 41.1 us  [local(): pl.pallas_call(blend_kernel, out_shape=jax.ShapeDtypeStruct((OWNERS, 8, 1...]
    pallas_call x1 -> x2, Pallas kernels: 8.78 us -> 15.7 us  [the longest x1 9.2 us: local(): pl.pallas_call(grads_kernel, out_shape=(jax.ShapeDtypeStruct((PARAMS, 409...]
    all_to_all x1, waiting for transfers between devices: 16.3 us -> 10.4 us  [exchange(): lax.all_to_all(values, 'dev', split_axis=0, concat_axis=0, tiled=True)]
    unnamed x27 -> x21, local copies, waits for them, and re-layouts: 7.68 us -> 3.82 us
  transfers between devices with their start and end apart: 1 -> 1, of which waited for: 1 -> 1; matrix products, arithmetic and copies ran while one was open for 2% -> 1% of each run, Pallas kernels for 0% -> 5%
where the time goes in v3:
time: 123 us; the launch traced here: 122 us
  Pallas kernels  71.8 us (58%)
  blocking collectives  21.3 us (17%)
  starting transfers between devices  11.5 us (9%)
  waiting for transfers between devices  10.4 us (8%)
  local copies, waits for them, and re-layouts  5.71 us (5%)
    pallas_call x1, Pallas kernels, local(): pl.pallas_call(blend_kernel, out_shape=jax.ShapeDtypeStruct((OWNERS, 8, 1...  41.1 us
    all_to_all x1, blocking collectives, exchange(): lax.all_to_all(values, 'dev', split_axis=0, concat_axis=0, tiled=True)  21.3 us
    pallas_call x1, Pallas kernels, local(): pl.pallas_call(offer_kernel, out_shape=jax.ShapeDtypeStruct((OWNERS, 16,...  14.9 us
    all_to_all x1, starting transfers between devices, exchange(): lax.all_to_all(values, 'dev', split_axis=0, concat_axis=0, tiled=True)  11.5 us
    all_to_all x1, waiting for transfers between devices, exchange(): lax.all_to_all(values, 'dev', split_axis=0, concat_axis=0, tiled=True)  10.4 us
    pallas_call x1, Pallas kernels, local(): pl.pallas_call(grads_kernel, out_shape=(jax.ShapeDtypeStruct((PARAMS, 409...  9.2 us
    pallas_call x1, Pallas kernels, local(): pl.pallas_call(views_kernel, out_shape=jax.ShapeDtypeStruct((BATCHES, 32,...  6.54 us
    unnamed x21, local copies, waits for them, and re-layouts  3.82 us
  transfers between devices with their start and end apart: 1, of which 1 were waited for; matrix products, arithmetic and copies ran while one was open for 1% of the time, Pallas kernels for 5%

profile of v3, /device:TPU:1, one launch (start us, length us, event | category | flops | bytes accessed | tf_op | source)
XLA Modules:
  0.0 122.5 jit_solution(4315703407334342774)
XLA Ops:
  0.6 1.2 slice_reduce_fusion
  1.8 0.0 copy-start.3
  2.0 0.6 copy-done.3
  2.6 0.1 copy.35
  2.7 0.7 reshape_squeeze.3.send_ref
  3.4 0.0 copy-start.2
  3.4 0.6 copy-done.2
  4.0 14.9 %offer.1 = f32[128,16,128]{2,1,0:T(8,128)} custom-call(f32[17,2,4]{2,1,0:T(2,128)} %copy-done.2, f32[59,4096]{1,0:T(8,128)} %params_ref.3, s32[2,16,256]{2,1,0:T(8,128)} %reshape_squeeze.3.send_ref), custom_call_target="tpu_custom_call" | custom-call | tf_op jit(solution)/shard_map/offer/pallas_call | solution.py:831
  19.0 0.0 copy-start.1
  19.0 11.5 %all-to-all-start = ((f32[128,16,128]{2,1,0:T(8,128)}), f32[128,16,128]{2,1,0:T(8,128)S(1)}, u32[]{:S(2)}, u32[]{:S(2)}) async-start(f32[128,16,128]{2,1,0:T(8,128)} %offer.1), calls=%async_computation | async-start | bytes 2097152 | tf_op jit(solution)/shard_map/all_to_all | solution.py:809
  30.5 0.0 copy-done.1
  30.5 0.8 copy.36.target_ref
  31.3 6.5 %slot_views.1.view_ref = f32[2,32,128]{2,1,0:T(8,128)} custom-call(s32[2,32]{1,0:T(2,128)} %ids_ref.3, s32[2,32,256]{2,1,0:T(8,128)} %slots_ref.3), custom_call_target="tpu_custom_call" | custom-call | tf_op jit(solution)/shard_map/slot_views/pallas_call | solution.py:848
  37.9 0.0 copy-start.4
  37.9 0.7 copy-done.4
  38.6 0.2 convert_reduce_fusion
  38.8 0.7 select_reduce_fusion.order_ref
  39.4 10.4 %all-to-all-done.feat_ref = f32[128,16,128]{2,1,0:T(8,128)S(1)} async-done(((f32[128,16,128]{2,1,0:T(8,128)}), f32[128,16,128]{2,1,0:T(8,128)S(1)}, u32[]{:S(2)}, u32[]{:S(2)}) %all-to-all-start) | async-done | bytes 1048608 | tf_op jit(solution)/shard_map/all_to_all | solution.py:809
  49.8 0.0 copy-start
  49.8 1.0 copy-done
  50.8 41.1 %blend.1 = f32[128,8,128]{2,1,0:T(8,128)} custom-call(s32[2,32]{1,0:T(2,128)} %select_reduce_fusion.order_ref, s32[2,32]{1,0:T(2,128)} %ids_ref.3, s32[2,32]{1,0:T(2,128)} %bitcast.114, f32[17,2,4]{2,1,0:T(2,128)} %copy-done.2, f32[128,16,128]{2,1,0:T(8,128)} %copy-done, f32[2,32,128]{2,1,0:T(8,128)} %slot_views.1.view_ref, s32[2,32,256]{2,1,0:T(8,128)} %slots_ref.3, ...), custom_call_target="tpu_custom_call" | custom-call | tf_op jit(solution)/shard_map/blend/pallas_call | solution.py:858
  91.9 21.3 %all_to_all.10.grad_ref = f32[128,8,128]{2,1,0:T(8,128)} all-to-all(f32[128,8,128]{2,1,0:T(8,128)} %blend.1), channel_id=1, replica_groups=mesh['dev'=128] {'dev'}, dimensions={0} | all-to-all | bytes 1048576 | tf_op jit(solution)/shard_map/all_to_all | solution.py:809
  113.3 9.2 %param_grads.1 = (f32[59,4096]{1,0:T(8,128)}, f32[1,1]{1,0:T(1,128)}) custom-call(f32[17,2,4]{2,1,0:T(2,128)} %copy-done.2, f32[59,4096]{1,0:T(8,128)} %params_ref.3, s32[2,16,256]{2,1,0:T(8,128)} %reshape_squeeze.3.send_ref, f32[128,8,128]{2,1,0:T(8,128)} %all_to_all.10.grad_ref), custom_call_target="tpu_custom_call" | custom-call | tf_op jit(solution)/shard_map/param_grads/pallas_call | solution.py:889
  (18 shorter events, 0.2 us)
Async XLA Ops:
  1.8 0.8 copy-start.3
  3.4 0.6 copy-start.2
  19.0 11.5 %copy-start.1 = (f32[2,32,3,256]{3,1,2,0:T(8,128)S(1)}, f32[2,32,3,256]{3,1,2,0:T(8,128)}, u32[]{:S(2)}) copy-start(f32[2,32,3,256]{3,1,2,0:T(8,128)} %param.13) | copy-start | bytes 589828
  19.0 30.9 %all-to-all-start = ((f32[128,16,128]{2,1,0:T(8,128)}), f32[128,16,128]{2,1,0:T(8,128)S(1)}, u32[]{:S(2)}, u32[]{:S(2)}) async-start(f32[128,16,128]{2,1,0:T(8,128)} %offer.1), calls=%async_computation | async-start | bytes 2097152 | tf_op jit(solution)/shard_map/all_to_all | solution.py:809
  37.9 0.7 copy-start.4
  49.8 1.0 copy-start

commit v4 on v3

--- a/solution.py
+++ b/solution.py
@@ -18,7 +18,6 @@
 CAP = 32
 SLOTS = 4096
 GROUPS = 4
-UNROLL = 2
 PITCH = 72
 LOG2_E = 1.4426950408889634
 VMEM_BYTES = 56 * 1024 * 1024
@@ -236,12 +235,11 @@
 
 
 def offer_kernel(
-    cam_ref, params_ref, send_ref, out_ref, flat_ref, tab_ref, two_ref, third_ref, sems
+    cam_ref, params_ref, send_ref, out_ref, flat_ref, tab_ref, two_ref, sems
 ):
     copies = fetch_params(params_ref, flat_ref, sems)
     quarter = lax.broadcasted_iota(jnp.int32, (8, 128), 1) >> 5
     row_low = lax.broadcasted_iota(jnp.int32, (128, 256), 0)
-    is_place = lax.broadcasted_iota(jnp.int32, (8, 128), 0) < 3
     for copy in copies:
         copy.wait()
 
@@ -271,18 +269,12 @@
 
     def pieces(step, carry):
         for batch_no in range(BATCHES):
-            row0 = pl.multiple_of(step * 192, 192)
-            value = tab_ref[batch_no, pl.ds(row0, 192), :]
-            hi, rest = split2(value)
-            mid, lo = split2(rest)
-            two_ref[batch_no, pl.ds(row0, 192), 0:128] = hi.astype(BF16)
-            two_ref[batch_no, pl.ds(row0, 192), 128:256] = mid.astype(BF16)
-            low = jnp.concatenate(
-                [jnp.where(is_place, lo[n * 24 : n * 24 + 8], 0.0) for n in range(8)], axis=0
-            )
-            row1 = pl.multiple_of(step * 64, 64)
-            third_ref[batch_no, pl.ds(row1, 64), 0:128] = low.astype(BF16)
-            third_ref[batch_no, pl.ds(row1, 64), 128:256] = jnp.zeros((64, 128), BF16)
+            for n in range(8):
+                h = step * 8 + n
+                hi, mid = split2(tab_ref[batch_no, pl.ds(pl.multiple_of(h * 24 + 8, 8), 16), :])
+                row = pl.multiple_of(h * 16, 16)
+                two_ref[batch_no, pl.ds(row, 16), 0:128] = hi.astype(BF16)
+                two_ref[batch_no, pl.ds(row, 16), 128:256] = mid.astype(BF16)
         return carry
 
     lax.fori_loop(0, 4, pieces, 0)
@@ -291,21 +283,28 @@
         for batch_no in range(BATCHES):
             index = send_ref[batch_no, pl.ds(chunk, 1), :]
             high = jnp.broadcast_to(index >> 7, (8, 256))
+            low = jnp.broadcast_to(index & 127, (8, 256))
             one = jnp.where(row_low == (index & 127), 1.0, 0.0).astype(BF16)
             one = jnp.concatenate([one, one], axis=0)
-            acc = [jnp.zeros((8, 256), F32)] * 4
+            exact = [jnp.zeros((8, 128), F32)] * 2
+            acc = [jnp.zeros((8, 256), F32)] * 2
             for part in range(4):
-                got = dot(two_ref[batch_no, part * 192 : part * 192 + 192, :], one, NN)
-                low = dot(third_ref[batch_no, part * 64 : part * 64 + 64, :], one, NN)
-                for h in range(8):
-                    hit = high == part * 8 + h
-                    for q in range(3):
-                        row = h * 24 + q * 8
+                got = dot(two_ref[batch_no, part * 128 : part * 128 + 128, :], one, NN)
+                for n in range(8):
+                    h = part * 8 + n
+                    hit = high == h
+                    for q in range(2):
+                        row = n * 16 + q * 8
                         acc[q] = jnp.where(hit, got[row : row + 8], acc[q])
-                    acc[3] = jnp.where(hit, low[h * 8 : h * 8 + 8], acc[3])
-            acc[0] = acc[0] + acc[3]
+                    rows = tab_ref[batch_no, h * 24 : h * 24 + 8, :]
+                    for half in range(2):
+                        lanes = slice(half * 128, half * 128 + 128)
+                        exact[half] = jnp.where(
+                            hit[:, lanes], take_lanes(rows, low[:, lanes]), exact[half]
+                        )
             for half in range(2):
-                cut = [acc[q][:, half * 128 : half * 128 + 128] for q in range(3)]
+                lanes = slice(half * 128, half * 128 + 128)
+                cut = [exact[half], acc[0][:, lanes], acc[1][:, lanes]]
                 for r in range(4):
                     out_ref[(chunk * 2 + half) * 4 + r, batch_no * 8 : batch_no * 8 + 8, :] = (
                         by_quarter(quarter, [turn(cut[q], q - r) for q in range(3)])
@@ -315,7 +314,49 @@
     lax.fori_loop(0, 16, pick, 0)
 
 
-def views_kernel(ids_ref, slots_ref, out_ref):
+def plan_kernel(
+    order_ref, ids_ref, len_ref, slots_ref, target_ref,
+    out_ref, ix_ref, tile_ref, aim_ref, sl_ref,
+):
+    lane = lax.broadcasted_iota(jnp.int32, (8, 128), 1)
+    sub = lax.broadcasted_iota(jnp.int32, (8, 128), 0)
+    diag = sub == (lane & 7)
+
+    def group(group_no, carry):
+        for b in range(BATCHES):
+            cx = jnp.zeros((1, 128), F32)
+            cy = jnp.zeros((1, 128), F32)
+            length = jnp.zeros((1, 128), F32)
+            for t in range(8):
+                tile = order_ref[b, group_no * 8 + t]
+                in_view = lax.rem(ids_ref[b, tile], TILES_VIEW)
+                row_t = lax.div(in_view, TILES_X)
+                col_t = in_view - row_t * TILES_X
+                here = (lane[0:1] & 7) == t
+                cx = jnp.where(here, (col_t * TILE + 8).astype(F32), cx)
+                cy = jnp.where(here, (row_t * TILE + 8).astype(F32), cy)
+                length = jnp.where(here, len_ref[b, tile].astype(F32), length)
+                sl_ref[b, t : t + 1, :] = slots_ref[b, pl.ds(tile, 1), :]
+                for channel in range(3):
+                    aim_ref[b, pl.ds(group_no * 24 + channel * 8 + t, 1), :] = target_ref[
+                        b, pl.ds(tile, 1), channel, :
+                    ]
+            tile_ref[b, pl.ds(pl.multiple_of(group_no * 8, 8), 8), :] = jnp.concatenate(
+                [cx, cy, length, jnp.zeros((5, 128), F32)], axis=0
+            )
+            picks = []
+            for j in range(16):
+                half = (j // 8) * 128
+                picked = take_lanes(sl_ref[b, :, half : half + 128], (lane >> 3) + (j % 8) * 16)
+                picks.append(
+                    jnp.sum(jnp.where(diag, picked.astype(F32), 0.0), axis=0, keepdims=True)
+                )
+            ix_ref[b, pl.ds(pl.multiple_of(group_no * 16, 16), 16), :] = jnp.concatenate(
+                picks, axis=0
+            ).astype(jnp.int32)
+        return carry
+
+    lax.fori_loop(0, GROUPS, group, 0)
     row_high = lax.broadcasted_iota(jnp.int32, (32, PAIRS), 0)
     row_low = lax.broadcasted_iota(jnp.int32, (128, PAIRS), 0)
 
@@ -336,8 +377,8 @@
 
 
 def blend_kernel(
-    order_ref, ids_ref, len_ref, cam_ref, feat_ref, view_ref, slots_ref, target_ref, out_ref,
-    sf_ref, tab_ref, last_ref, sl_ref, tg_ref, fr_ref, ix_ref, co_ref, cc_ref,
+    order_ref, len_ref, cam_ref, feat_ref, view_ref, ix_ref, tile_ref, aim_ref, out_ref,
+    sf_ref, tab_ref, two_ref, fr_ref, co_ref, cc_ref,
     al_ref, w_ref, ww_ref, pl_ref, dd_ref, rt_ref, mo_ref, gr_ref, sg_ref, err_ref,
 ):
     lane = lax.broadcasted_iota(jnp.int32, (8, 128), 1)
@@ -346,6 +387,7 @@
     diag = sub == (lane & 7)
     lane_k = lane >> 3
     row_a = lax.broadcasted_iota(jnp.int32, (16, 256), 0)
+    row_low = lax.broadcasted_iota(jnp.int32, (128, 256), 0)
     pix = lax.broadcasted_iota(jnp.int32, (8, 256), 1)
     term = lax.broadcasted_iota(jnp.int32, (8, 256), 0)
     px = (pix & 15).astype(F32) - 7.5
@@ -407,65 +449,68 @@
                 for view_no in range(1, VIEWS):
                     shade = jnp.where(view == view_no, raw(11 + 3 * view_no + channel), shade)
                 feats.append(shade)
-            for f in range(8):
-                tab_ref[b, pl.ds(row0 * 8 + f, 8, stride=8), :] = feats[f]
-            last_ref[b, pl.ds(row0, 8), :] = feats[8]
+            for f in range(4):
+                tab_ref[b, pl.ds(row0 * 4 + f, 8, stride=4), :] = feats[f]
+                tab_ref[b, pl.ds(128 + row0 * 4 + f, 8, stride=4), :] = feats[4 + f]
+            tab_ref[b, pl.ds(256 + row0, 8), :] = feats[8]
         return carry
 
     lax.fori_loop(0, 4, screen, 0)
+    for b in both:
+        hi, mid = split2(tab_ref[b, 128:288, :])
+        two_ref[b, :, 0:128] = hi.astype(BF16)
+        two_ref[b, :, 128:256] = mid.astype(BF16)
 
     def group(group_no, carry):
         longest = jnp.int32(0)
         centre = []
         lengths = []
+        unit0 = group_no * 16
         for b in both:
-            cx = zero8
-            cy = zero8
-            length = jnp.zeros((8, 128), jnp.int32)
-            for t in range(8):
-                tile = order_ref[b, group_no * 8 + t]
-                tile_id = ids_ref[b, tile]
-                in_view = lax.rem(tile_id, TILES_VIEW)
-                row_t = lax.div(in_view, TILES_X)
-                col_t = in_view - row_t * TILES_X
-                tile_len = len_ref[b, tile]
-                longest = jnp.maximum(longest, tile_len)
-                here = (lane & 7) == t
-                cx = jnp.where(here, (col_t * TILE + 8).astype(F32), cx)
-                cy = jnp.where(here, (row_t * TILE + 8).astype(F32), cy)
-                length = jnp.where(here, tile_len, length)
-                sl_ref[b, t : t + 1, :] = slots_ref[b, pl.ds(tile, 1), :]
-                for channel in range(3):
-                    tg_ref[b, channel * 8 + t : channel * 8 + t + 1, :] = target_ref[
-                        b, pl.ds(tile, 1), channel, :
-                    ]
+            longest = jnp.maximum(longest, len_ref[b, order_ref[b, group_no * 8]])
+            row = tile_ref[b, pl.ds(pl.multiple_of(group_no * 8, 8), 8), :]
+            cx, cy, length = [jnp.broadcast_to(row[n : n + 1], (8, 128)) for n in range(3)]
             centre.append((cx, cy))
             lengths.append(length)
-        chunks = lax.div(longest + (16 * UNROLL - 1), 16 * UNROLL)
-
-        def gather(i, carry):
-            for b in both:
-                for n in range(UNROLL):
-                    j = i * UNROLL + n
-                    half = pl.multiple_of(lax.div(j, 8) * 128, 128)
-                    picked = take_lanes(
-                        sl_ref[b, :, pl.ds(half, 128)], lane_k + lax.rem(j, 8) * 16
+        chunks = lax.div(longest + 31, 32)
+
+        def gather(step, carry):
+            for b, i in [(b, step * 2 + n) for n in range(2) for b in both]:
+                units = [ix_ref[b, pl.ds(unit0 + i * 2 + n, 1), :] for n in range(2)]
+                index = jnp.concatenate(units, axis=1)
+                one = jnp.where(row_low == (index & 127), 1.0, 0.0).astype(BF16)
+                got = dot(two_ref[b], jnp.concatenate([one, one], axis=0), NN)
+                for n in range(2):
+                    lanes = slice(n * 128, n * 128 + 128)
+                    unit = jnp.broadcast_to(units[n], (8, 128))
+                    low = unit & 127
+                    high = unit >> 7
+                    odd = (high & 1) == 1
+                    exact = zero8
+                    near = zero8
+                    last = zero8
+                    for h in range(16):
+                        rows = slice(h * 8, h * 8 + 8)
+                        hit = (high >> 1) == h
+                        exact = jnp.where(hit, take_lanes(tab_ref[b, rows, :], low), exact)
+                        near = jnp.where(hit, got[rows, lanes], near)
+                    for h in range(4):
+                        rows = slice(128 + h * 8, 136 + h * 8)
+                        last = jnp.where((high >> 3) == h, got[rows, lanes], last)
+                    last = jnp.sum(
+                        jnp.where(sub == (high & 7), last, 0.0), axis=0, keepdims=True
                     )
-                    picked = jnp.sum(
-                        jnp.where(diag, picked.astype(F32), 0.0), axis=0, keepdims=True
+                    feats = jnp.where(
+                        sub < 4,
+                        jnp.where(odd, pltpu.roll(exact, 4, 0), exact),
+                        jnp.where(odd, near, pltpu.roll(near, 4, 0)),
                     )
-                    index = jnp.broadcast_to(picked.astype(jnp.int32), (8, 128))
-                    low = index & 127
-                    high = index >> 7
-                    acc = zero8
-                    for h in range(32):
-                        got = take_lanes(tab_ref[b, h * 8 : h * 8 + 8, :], low)
-                        acc = jnp.where(high == h, got, acc)
-                    ix_ref[b, pl.ds(j, 1), :] = index[0:1]
-                    fr_ref[b, pl.ds(j, 8, stride=16), :] = acc
+                    j = i * 2 + n
+                    fr_ref[b, pl.ds(j, 8, stride=16), :] = feats
+                    fr_ref[b, pl.ds(128 + j, 1), :] = last
             return carry
 
-        lax.fori_loop(0, chunks, gather, 0)
+        lax.fori_loop(0, lax.div(chunks + 1, 2), gather, 0)
 
         for b in both:
             cx, cy = centre[b]
@@ -475,19 +520,12 @@
                 def got(f, b=b, c0=c0):
                     return fr_ref[b, f * 16 + c0 : f * 16 + c0 + 8, :]
 
-                index = ix_ref[b, c0 : c0 + 8, :]
-                low = index & 127
-                high = index >> 7
-                last = zero8
-                for h in range(32):
-                    row = jnp.broadcast_to(last_ref[b, h : h + 1, :], (8, 128))
-                    last = jnp.where(high == h, take_lanes(row, low), last)
                 u = got(0) - cx
                 v = got(1) - cy
                 con_a, con_b, con_c = [got(f) for f in range(2, 5)]
                 fr_ref[b, c0 : c0 + 8, :] = u
                 fr_ref[b, 16 + c0 : 16 + c0 + 8, :] = v
-                live = (lane_k + (sub + c0) * 16) < lengths[b]
+                live = (lane_k + (sub + c0) * 16).astype(F32) < lengths[b]
                 coefs = [
                     con_a * (-0.5 * LOG2_E),
                     con_b * -LOG2_E,
@@ -505,7 +543,7 @@
                     mid, lo = split2(rest)
                     for p, piece in enumerate((hi, mid, lo)):
                         co_ref[b, pl.ds(c0 * 32 + p * 8 + f, 8, stride=32), :] = piece
-                for channel, shade in enumerate((got(6), got(7), last)):
+                for channel, shade in enumerate((got(6), got(7), got(8))):
                     hi, lo = split2(shade)
                     cc_ref[b, pl.ds(c0 * 8 + channel, 8, stride=8), :] = hi
                     cc_ref[b, pl.ds(c0 * 8 + 3 + channel, 8, stride=8), :] = lo
@@ -569,7 +607,7 @@
         done = [(None, shade(b, chunks - 1, done[b][1])) for b in both]
         r_four = []
         for b in both:
-            resid = done[b][1] - tg_ref[b]
+            resid = done[b][1] - aim_ref[b, pl.ds(pl.multiple_of(group_no * 24, 8), 24), :]
             err_ref[b] += resid * resid
             r_hi, r_lo = split2(2.0 * resid)
             r_four.append(jnp.concatenate([r_hi, r_hi, r_lo, r_lo], axis=0).astype(BF16))
@@ -657,32 +695,36 @@
                     moment(9),
                     moment(10),
                 ]
+                used = (sub + c0) < 2 * chunks
                 for f, value in enumerate(grads):
-                    hi, lo = split2(value)
+                    hi, lo = split2(jnp.where(used, value, 0.0))
                     gr_ref[b, f * 16 + c0 : f * 16 + c0 + 8, :] = hi
                     gr_ref[b, 144 + f * 16 + c0 : 144 + f * 16 + c0 + 8, :] = lo
 
-        def scatter(i, carry):
-            j = i * 2
+        def scatter(step, carry):
             for b in both:
-                index = jnp.concatenate(
-                    [ix_ref[b, pl.ds(j, 1), :], ix_ref[b, pl.ds(j + 1, 1), :]], axis=1
-                )
-                hit = row_a == (index >> 8)
-                rows = []
-                for f in range(18):
-                    row = f * 16 + j
-                    value = jnp.concatenate(
-                        [gr_ref[b, pl.ds(row, 1), :], gr_ref[b, pl.ds(row + 1, 1), :]], axis=1
+                total = None
+                for n in range(2):
+                    j = step * 4 + n * 2
+                    index = jnp.concatenate(
+                        [ix_ref[b, pl.ds(unit0 + j + n, 1), :] for n in range(2)], axis=1
                     )
-                    rows.append(jnp.where(hit, value, 0.0))
-                add = dot(jnp.concatenate(rows, axis=0).astype(BF16), scatter_rhs(index), NT)
-                add = add[0:144] + add[144:288]
+                    hit = row_a == (index >> 8)
+                    rows = []
+                    for f in range(18):
+                        row = f * 16 + j
+                        value = jnp.concatenate(
+                            [gr_ref[b, pl.ds(row, 1), :], gr_ref[b, pl.ds(row + 1, 1), :]], axis=1
+                        )
+                        rows.append(jnp.where(hit, value, 0.0))
+                    add = dot(jnp.concatenate(rows, axis=0).astype(BF16), scatter_rhs(index), NT)
+                    add = add[0:144] + add[144:288]
+                    total = add if total is None else total + add
                 for half in range(2):
-                    sg_ref[b, half, 0:144, :] += add[:, half * 128 : half * 128 + 128]
+                    sg_ref[b, half, 0:144, :] += total[:, half * 128 : half * 128 + 128]
             return carry
 
-        lax.fori_loop(0, chunks, scatter, 0)
+        lax.fori_loop(0, lax.div(chunks + 1, 2), scatter, 0)
         return carry
 
     lax.fori_loop(0, GROUPS, group, 0)
@@ -836,8 +878,7 @@
         scratch_shapes=[
             pltpu.VMEM((32 * PITCH, 128), F32),
             pltpu.VMEM((BATCHES, 768, 128), F32),
-            pltpu.VMEM((BATCHES, 768, 256), BF16),
-            pltpu.VMEM((BATCHES, 256, 256), BF16),
+            pltpu.VMEM((BATCHES, 512, 256), BF16),
             pltpu.SemaphoreType.DMA((32,)),
         ],
         compiler_params=CALL,
@@ -845,29 +886,32 @@
     )(cams, params, send)
     feats = exchange(feats)
 
-    views = pl.pallas_call(
-        views_kernel,
-        out_shape=jax.ShapeDtypeStruct((BATCHES, 32, 128), F32),
-        in_specs=[SMEM, VMEM],
-        out_specs=VMEM,
+    views, slots, tiles, aims = pl.pallas_call(
+        plan_kernel,
+        out_shape=(
+            jax.ShapeDtypeStruct((BATCHES, 32, 128), F32),
+            jax.ShapeDtypeStruct((BATCHES, GROUPS * 16, 128), jnp.int32),
+            jax.ShapeDtypeStruct((BATCHES, GROUPS * 8, 128), F32),
+            jax.ShapeDtypeStruct((BATCHES, GROUPS * 24, 256), F32),
+        ),
+        in_specs=[SMEM, SMEM, SMEM, VMEM, VMEM],
+        out_specs=(VMEM, VMEM, VMEM, VMEM),
+        scratch_shapes=[pltpu.VMEM((BATCHES, 8, 256), jnp.int32)],
         compiler_params=CALL,
-        name="slot_views",
-    )(tile_ids, tile_slots)
+        name="plan",
+    )(order, tile_ids, lengths, tile_slots, targets)
 
     rows = TILES_DEV // GROUPS * PAIRS
     slot_grads = pl.pallas_call(
         blend_kernel,
         out_shape=jax.ShapeDtypeStruct((OWNERS, 8, 128), F32),
-        in_specs=[SMEM, SMEM, SMEM, SMEM, VMEM, VMEM, VMEM, VMEM],
+        in_specs=[SMEM, SMEM, SMEM, VMEM, VMEM, VMEM, VMEM, VMEM],
         out_specs=VMEM,
         scratch_shapes=[
             pltpu.VMEM((BATCHES, 768, 128), F32),
-            pltpu.VMEM((BATCHES, 256, 128), F32),
-            pltpu.VMEM((BATCHES, 32, 128), F32),
-            pltpu.VMEM((BATCHES, 8, 256), jnp.int32),
-            pltpu.VMEM((BATCHES, 24, 256), F32),
-            pltpu.VMEM((BATCHES, 128, 128), F32),
-            pltpu.VMEM((BATCHES, 16, 128), jnp.int32),
+            pltpu.VMEM((BATCHES, 288, 128), F32),
+            pltpu.VMEM((BATCHES, 160, 256), BF16),
+            pltpu.VMEM((BATCHES, 144, 128), F32),
             pltpu.VMEM((BATCHES, 576, 128), F32),
             pltpu.VMEM((BATCHES, 128, 128), F32),
             pltpu.VMEM((BATCHES, rows + 256, 256), F32),
@@ -883,7 +927,7 @@
         ],
         compiler_params=CALL,
         name="blend",
-    )(order, tile_ids, lengths, cams, feats, views, tile_slots, targets)
+    )(order, lengths, cams, feats, views, slots, tiles, aims)
     slot_grads = exchange(slot_grads)
 
     grads, err = pl.pallas_call(

time: 123 us -> 113 us (0.919)
  Pallas kernels: 71.8 us -> 64.1 us
    pallas_call x1, Pallas kernels: 41.1 us -> 35.3 us  [local(): pl.pallas_call(blend_kernel, out_shape=jax.ShapeDtypeStruct((OWNERS, 8, 1...]
    pallas_call x1, Pallas kernels: 14.9 us -> 11.9 us  [local(): pl.pallas_call(offer_kernel, out_shape=jax.ShapeDtypeStruct((OWNERS, 16,...]
  transfers between devices with their start and end apart: 1 -> 1, of which waited for: 1 -> 1; matrix products, arithmetic and copies ran while one was open for 1% -> 1% of each run, Pallas kernels for 5% -> 7%
where the time goes in v4:
time: 113 us
  Pallas kernels  64.1 us (57%)
  blocking collectives  20.7 us (18%)
  starting transfers between devices  11.4 us (10%)
  waiting for transfers between devices  9.28 us (8%)
  local copies, waits for them, and re-layouts  5.7 us (5%)
    pallas_call x1, Pallas kernels, local(): pl.pallas_call(blend_kernel, out_shape=jax.ShapeDtypeStruct((OWNERS, 8, 1...  35.3 us
    all_to_all x1, blocking collectives, exchange(): lax.all_to_all(values, 'dev', split_axis=0, concat_axis=0, tiled=True)  20.7 us
    pallas_call x1, Pallas kernels, local(): pl.pallas_call(offer_kernel, out_shape=jax.ShapeDtypeStruct((OWNERS, 16,...  11.9 us
    all_to_all x1, starting transfers between devices, exchange(): lax.all_to_all(values, 'dev', split_axis=0, concat_axis=0, tiled=True)  11.4 us
    all_to_all x1, waiting for transfers between devices, exchange(): lax.all_to_all(values, 'dev', split_axis=0, concat_axis=0, tiled=True)  9.28 us
    pallas_call x1, Pallas kernels, local(): pl.pallas_call(grads_kernel, out_shape=(jax.ShapeDtypeStruct((PARAMS, 409...  9.19 us
    pallas_call x1, Pallas kernels, local(): pl.pallas_call(plan_kernel, out_shape=(jax.ShapeDtypeStruct((BATCHES, 32,...  7.69 us
    unnamed x21, local copies, waits for them, and re-layouts  3.81 us
  transfers between devices with their start and end apart: 1, of which 1 were waited for; matrix products, arithmetic and copies ran while one was open for 1% of the time, Pallas kernels for 7%

profile of v4, /device:TPU:1, one launch (start us, length us, event | category | flops | bytes accessed | tf_op | source)
XLA Modules:
  0.0 113.0 jit_solution(4021236392486079111)
XLA Ops:
  0.6 1.2 %slice_reduce_fusion = (f32[2,4]{1,0:T(2,128)S(1)}, f32[2,4]{1,0:T(2,128)S(1)}, f32[2,4]{1,0:T(2,128)S(1)}, f32[2,4]{1,0:T(2,128)S(1)}, f32[2,4]{1,0:T(2,128)S(1...) fusion(f32[2,4,8]{2,1,0:T(4,128)} %param.8), kind=kLoop, calls=%fused_computation.21 | loop fusion | bytes 576 | tf_op jit(solution)/shard_map/slice | solution.py:81
  1.8 0.0 copy-start.3
  2.0 0.6 copy-done.3
  2.6 0.1 copy.35
  2.7 0.7 reshape_squeeze.3.send_ref
  3.4 0.0 copy-start.2
  3.4 0.6 copy-done.2
  4.0 11.9 %offer.1 = f32[128,16,128]{2,1,0:T(8,128)} custom-call(f32[17,2,4]{2,1,0:T(2,128)} %copy-done.2, f32[59,4096]{1,0:T(8,128)} %params_ref.3, s32[2,16,256]{2,1,0:T(8,128)} %reshape_squeeze.3.send_ref), custom_call_target="tpu_custom_call" | custom-call | tf_op jit(solution)/shard_map/offer/pallas_call | solution.py:873
  15.9 0.0 copy-start.1
  15.9 11.4 %all-to-all-start = ((f32[128,16,128]{2,1,0:T(8,128)}), f32[128,16,128]{2,1,0:T(8,128)S(1)}, u32[]{:S(2)}, u32[]{:S(2)}) async-start(f32[128,16,128]{2,1,0:T(8,128)} %offer.1), calls=%async_computation | async-start | bytes 2097152 | tf_op jit(solution)/shard_map/all_to_all | solution.py:851
  27.4 0.0 copy-done.1
  27.4 0.8 copy.36.target_ref
  28.2 0.0 copy-start.4
  28.2 0.7 copy-done.4
  28.9 0.2 convert_reduce_fusion
  29.1 0.7 select_reduce_fusion.order_ref
  29.7 7.7 %plan.1 = (f32[2,32,128]{2,1,0:T(8,128)}, s32[2,64,128]{2,1,0:T(8,128)}, f32[2,32,128]{2,1,0:T(8,128)}, f32[2,96,256]{2,1,0:T(8,128)}) custom-call(s32[2,32]{1,0:T(2,128)} %select_reduce_fusion.order_ref, s32[2,32]{1,0:T(2,128)} %ids_ref.1, s32[2,32]{1,0:T(2,128)} %bitcast.114, s32[2,32,256]{2,1,0:T(8,128)} %slots_ref.1, f32[2,32,3,256]{3,2,1,0:T(4,128)} %copy.36.target_ref), custom_call_target="tpu_custom_call" | custom-call | tf_op jit(solution)/shard_map/plan/pallas_call | solution.py:889
  37.4 9.3 %all-to-all-done.feat_ref = f32[128,16,128]{2,1,0:T(8,128)S(1)} async-done(((f32[128,16,128]{2,1,0:T(8,128)}), f32[128,16,128]{2,1,0:T(8,128)S(1)}, u32[]{:S(2)}, u32[]{:S(2)}) %all-to-all-start) | async-done | bytes 1048608 | tf_op jit(solution)/shard_map/all_to_all | solution.py:851
  46.7 0.0 copy-start
  46.7 1.0 copy-done
  47.7 35.3 %blend.1 = f32[128,8,128]{2,1,0:T(8,128)} custom-call(s32[2,32]{1,0:T(2,128)} %select_reduce_fusion.order_ref, s32[2,32]{1,0:T(2,128)} %bitcast.115, f32[17,2,4]{2,1,0:T(2,128)} %copy-done.2, f32[128,16,128]{2,1,0:T(8,128)} %copy-done, f32[2,32,128]{2,1,0:T(8,128)} %get-tuple-element.8.view_ref, s32[2,64,128]{2,1,0:T(8,128)} %get-tuple-element.9.ix_ref, ...), custom_call_target="tpu_custom_call" | custom-call | tf_op jit(solution)/shard_map/blend/pallas_call | solution.py:905
  83.0 20.7 %all_to_all.10.grad_ref = f32[128,8,128]{2,1,0:T(8,128)} all-to-all(f32[128,8,128]{2,1,0:T(8,128)} %blend.1), channel_id=1, replica_groups=mesh['dev'=128] {'dev'}, dimensions={0} | all-to-all | bytes 1048576 | tf_op jit(solution)/shard_map/all_to_all | solution.py:851
  103.8 9.2 %param_grads.1 = (f32[59,4096]{1,0:T(8,128)}, f32[1,1]{1,0:T(1,128)}) custom-call(f32[17,2,4]{2,1,0:T(2,128)} %copy-done.2, f32[59,4096]{1,0:T(8,128)} %params_ref.3, s32[2,16,256]{2,1,0:T(8,128)} %reshape_squeeze.3.send_ref, f32[128,8,128]{2,1,0:T(8,128)} %all_to_all.10.grad_ref), custom_call_target="tpu_custom_call" | custom-call | tf_op jit(solution)/shard_map/param_grads/pallas_call | solution.py:933
  (18 shorter events, 0.2 us)
Async XLA Ops:
  1.8 0.8 copy-start.3
  3.4 0.6 copy-start.2
  15.9 11.5 %copy-start.1 = (f32[2,32,3,256]{3,1,2,0:T(8,128)S(1)}, f32[2,32,3,256]{3,1,2,0:T(8,128)}, u32[]{:S(2)}) copy-start(f32[2,32,3,256]{3,1,2,0:T(8,128)} %param.13) | copy-start | bytes 589828
  15.9 30.8 %all-to-all-start = ((f32[128,16,128]{2,1,0:T(8,128)}), f32[128,16,128]{2,1,0:T(8,128)S(1)}, u32[]{:S(2)}, u32[]{:S(2)}) async-start(f32[128,16,128]{2,1,0:T(8,128)} %offer.1), calls=%async_computation | async-start | bytes 2097152 | tf_op jit(solution)/shard_map/all_to_all | solution.py:851
  28.2 0.7 copy-start.4
  46.7 1.0 copy-start

commit v5 on v4

--- a/solution.py
+++ b/solution.py
@@ -58,10 +58,11 @@
 
 
 def camera_table(cameras):
-    cos_yaw = jnp.cos(cameras[:, :, 0])
-    sin_yaw = jnp.sin(cameras[:, :, 0])
-    cos_pitch = jnp.cos(cameras[:, :, 1])
-    sin_pitch = jnp.sin(cameras[:, :, 1])
+    fields = [jnp.broadcast_to(cameras[:, n : n + 1], (8, 128)) for n in range(8)]
+    cos_yaw = jnp.cos(fields[0])
+    sin_yaw = jnp.sin(fields[0])
+    cos_pitch = jnp.cos(fields[1])
+    sin_pitch = jnp.sin(fields[1])
     frame = [
         cos_yaw,
         sin_yaw,
@@ -72,14 +73,13 @@
         sin_pitch,
         cos_pitch * cos_yaw,
     ]
-    shift = [cameras[:, :, 2], cameras[:, :, 3], cameras[:, :, 4]]
+    shift = fields[2:5]
     centre = [
         -(frame[0] * shift[0] + frame[2] * shift[1] + frame[5] * shift[2]),
         -(frame[3] * shift[1] + frame[6] * shift[2]),
         -(frame[1] * shift[0] + frame[4] * shift[1] + frame[7] * shift[2]),
     ]
-    rest = [cameras[:, :, 5], cameras[:, :, 6], cameras[:, :, 7]]
-    return jnp.stack(frame + shift + centre + rest)
+    return frame + shift + centre + fields[5:8]
 
 
 CAM_ROWS = 17
@@ -185,12 +185,19 @@
     return sh_basis(ray[0] * inv_len, ray[1] * inv_len, ray[2] * inv_len)
 
 
+def camera_field(cam_ref, field, batch_no, view_no):
+    row = field * 8 + batch_no * VIEWS + view_no
+    return jnp.broadcast_to(cam_ref[row : row + 1, :], (8, 128))
+
+
 def pick_camera(cam_ref, batch_no, view):
     picked = []
-    for row in range(CAM_ROWS):
-        value = jnp.full(view.shape, cam_ref[row, batch_no, VIEWS - 1], F32)
+    for field in range(CAM_ROWS):
+        value = camera_field(cam_ref, field, batch_no, VIEWS - 1)
         for view_no in range(VIEWS - 2, -1, -1):
-            value = jnp.where(view == view_no, cam_ref[row, batch_no, view_no], value)
+            value = jnp.where(
+                view == view_no, camera_field(cam_ref, field, batch_no, view_no), value
+            )
         picked.append(value)
     return picked
 
@@ -235,11 +242,25 @@
 
 
 def offer_kernel(
-    cam_ref, params_ref, send_ref, out_ref, flat_ref, tab_ref, two_ref, sems
+    camera_ref, params_ref, list_ref, out_ref, cam_ref, send_ref, flat_ref, tab_ref, two_ref, sems
 ):
     copies = fetch_params(params_ref, flat_ref, sems)
     quarter = lax.broadcasted_iota(jnp.int32, (8, 128), 1) >> 5
+    upper = lax.broadcasted_iota(jnp.int32, (8, 128), 0) < 4
     row_low = lax.broadcasted_iota(jnp.int32, (128, 256), 0)
+    place = (lax.broadcasted_iota(jnp.int32, (8, 128), 0) & 3) == quarter
+    cameras = jnp.concatenate([camera_ref[0], camera_ref[1]], axis=0)
+    for field, value in enumerate(camera_table(cameras)):
+        cam_ref[field * 8 : field * 8 + 8, :] = value
+    for batch_no in range(BATCHES):
+        for chunk in range(16):
+            lists = list_ref[batch_no, 0, chunk * 8 : chunk * 8 + 8, :].astype(F32)
+            lists = jnp.where(place, jnp.concatenate([lists] * 4, axis=1), 0.0)
+            for half in range(2):
+                line = jnp.sum(lists[half * 4 : half * 4 + 4], axis=0, keepdims=True)
+                send_ref[batch_no, chunk : chunk + 1, half * 128 : half * 128 + 128] = line.astype(
+                    jnp.int32
+                )
     for copy in copies:
         copy.wait()
 
@@ -252,7 +273,9 @@
         for batch_no in range(BATCHES):
             feats = list(shared)
             for view_no in range(VIEWS):
-                cam = [cam_ref[row, batch_no, view_no] for row in range(CAM_ROWS)]
+                cam = [
+                    camera_field(cam_ref, field, batch_no, view_no) for field in range(CAM_ROWS)
+                ]
                 basis = ray_basis(cols[0:3], cam)
                 for channel in range(3):
                     shade = 0.5
@@ -280,6 +303,7 @@
     lax.fori_loop(0, 4, pieces, 0)
 
     def pick(chunk, carry):
+        cut = []
         for batch_no in range(BATCHES):
             index = send_ref[batch_no, pl.ds(chunk, 1), :]
             high = jnp.broadcast_to(index >> 7, (8, 256))
@@ -302,13 +326,34 @@
                         exact[half] = jnp.where(
                             hit[:, lanes], take_lanes(rows, low[:, lanes]), exact[half]
                         )
-            for half in range(2):
-                lanes = slice(half * 128, half * 128 + 128)
-                cut = [exact[half], acc[0][:, lanes], acc[1][:, lanes]]
-                for r in range(4):
-                    out_ref[(chunk * 2 + half) * 4 + r, batch_no * 8 : batch_no * 8 + 8, :] = (
-                        by_quarter(quarter, [turn(cut[q], q - r) for q in range(3)])
+            cut.append((exact, [[a[:, 0:128], a[:, 128:256]] for a in acc]))
+        for half in range(2):
+            heads = [cut[0][0][half], cut[0][1][0][half], cut[0][1][1][half], cut[1][0][half]]
+            tails = [cut[1][1][q][half] for q in range(2)]
+            folded = [pltpu.roll(tail, 4, 0) for tail in tails]
+            main = []
+            tail = []
+            for r in range(4):
+                main.append(by_quarter(quarter, [turn(heads[q], q - r) for q in range(4)]))
+                tail.append(
+                    by_quarter(
+                        quarter,
+                        [
+                            turn(tails[0], -r),
+                            turn(folded[0], 1 - r),
+                            turn(tails[1], 2 - r),
+                            turn(folded[1], 3 - r),
+                        ],
                     )
+                )
+            for r in range(0, 4, 2):
+                row0 = pl.multiple_of((chunk * 2 + half) * 48 + r * 12, 8)
+                middle = pltpu.roll(main[r + 1], 4, 0)
+                out_ref[pl.ds(row0, 8), :] = main[r]
+                out_ref[pl.ds(row0 + 8, 8), :] = jnp.where(upper, tail[r], middle)
+                out_ref[pl.ds(row0 + 16, 8), :] = jnp.where(
+                    upper, middle, pltpu.roll(tail[r + 1], 4, 0)
+                )
         return carry
 
     lax.fori_loop(0, 16, pick, 0)
@@ -419,15 +464,35 @@
         rt_ref[b, 0:256, :] = basis_t
         rt_ref[b, 256:512, :] = basis_t
 
+    upper = sub < 4
+
     def table(step, carry):
         for n in range(4):
             high = step * 4 + n
-            for b in both:
-                tiles = [feat_ref[high * 4 + i, b * 8 : b * 8 + 8, :] for i in range(4)]
-                for q in range(3):
-                    sf_ref[b, pl.ds(q * 256 + high, 8, stride=32), :] = by_quarter(
-                        quarter, [turn(tiles[i], i - q) for i in range(4)]
-                    )
+            main = []
+            tail = []
+            for r in range(0, 4, 2):
+                row0 = pl.multiple_of(high * 48 + r * 12, 8)
+                tiles = [feat_ref[pl.ds(row0 + m * 8, 8), :] for m in range(3)]
+                main.append(tiles[0])
+                main.append(pltpu.roll(jnp.where(upper, tiles[2], tiles[1]), 4, 0))
+                tail.append(tiles[1])
+                tail.append(pltpu.roll(tiles[2], 4, 0))
+            folded = [pltpu.roll(value, 4, 0) for value in tail]
+            for q in range(4):
+                sf_ref[q // 3, pl.ds((q % 3) * 256 + high, 8, stride=32), :] = by_quarter(
+                    quarter, [turn(main[i], i - q) for i in range(4)]
+                )
+            for q in range(2):
+                sf_ref[1, pl.ds((q + 1) * 256 + high, 8, stride=32), :] = by_quarter(
+                    quarter,
+                    [
+                        jnp.where(
+                            upper, turn(tail[i], i - 2 * q), turn(folded[i], i - 2 * q - 1)
+                        )
+                        for i in range(4)
+                    ],
+                )
         return carry
 
     lax.fori_loop(0, 8, table, 0)
@@ -755,12 +820,14 @@
     quarter = lax.broadcasted_iota(jnp.int32, (8, 128), 1) >> 5
     gg_ref[...] = jnp.zeros(gg_ref.shape, F32)
 
-    def place(chunk, total):
-        tiles = [grad_ref[chunk * 8 + i] for i in range(8)]
-        for tile in tiles:
+    def place(step, total):
+        tiles_of = [[grad_ref[step * 16 + n * 8 + i] for i in range(8)] for n in range(2)]
+        for tile in tiles_of[0] + tiles_of[1]:
             total = total + tile
-        for batch_no in range(BATCHES):
-            index = send_ref[batch_no, pl.ds(chunk, 1), :]
+        sums = [None] * BATCHES
+        for part, batch_no in [(n, b) for n in range(2) for b in range(BATCHES)]:
+            tiles = tiles_of[part]
+            index = send_ref[batch_no, pl.ds(step * 2 + part, 1), :]
             hit = row_a == (index >> 8)
             rhs = scatter_rhs(index)
             high = []
@@ -781,10 +848,13 @@
                     high.append(jnp.where(hit, g_hi[f : f + 1], 0.0))
                     low.append(jnp.where(hit, g_lo[f : f + 1], 0.0))
             add = dot(jnp.concatenate(high + low, axis=0).astype(BF16), rhs, NT)
-            gg_ref[batch_no] += add[0:160] + add[160:320]
+            add = add[0:160] + add[160:320]
+            sums[batch_no] = add if part == 0 else sums[batch_no] + add
+        for batch_no in range(BATCHES):
+            gg_ref[batch_no] += sums[batch_no]
         return total
 
-    total = lax.fori_loop(0, 16, place, jnp.zeros((8, 128), F32))
+    total = lax.fori_loop(0, 8, place, jnp.zeros((8, 128), F32))
     for copy in copies:
         copy.wait()
 
@@ -858,7 +928,6 @@
 
 
 def local(params, cameras, send_lists, tile_slots, tile_ids, tile_len, targets):
-    cams = camera_table(cameras)
     lengths = tile_len[:, 0]
     tile_no = jnp.arange(TILES_DEV, dtype=jnp.int32)
     ahead = (lengths[:, None, :] > lengths[:, :, None]) | (
@@ -868,13 +937,16 @@
     order = jnp.sum(
         jnp.where(rank[:, None, :] == tile_no[None, :, None], tile_no[None, None, :], 0), axis=2
     )
-    send = send_lists[:, 0].reshape(BATCHES, 16, 256)
-
-    feats = pl.pallas_call(
+
+    feats, cams, send = pl.pallas_call(
         offer_kernel,
-        out_shape=jax.ShapeDtypeStruct((OWNERS, 16, 128), F32),
-        in_specs=[SMEM, HBM, VMEM],
-        out_specs=VMEM,
+        out_shape=(
+            jax.ShapeDtypeStruct((OWNERS * 12, 128), F32),
+            jax.ShapeDtypeStruct((CAM_ROWS * 8, 128), F32),
+            jax.ShapeDtypeStruct((BATCHES, 16, 256), jnp.int32),
+        ),
+        in_specs=[VMEM, HBM, VMEM],
+        out_specs=(VMEM, VMEM, VMEM),
         scratch_shapes=[
             pltpu.VMEM((32 * PITCH, 128), F32),
             pltpu.VMEM((BATCHES, 768, 128), F32),
@@ -883,8 +955,8 @@
         ],
         compiler_params=CALL,
         name="offer",
-    )(cams, params, send)
-    feats = exchange(feats)
+    )(cameras, params, send_lists)
+    feats = exchange(feats.reshape(OWNERS, 1, 1536)).reshape(OWNERS * 12, 128)
 
     views, slots, tiles, aims = pl.pallas_call(
         plan_kernel,
@@ -905,7 +977,7 @@
     slot_grads = pl.pallas_call(
         blend_kernel,
         out_shape=jax.ShapeDtypeStruct((OWNERS, 8, 128), F32),
-        in_specs=[SMEM, SMEM, SMEM, VMEM, VMEM, VMEM, VMEM, VMEM],
+        in_specs=[SMEM, SMEM, VMEM, VMEM, VMEM, VMEM, VMEM, VMEM],
         out_specs=VMEM,
         scratch_shapes=[
             pltpu.VMEM((BATCHES, 768, 128), F32),
@@ -936,7 +1008,7 @@
             jax.ShapeDtypeStruct((PARAMS, 4096), F32),
             jax.ShapeDtypeStruct((1, 1), F32),
         ),
-        in_specs=[SMEM, HBM, VMEM, VMEM],
+        in_specs=[VMEM, HBM, VMEM, VMEM],
         out_specs=(HBM, VMEM),
         scratch_shapes=[
             pltpu.VMEM((32 * PITCH, 128), F32),

time: 113 us -> 106 us (0.938)
  waiting for transfers between devices: 9.28 us -> 6.43 us
  local copies, waits for them, and re-layouts: 5.7 us -> 3.89 us
  blocking collectives: 20.7 us -> 19.1 us
    all_to_all x1, waiting for transfers between devices: 9.28 us -> 6.43 us  [exchange(): lax.all_to_all(values, 'dev', split_axis=0, concat_axis=0, tiled=True)]
    all_to_all x1, blocking collectives: 20.7 us -> 19.1 us  [exchange(): lax.all_to_all(values, 'dev', split_axis=0, concat_axis=0, tiled=True)]
    pallas_call x1, Pallas kernels: 9.19 us -> 7.55 us  [local(): pl.pallas_call(grads_kernel, out_shape=(jax.ShapeDtypeStruct((PARAMS, 409...]
    slice x1 -> x0, local copies, waits for them, and re-layouts: 1.19 us -> none  [camera_table(): rest = [cameras[:, :, 5], cameras[:, :, 6], cameras[:, :, 7]]]
    unnamed x21 -> x8, local copies, waits for them, and re-layouts: 3.81 us -> 3.89 us
  transfers between devices with their start and end apart: 1 -> 1, of which waited for: 1 -> 1; matrix products, arithmetic and copies ran while one was open for 1% -> 2% of each run, Pallas kernels for 7% -> 7%
where the time goes in v5:
time: 106 us
  Pallas kernels  63.1 us (60%)
  blocking collectives  19.1 us (18%)
  starting transfers between devices  11.5 us (11%)
  waiting for transfers between devices  6.43 us (6%)
  local copies, waits for them, and re-layouts  3.89 us (4%)
    pallas_call x1, Pallas kernels, local(): pl.pallas_call(blend_kernel, out_shape=jax.ShapeDtypeStruct((OWNERS, 8, 1...  36.4 us
    all_to_all x1, blocking collectives, exchange(): lax.all_to_all(values, 'dev', split_axis=0, concat_axis=0, tiled=True)  19.1 us
    all_to_all x1, starting transfers between devices, exchange(): lax.all_to_all(values, 'dev', split_axis=0, concat_axis=0, tiled=True)  11.5 us
    pallas_call x1, Pallas kernels, local(): pl.pallas_call(offer_kernel, out_shape=(jax.ShapeDtypeStruct((OWNERS * 12...  11.5 us
    pallas_call x1, Pallas kernels, local(): pl.pallas_call(plan_kernel, out_shape=(jax.ShapeDtypeStruct((BATCHES, 32,...  7.7 us
    pallas_call x1, Pallas kernels, local(): pl.pallas_call(grads_kernel, out_shape=(jax.ShapeDtypeStruct((PARAMS, 409...  7.55 us
    all_to_all x1, waiting for transfers between devices, exchange(): lax.all_to_all(values, 'dev', split_axis=0, concat_axis=0, tiled=True)  6.43 us
    unnamed x8, local copies, waits for them, and re-layouts  3.89 us
  transfers between devices with their start and end apart: 1, of which 1 were waited for; matrix products, arithmetic and copies ran while one was open for 2% of the time, Pallas kernels for 7%

profile of v5, /device:TPU:1, one launch (start us, length us, event | category | flops | bytes accessed | tf_op | source)
XLA Modules:
  0.0 105.5 jit_solution(5004579924601163485)
XLA Ops:
  0.6 1.5 %copy.14.list_ref = s32[2,1,128,32]{3,2,1,0:T(8,128)} copy(s32[2,1,128,32]{2,3,1,0:T(8,128)} %param.9) | data formatting | bytes 65536 | tf_op args[2]
  2.1 11.5 %offer.1 = (f32[1536,128]{1,0:T(8,128)}, f32[136,128]{1,0:T(8,128)}, s32[2,16,256]{2,1,0:T(8,128)}) custom-call(f32[2,4,8]{2,1,0:T(4,128)} %camera_ref.1, f32[59,4096]{1,0:T(8,128)} %params_ref.3, s32[2,1,128,32]{3,2,1,0:T(8,128)} %copy.14.list_ref), custom_call_target="tpu_custom_call" | custom-call | tf_op jit(solution)/shard_map/offer/pallas_call | solution.py:941
  13.6 0.0 copy-start.1
  13.6 11.5 %all-to-all-start = ((f32[128,1,1536]{2,1,0:T(1,128)}), f32[128,1,1536]{2,1,0:T(1,128)S(1)}, u32[]{:S(2)}, u32[]{:S(2)}) async-start(f32[128,1,1536]{2,1,0:T(1,128)} %bitcast.5), calls=%async_computation | async-start | bytes 1572864 | tf_op jit(solution)/shard_map/all_to_all | solution.py:921
  25.1 0.0 copy-done.1
  25.1 0.8 copy.16.target_ref
  26.0 0.0 copy-start.2
  26.0 0.7 copy-done.2
  26.6 0.2 convert_reduce_fusion
  26.8 0.7 select_reduce_fusion.order_ref
  27.5 7.7 %plan.1 = (f32[2,32,128]{2,1,0:T(8,128)}, s32[2,64,128]{2,1,0:T(8,128)}, f32[2,32,128]{2,1,0:T(8,128)}, f32[2,96,256]{2,1,0:T(8,128)}) custom-call(s32[2,32]{1,0:T(2,128)} %select_reduce_fusion.order_ref, s32[2,32]{1,0:T(2,128)} %ids_ref.1, s32[2,32]{1,0:T(2,128)} %bitcast.6, s32[2,32,256]{2,1,0:T(8,128)} %slots_ref.1, f32[2,32,3,256]{3,2,1,0:T(4,128)} %copy.16.target_ref), custom_call_target="tpu_custom_call" | custom-call | tf_op jit(solution)/shard_map/plan/pallas_call | solution.py:961
  35.2 6.4 %all-to-all-done = f32[128,1,1536]{2,1,0:T(1,128)S(1)} async-done(((f32[128,1,1536]{2,1,0:T(1,128)}), f32[128,1,1536]{2,1,0:T(1,128)S(1)}, u32[]{:S(2)}, u32[]{:S(2)}) %all-to-all-start) | async-done | bytes 786464 | tf_op jit(solution)/shard_map/all_to_all | solution.py:921
  41.7 0.0 copy-start
  41.7 0.9 copy-done
  42.5 36.4 %blend.1 = f32[128,8,128]{2,1,0:T(8,128)} custom-call(s32[2,32]{1,0:T(2,128)} %select_reduce_fusion.order_ref, s32[2,32]{1,0:T(2,128)} %bitcast.7, f32[136,128]{1,0:T(8,128)} %get-tuple-element.11.cam_ref, f32[1536,128]{1,0:T(8,128)} %bitcast.4, f32[2,32,128]{2,1,0:T(8,128)} %get-tuple-element.14.view_ref, s32[2,64,128]{2,1,0:T(8,128)} %get-tuple-element.15.ix_ref, ...), custom_call_target="tpu_custom_call" | custom-call | tf_op jit(solution)/shard_map/blend/pallas_call | solution.py:977
  78.9 19.1 %all_to_all.10.grad_ref = f32[128,8,128]{2,1,0:T(8,128)} all-to-all(f32[128,8,128]{2,1,0:T(8,128)} %blend.1), channel_id=1, replica_groups=mesh['dev'=128] {'dev'}, dimensions={0} | all-to-all | bytes 1048576 | tf_op jit(solution)/shard_map/all_to_all | solution.py:921
  98.0 7.5 %param_grads.1 = (f32[59,4096]{1,0:T(8,128)}, f32[1,1]{1,0:T(1,128)}) custom-call(f32[136,128]{1,0:T(8,128)} %get-tuple-element.11.cam_ref, f32[59,4096]{1,0:T(8,128)} %params_ref.3, s32[2,16,256]{2,1,0:T(8,128)} %get-tuple-element.12.send_ref, f32[128,8,128]{2,1,0:T(8,128)} %all_to_all.10.grad_ref), custom_call_target="tpu_custom_call" | custom-call | tf_op jit(solution)/shard_map/param_grads/pallas_call | solution.py:1005
  (1 shorter events, 0.0 us)
Async XLA Ops:
  13.6 11.5 %copy-start.1 = (f32[2,32,3,256]{3,1,2,0:T(8,128)S(1)}, f32[2,32,3,256]{3,1,2,0:T(8,128)}, u32[]{:S(2)}) copy-start(f32[2,32,3,256]{3,1,2,0:T(8,128)} %param.13) | copy-start | bytes 589828
  13.6 28.0 %all-to-all-start = ((f32[128,1,1536]{2,1,0:T(1,128)}), f32[128,1,1536]{2,1,0:T(1,128)S(1)}, u32[]{:S(2)}, u32[]{:S(2)}) async-start(f32[128,1,1536]{2,1,0:T(1,128)} %bitcast.5), calls=%async_computation | async-start | bytes 1572864 | tf_op jit(solution)/shard_map/all_to_all | solution.py:921
  26.0 0.7 copy-start.2
  41.7 0.9 copy-start

commit v6 on v5

--- a/solution.py
+++ b/solution.py
@@ -20,7 +20,6 @@
 GROUPS = 4
 PITCH = 72
 LOG2_E = 1.4426950408889634
-VMEM_BYTES = 56 * 1024 * 1024
 
 SH_ZERO = 0.28209479177387814
 SH_ONE = 0.4886025119029199
@@ -253,16 +252,16 @@
     for field, value in enumerate(camera_table(cameras)):
         cam_ref[field * 8 : field * 8 + 8, :] = value
     for batch_no in range(BATCHES):
+        by_owner = jnp.transpose(
+            jnp.concatenate([list_ref[batch_no, 0].astype(F32)] * 4, axis=0)
+        )
         for chunk in range(16):
-            lists = list_ref[batch_no, 0, chunk * 8 : chunk * 8 + 8, :].astype(F32)
-            lists = jnp.where(place, jnp.concatenate([lists] * 4, axis=1), 0.0)
+            lists = jnp.where(place, by_owner[chunk * 8 : chunk * 8 + 8], 0.0)
             for half in range(2):
                 line = jnp.sum(lists[half * 4 : half * 4 + 4], axis=0, keepdims=True)
                 send_ref[batch_no, chunk : chunk + 1, half * 128 : half * 128 + 128] = line.astype(
                     jnp.int32
                 )
-    for copy in copies:
-        copy.wait()
 
     def block(block_no, carry):
         row0 = (block_no // 2) * 8
@@ -288,7 +287,10 @@
                 tab_ref[batch_no, pl.ds(start, 8, stride=48), :] = value
         return carry
 
-    lax.fori_loop(0, 4, block, 0)
+    for part in range(2):
+        for copy in copies[part * 16 : part * 16 + 16]:
+            copy.wait()
+        lax.fori_loop(part * 2, part * 2 + 2, block, 0)
 
     def pieces(step, carry):
         for batch_no in range(BATCHES):
@@ -897,7 +899,6 @@
             res_ref[pl.ds((2 * row0 + half) * PITCH + p, 8, stride=2 * PITCH), :] = value
         return carry
 
-    lax.fori_loop(0, 4, block, 0)
     copies = [
         pltpu.make_async_copy(
             res_ref.at[pl.ds(j * PITCH, PARAMS), :],
@@ -906,8 +907,10 @@
         )
         for j in range(32)
     ]
-    for copy in copies:
-        copy.start()
+    for part in range(2):
+        lax.fori_loop(part * 2, part * 2 + 2, block, 0)
+        for copy in copies[part * 16 : part * 16 + 16]:
+            copy.start()
     lane = lax.broadcasted_iota(jnp.int32, (1, 128), 1)
     errors = jnp.sum(
         jnp.where((lane == 32) | (lane == 96), total[7:8], 0.0), axis=1, keepdims=True
@@ -923,8 +926,10 @@
 
 SMEM = pl.BlockSpec(memory_space=pltpu.SMEM)
 VMEM = pl.BlockSpec(memory_space=pltpu.VMEM)
-HBM = pl.BlockSpec(memory_space=pl.ANY)
-CALL = pltpu.CompilerParams(vmem_limit_bytes=VMEM_BYTES)
+HBM = pl.BlockSpec(memory_space=pltpu.HBM)
+CALL = pltpu.CompilerParams(vmem_limit_bytes=16 * 1024 * 1024)
+OFFER_CALL = pltpu.CompilerParams(vmem_limit_bytes=60 * 1024 * 1024)
+BLEND_CALL = pltpu.CompilerParams(vmem_limit_bytes=28 * 1024 * 1024)
 
 
 def local(params, cameras, send_lists, tile_slots, tile_ids, tile_len, targets):
@@ -953,9 +958,9 @@
             pltpu.VMEM((BATCHES, 512, 256), BF16),
             pltpu.SemaphoreType.DMA((32,)),
         ],
-        compiler_params=CALL,
+        compiler_params=OFFER_CALL,
         name="offer",
-    )(cameras, params, send_lists)
+    )(cameras, params, jnp.transpose(send_lists, (0, 1, 3, 2)))
     feats = exchange(feats.reshape(OWNERS, 1, 1536)).reshape(OWNERS * 12, 128)
 
     views, slots, tiles, aims = pl.pallas_call(
@@ -997,7 +1002,7 @@
             pltpu.VMEM((BATCHES, 2, 256, 128), F32),
             pltpu.VMEM((BATCHES, 24, 256), F32),
         ],
-        compiler_params=CALL,
+        compiler_params=BLEND_CALL,
         name="blend",
     )(order, lengths, cams, feats, views, slots, tiles, aims)
     slot_grads = exchange(slot_grads)

time: 106 us -> 99.6 us (0.940)
  Pallas kernels: 63.1 us -> 59.7 us
  local copies, waits for them, and re-layouts: 3.89 us -> 1.39 us
  waiting for transfers between devices: 6.43 us -> 8.15 us
  blocking collectives: 19.1 us -> 17.9 us
    unnamed x8 -> x15, local copies, waits for them, and re-layouts: 3.89 us -> 1.39 us
    all_to_all x1, waiting for transfers between devices: 6.43 us -> 8.15 us  [exchange(): lax.all_to_all(values, 'dev', split_axis=0, concat_axis=0, tiled=True)]
    all_to_all x1, blocking collectives: 19.1 us -> 17.9 us  [exchange(): lax.all_to_all(values, 'dev', split_axis=0, concat_axis=0, tiled=True)]
    pallas_call x1, Pallas kernels: 7.55 us -> 6.41 us  [local(): pl.pallas_call(grads_kernel, out_shape=(jax.ShapeDtypeStruct((PARAMS, 409...]
  transfers between devices with their start and end apart: 1 -> 1, of which waited for: 1 -> 1; matrix products, arithmetic and copies ran while one was open for 2% -> 0% of each run, Pallas kernels for 7% -> 7%
where the time goes in v6:
time: 99.6 us; the launch traced here: 99.7 us
  Pallas kernels  59.7 us (60%)
  blocking collectives  17.9 us (18%)
  starting transfers between devices  11.5 us (12%)
  waiting for transfers between devices  8.15 us (8%)
  local copies, waits for them, and re-layouts  1.39 us (1%)
    pallas_call x1, Pallas kernels, local(): pl.pallas_call(blend_kernel, out_shape=jax.ShapeDtypeStruct((OWNERS, 8, 1...  35.5 us
    all_to_all x1, blocking collectives, exchange(): lax.all_to_all(values, 'dev', split_axis=0, concat_axis=0, tiled=True)  17.9 us
    all_to_all x1, starting transfers between devices, exchange(): lax.all_to_all(values, 'dev', split_axis=0, concat_axis=0, tiled=True)  11.5 us
    pallas_call x1, Pallas kernels, local(): pl.pallas_call(offer_kernel, out_shape=(jax.ShapeDtypeStruct((OWNERS * 12...  11 us
    all_to_all x1, waiting for transfers between devices, exchange(): lax.all_to_all(values, 'dev', split_axis=0, concat_axis=0, tiled=True)  8.15 us
    pallas_call x1, Pallas kernels, local(): pl.pallas_call(plan_kernel, out_shape=(jax.ShapeDtypeStruct((BATCHES, 32,...  6.65 us
    pallas_call x1, Pallas kernels, local(): pl.pallas_call(grads_kernel, out_shape=(jax.ShapeDtypeStruct((PARAMS, 409...  6.41 us
  transfers between devices with their start and end apart: 1, of which 1 were waited for; matrix products, arithmetic and copies ran while one was open for 0% of the time, Pallas kernels for 7%

profile of v6, /device:TPU:1, one launch (start us, length us, event | category | flops | bytes accessed | tf_op | source)
XLA Modules:
  0.0 99.7 jit_solution(6290714300466379334)
XLA Ops:
  0.6 11.0 %offer.1 = (f32[1536,128]{1,0:T(8,128)}, f32[136,128]{1,0:T(8,128)}, s32[2,16,256]{2,1,0:T(8,128)}) custom-call(f32[2,4,8]{2,1,0:T(4,128)} %camera_ref.1, f32[59,4096]{1,0:T(8,128)} %params_ref.3, s32[2,1,32,128]{3,2,1,0:T(8,128)} %bitcast.10), custom_call_target="tpu_custom_call" | custom-call | tf_op jit(solution)/shard_map/offer/pallas_call | solution.py:946
  11.7 0.0 copy-start.6
  11.7 11.5 %all-to-all-start = ((f32[128,1,1536]{2,1,0:T(1,128)}), f32[128,1,1536]{2,1,0:T(1,128)S(1)}, u32[]{:S(2)}, u32[]{:S(2)}) async-start(f32[128,1,1536]{2,1,0:T(1,128)} %bitcast.9), calls=%async_computation | async-start | bytes 1572864 | tf_op jit(solution)/shard_map/all_to_all | solution.py:924
  23.2 0.0 copy-done.6
  23.2 0.0 copy-start.2
  23.2 0.1 copy.13.target_ref
  23.4 0.0 copy-start.4
  23.4 0.7 copy-done.4
  24.1 0.2 convert_reduce_fusion
  24.3 0.0 copy-start.5
  24.3 0.1 select_reduce_fusion.order_ref
  24.4 0.0 copy-done.2
  24.4 0.6 copy-done.5
  24.9 0.0 copy-start.1
  24.9 6.7 %plan.1 = (f32[2,32,128]{2,1,0:T(8,128)S(1)}, s32[2,64,128]{2,1,0:T(8,128)S(1)}, f32[2,32,128]{2,1,0:T(8,128)S(1)}, f32[2,96,256]{2,1,0:T(8,128)S(1)}) custom-call(s32[2,32]{1,0:T(2,128)S(1)} %select_reduce_fusion.order_ref, s32[2,32]{1,0:T(2,128)S(1)} %copy-done.5, s32[2,32]{1,0:T(2,128)S(1)} %bitcast.7, s32[2,32,256]{2,1,0:T(8,128)S(1)} %copy-done.2, ...), custom_call_target="tpu_custom_call" | custom-call | tf_op jit(solution)/shard_map/plan/pallas_call | solution.py:966
  31.6 8.2 %all-to-all-done = f32[128,1,1536]{2,1,0:T(1,128)S(1)} async-done(((f32[128,1,1536]{2,1,0:T(1,128)}), f32[128,1,1536]{2,1,0:T(1,128)S(1)}, u32[]{:S(2)}, u32[]{:S(2)}) %all-to-all-start) | async-done | bytes 786464 | tf_op jit(solution)/shard_map/all_to_all | solution.py:924
  39.7 0.0 copy-done.1
  39.8 0.0 copy-start
  39.8 35.5 %blend.1 = f32[128,8,128]{2,1,0:T(8,128)S(1)} custom-call(s32[2,32]{1,0:T(2,128)S(1)} %select_reduce_fusion.order_ref, s32[2,32]{1,0:T(2,128)S(1)} %bitcast.8, f32[136,128]{1,0:T(8,128)S(1)} %copy-done.1, f32[1536,128]{1,0:T(8,128)S(1)} %bitcast.5, f32[2,32,128]{2,1,0:T(8,128)S(1)} %get-tuple-element.14.view_ref, ...), custom_call_target="tpu_custom_call" | custom-call | tf_op jit(solution)/shard_map/blend/pallas_call | solution.py:982
  75.3 0.0 copy-start.3
  75.3 17.9 %all_to_all.10.grad_ref = f32[128,8,128]{2,1,0:T(8,128)S(1)} all-to-all(f32[128,8,128]{2,1,0:T(8,128)S(1)} %blend.1), channel_id=1, replica_groups=mesh['dev'=128] {'dev'}, dimensions={0} | all-to-all | bytes 1048576 | tf_op jit(solution)/shard_map/all_to_all | solution.py:924
  93.3 0.0 copy-done
  93.3 0.0 copy-done.3
  93.3 6.4 %param_grads.1 = (f32[59,4096]{1,0:T(8,128)}, f32[1,1]{1,0:T(1,128)}) custom-call(f32[136,128]{1,0:T(8,128)S(1)} %copy-done.1, f32[59,4096]{1,0:T(8,128)S(1)} %copy-done, s32[2,16,256]{2,1,0:T(8,128)S(1)} %copy-done.3, f32[128,8,128]{2,1,0:T(8,128)S(1)} %all_to_all.10.grad_ref), custom_call_target="tpu_custom_call" | custom-call | tf_op jit(solution)/shard_map/param_grads/pallas_call | solution.py:1010
  (1 shorter events, 0.0 us)
Async XLA Ops:
  11.7 11.5 %copy-start.6 = (f32[2,32,3,256]{3,1,2,0:T(8,128)S(1)}, f32[2,32,3,256]{3,1,2,0:T(8,128)}, u32[]{:S(2)}) copy-start(f32[2,32,3,256]{3,1,2,0:T(8,128)} %param.13) | copy-start | bytes 589828
  11.7 28.1 %all-to-all-start = ((f32[128,1,1536]{2,1,0:T(1,128)}), f32[128,1,1536]{2,1,0:T(1,128)S(1)}, u32[]{:S(2)}, u32[]{:S(2)}) async-start(f32[128,1,1536]{2,1,0:T(1,128)} %bitcast.9), calls=%async_computation | async-start | bytes 1572864 | tf_op jit(solution)/shard_map/all_to_all | solution.py:924
  23.2 1.2 %copy-start.2 = (s32[2,32,256]{2,1,0:T(8,128)S(1)}, s32[2,32,256]{2,1,0:T(8,128)}, u32[]{:S(2)}) copy-start(s32[2,32,256]{2,1,0:T(8,128)} %slots_ref.1) | copy-start | bytes 196612
  23.4 0.7 copy-start.4
  24.3 0.7 copy-start.5
  24.9 14.8 %copy-start.1 = (f32[136,128]{1,0:T(8,128)S(1)}, f32[136,128]{1,0:T(8,128)}, u32[]{:S(2)}) copy-start(f32[136,128]{1,0:T(8,128)} %get-tuple-element.11.cam_ref) | copy-start | bytes 208900
  39.8 53.5 %copy-start = (f32[59,4096]{1,0:T(8,128)S(1)}, f32[59,4096]{1,0:T(8,128)}, u32[]{:S(2)}) copy-start(f32[59,4096]{1,0:T(8,128)} %params_ref.3) | copy-start | bytes 2899972
  75.3 17.9 %copy-start.3 = (s32[2,16,256]{2,1,0:T(8,128)S(1)}, s32[2,16,256]{2,1,0:T(8,128)}, u32[]{:S(2)}) copy-start(s32[2,16,256]{2,1,0:T(8,128)} %get-tuple-element.12.send_ref) | copy-start | bytes 98308

commit v7 on v6

--- a/solution.py
+++ b/solution.py
@@ -450,21 +450,16 @@
         ),
     )
     basis_b = jnp.concatenate([basis] * 4, axis=0).astype(BF16)
-    basis_t = jnp.transpose(
-        jnp.concatenate([basis, jnp.zeros((120, 256), F32)], axis=0)
-    ).astype(BF16)
+    basis_2 = jnp.concatenate([jnp.concatenate([basis, basis], axis=1)] * 2, axis=0).astype(BF16)
     row_t = lax.broadcasted_iota(jnp.int32, (256, 128), 0) & 7
     lane_t = lax.broadcasted_iota(jnp.int32, (256, 128), 1)
-    own = (lane_t < 8) | ((lane_t & 7) == row_t)
+    own = (lane_t & 7) == row_t
     zero8 = jnp.zeros((8, 128), F32)
     both = range(BATCHES)
 
     sg_ref[...] = jnp.zeros(sg_ref.shape, F32)
     co_ref[...] = jnp.zeros(co_ref.shape, F32)
     err_ref[...] = jnp.zeros(err_ref.shape, F32)
-    for b in both:
-        rt_ref[b, 0:256, :] = basis_t
-        rt_ref[b, 256:512, :] = basis_t
 
     upper = sub < 4
 
@@ -679,12 +674,10 @@
             r_hi, r_lo = split2(2.0 * resid)
             r_four.append(jnp.concatenate([r_hi, r_hi, r_lo, r_lo], axis=0).astype(BF16))
             r_t = jnp.transpose(
-                jnp.concatenate(
-                    [jnp.zeros((8, 256), F32), r_hi, r_lo, jnp.zeros((72, 256), F32)], axis=0
-                )
+                jnp.concatenate([r_hi, r_lo, jnp.zeros((80, 256), F32)], axis=0)
             ).astype(BF16)
-            rt_ref[b, 512:768, :] = r_t
-            rt_ref[b, 768:1024, :] = r_t
+            rt_ref[b, 0:256, :] = r_t
+            rt_ref[b, 256:512, :] = r_t
 
         def pull(b, i):
             c_two = colours_of(b, i)
@@ -707,15 +700,15 @@
 
         def collect(b, i):
             row0 = pl.multiple_of(i * 256, 256)
-            lhs = jnp.concatenate([dd_ref[b], ww_ref[b, pl.ds(row0, 256), :]], axis=1)
-            sums = jnp.where(own, dot(lhs, rt_ref[b], NN), 0.0)
+            mom = dot(basis_2, dd_ref[b], NT)
+            sums = jnp.where(own, dot(ww_ref[b, pl.ds(row0, 256), :], rt_ref[b], NN), 0.0)
             for n in range(2):
                 flip = jnp.transpose(sums[n * 128 : n * 128 + 128])
                 j = i * 2 + n
-                mo_ref[b, pl.ds(j, 8, stride=16), :] = flip[0:8]
+                mo_ref[b, pl.ds(j, 8, stride=16), :] = mom[0:8, n * 128 : n * 128 + 128]
                 for h in range(3):
                     mo_ref[b, pl.ds((8 + h) * 16 + j, 1), :] = jnp.sum(
-                        flip[8 + h * 8 : 16 + h * 8] + flip[32 + h * 8 : 40 + h * 8],
+                        flip[h * 8 : h * 8 + 8] + flip[24 + h * 8 : 32 + h * 8],
                         axis=0,
                         keepdims=True,
                     )
@@ -996,7 +989,7 @@
             pltpu.VMEM((BATCHES, rows, 512), BF16),
             pltpu.VMEM((BATCHES, 256, 256), F32),
             pltpu.VMEM((BATCHES, 256, 512), BF16),
-            pltpu.VMEM((BATCHES, 1024, 128), BF16),
+            pltpu.VMEM((BATCHES, 512, 128), BF16),
             pltpu.VMEM((BATCHES, 176, 128), F32),
             pltpu.VMEM((BATCHES, 288, 128), F32),
             pltpu.VMEM((BATCHES, 2, 256, 128), F32),

time: 99.6 us -> 99 us (level)
  Pallas kernels: 59.7 us -> 57.1 us
  blocking collectives: 17.9 us -> 19.5 us
    pallas_call x1, Pallas kernels: 35.5 us -> 33 us  [local(): pl.pallas_call(blend_kernel, out_shape=jax.ShapeDtypeStruct((OWNERS, 8, 1...]
    all_to_all x1, blocking collectives: 17.9 us -> 19.5 us  [exchange(): lax.all_to_all(values, 'dev', split_axis=0, concat_axis=0, tiled=True)]
where the time goes in v7:
time: 99 us; the launch traced here: 98.6 us
  Pallas kernels  57.1 us (58%)
  blocking collectives  19.5 us (20%)
  starting transfers between devices  11.5 us (12%)
  waiting for transfers between devices  8.15 us (8%)
  local copies, waits for them, and re-layouts  1.39 us (1%)
    pallas_call x1, Pallas kernels, local(): pl.pallas_call(blend_kernel, out_shape=jax.ShapeDtypeStruct((OWNERS, 8, 1...  33 us
    all_to_all x1, blocking collectives, exchange(): lax.all_to_all(values, 'dev', split_axis=0, concat_axis=0, tiled=True)  19.5 us
    all_to_all x1, starting transfers between devices, exchange(): lax.all_to_all(values, 'dev', split_axis=0, concat_axis=0, tiled=True)  11.5 us
    pallas_call x1, Pallas kernels, local(): pl.pallas_call(offer_kernel, out_shape=(jax.ShapeDtypeStruct((OWNERS * 12...  11 us
    all_to_all x1, waiting for transfers between devices, exchange(): lax.all_to_all(values, 'dev', split_axis=0, concat_axis=0, tiled=True)  8.15 us
    pallas_call x1, Pallas kernels, local(): pl.pallas_call(plan_kernel, out_shape=(jax.ShapeDtypeStruct((BATCHES, 32,...  6.65 us
    pallas_call x1, Pallas kernels, local(): pl.pallas_call(grads_kernel, out_shape=(jax.ShapeDtypeStruct((PARAMS, 409...  6.41 us
  transfers between devices with their start and end apart: 1, of which 1 were waited for; matrix products, arithmetic and copies ran while one was open for 0% of the time, Pallas kernels for 7%

profile of v7, /device:TPU:1, one launch (start us, length us, event | category | flops | bytes accessed | tf_op | source)
XLA Modules:
  0.0 98.6 jit_solution(16375231004830021667)
XLA Ops:
  0.6 11.0 %offer.1 = (f32[1536,128]{1,0:T(8,128)}, f32[136,128]{1,0:T(8,128)}, s32[2,16,256]{2,1,0:T(8,128)}) custom-call(f32[2,4,8]{2,1,0:T(4,128)} %camera_ref.1, f32[59,4096]{1,0:T(8,128)} %params_ref.3, s32[2,1,32,128]{3,2,1,0:T(8,128)} %bitcast.10), custom_call_target="tpu_custom_call" | custom-call | tf_op jit(solution)/shard_map/offer/pallas_call | solution.py:939
  11.7 0.0 copy-start.6
  11.7 11.5 %all-to-all-start = ((f32[128,1,1536]{2,1,0:T(1,128)}), f32[128,1,1536]{2,1,0:T(1,128)S(1)}, u32[]{:S(2)}, u32[]{:S(2)}) async-start(f32[128,1,1536]{2,1,0:T(1,128)} %bitcast.9), calls=%async_computation | async-start | bytes 1572864 | tf_op jit(solution)/shard_map/all_to_all | solution.py:917
  23.2 0.0 copy-done.6
  23.2 0.0 copy-start.2
  23.2 0.1 copy.13.target_ref
  23.4 0.0 copy-start.4
  23.4 0.7 copy-done.4
  24.1 0.2 convert_reduce_fusion
  24.3 0.0 copy-start.5
  24.3 0.1 select_reduce_fusion.order_ref
  24.4 0.0 copy-done.2
  24.4 0.6 copy-done.5
  24.9 0.0 copy-start.1
  24.9 6.7 %plan.1 = (f32[2,32,128]{2,1,0:T(8,128)S(1)}, s32[2,64,128]{2,1,0:T(8,128)S(1)}, f32[2,32,128]{2,1,0:T(8,128)S(1)}, f32[2,96,256]{2,1,0:T(8,128)S(1)}) custom-call(s32[2,32]{1,0:T(2,128)S(1)} %select_reduce_fusion.order_ref, s32[2,32]{1,0:T(2,128)S(1)} %copy-done.5, s32[2,32]{1,0:T(2,128)S(1)} %bitcast.7, s32[2,32,256]{2,1,0:T(8,128)S(1)} %copy-done.2, ...), custom_call_target="tpu_custom_call" | custom-call | tf_op jit(solution)/shard_map/plan/pallas_call | solution.py:959
  31.6 8.2 %all-to-all-done = f32[128,1,1536]{2,1,0:T(1,128)S(1)} async-done(((f32[128,1,1536]{2,1,0:T(1,128)}), f32[128,1,1536]{2,1,0:T(1,128)S(1)}, u32[]{:S(2)}, u32[]{:S(2)}) %all-to-all-start) | async-done | bytes 786464 | tf_op jit(solution)/shard_map/all_to_all | solution.py:917
  39.7 0.0 copy-done.1
  39.8 0.0 copy-start
  39.8 33.0 %blend.1 = f32[128,8,128]{2,1,0:T(8,128)S(1)} custom-call(s32[2,32]{1,0:T(2,128)S(1)} %select_reduce_fusion.order_ref, s32[2,32]{1,0:T(2,128)S(1)} %bitcast.8, f32[136,128]{1,0:T(8,128)S(1)} %copy-done.1, f32[1536,128]{1,0:T(8,128)S(1)} %bitcast.5, f32[2,32,128]{2,1,0:T(8,128)S(1)} %get-tuple-element.14.view_ref, ...), custom_call_target="tpu_custom_call" | custom-call | tf_op jit(solution)/shard_map/blend/pallas_call | solution.py:975
  72.7 0.0 copy-start.3
  72.7 19.5 %all_to_all.10.grad_ref = f32[128,8,128]{2,1,0:T(8,128)S(1)} all-to-all(f32[128,8,128]{2,1,0:T(8,128)S(1)} %blend.1), channel_id=1, replica_groups=mesh['dev'=128] {'dev'}, dimensions={0} | all-to-all | bytes 1048576 | tf_op jit(solution)/shard_map/all_to_all | solution.py:917
  92.2 0.0 copy-done
  92.2 0.0 copy-done.3
  92.2 6.4 %param_grads.1 = (f32[59,4096]{1,0:T(8,128)}, f32[1,1]{1,0:T(1,128)}) custom-call(f32[136,128]{1,0:T(8,128)S(1)} %copy-done.1, f32[59,4096]{1,0:T(8,128)S(1)} %copy-done, s32[2,16,256]{2,1,0:T(8,128)S(1)} %copy-done.3, f32[128,8,128]{2,1,0:T(8,128)S(1)} %all_to_all.10.grad_ref), custom_call_target="tpu_custom_call" | custom-call | tf_op jit(solution)/shard_map/param_grads/pallas_call | solution.py:1003
  (1 shorter events, 0.0 us)
Async XLA Ops:
  11.7 11.5 %copy-start.6 = (f32[2,32,3,256]{3,1,2,0:T(8,128)S(1)}, f32[2,32,3,256]{3,1,2,0:T(8,128)}, u32[]{:S(2)}) copy-start(f32[2,32,3,256]{3,1,2,0:T(8,128)} %param.13) | copy-start | bytes 589828
  11.7 28.1 %all-to-all-start = ((f32[128,1,1536]{2,1,0:T(1,128)}), f32[128,1,1536]{2,1,0:T(1,128)S(1)}, u32[]{:S(2)}, u32[]{:S(2)}) async-start(f32[128,1,1536]{2,1,0:T(1,128)} %bitcast.9), calls=%async_computation | async-start | bytes 1572864 | tf_op jit(solution)/shard_map/all_to_all | solution.py:917
  23.2 1.2 %copy-start.2 = (s32[2,32,256]{2,1,0:T(8,128)S(1)}, s32[2,32,256]{2,1,0:T(8,128)}, u32[]{:S(2)}) copy-start(s32[2,32,256]{2,1,0:T(8,128)} %slots_ref.1) | copy-start | bytes 196612
  23.4 0.7 copy-start.4
  24.3 0.7 copy-start.5
  24.9 14.8 %copy-start.1 = (f32[136,128]{1,0:T(8,128)S(1)}, f32[136,128]{1,0:T(8,128)}, u32[]{:S(2)}) copy-start(f32[136,128]{1,0:T(8,128)} %get-tuple-element.11.cam_ref) | copy-start | bytes 208900
  39.8 52.4 %copy-start = (f32[59,4096]{1,0:T(8,128)S(1)}, f32[59,4096]{1,0:T(8,128)}, u32[]{:S(2)}) copy-start(f32[59,4096]{1,0:T(8,128)} %params_ref.3) | copy-start | bytes 2899972
  72.7 19.5 %copy-start.3 = (s32[2,16,256]{2,1,0:T(8,128)S(1)}, s32[2,16,256]{2,1,0:T(8,128)}, u32[]{:S(2)}) copy-start(s32[2,16,256]{2,1,0:T(8,128)} %get-tuple-element.12.send_ref) | copy-start | bytes 98308

commit v8 on v7

--- a/solution.py
+++ b/solution.py
@@ -816,13 +816,13 @@
     gg_ref[...] = jnp.zeros(gg_ref.shape, F32)
 
     def place(step, total):
-        tiles_of = [[grad_ref[step * 16 + n * 8 + i] for i in range(8)] for n in range(2)]
-        for tile in tiles_of[0] + tiles_of[1]:
+        tiles_of = [[grad_ref[step * 32 + n * 8 + i] for i in range(8)] for n in range(4)]
+        for tile in sum(tiles_of, []):
             total = total + tile
         sums = [None] * BATCHES
-        for part, batch_no in [(n, b) for n in range(2) for b in range(BATCHES)]:
+        for part, batch_no in [(n, b) for n in range(4) for b in range(BATCHES)]:
             tiles = tiles_of[part]
-            index = send_ref[batch_no, pl.ds(step * 2 + part, 1), :]
+            index = send_ref[batch_no, pl.ds(step * 4 + part, 1), :]
             hit = row_a == (index >> 8)
             rhs = scatter_rhs(index)
             high = []
@@ -849,7 +849,7 @@
             gg_ref[batch_no] += sums[batch_no]
         return total
 
-    total = lax.fori_loop(0, 8, place, jnp.zeros((8, 128), F32))
+    total = lax.fori_loop(0, 4, place, jnp.zeros((8, 128), F32))
     for copy in copies:
         copy.wait()
 

time: 99 us -> 98.3 us (level)
  Pallas kernels: 57.1 us -> 56.1 us
where the time goes in v8:
time: 98.3 us; the launch traced here: 97.3 us
  Pallas kernels  56.1 us (57%)
  blocking collectives  19.1 us (19%)
  starting transfers between devices  11.5 us (12%)
  waiting for transfers between devices  8.15 us (8%)
  local copies, waits for them, and re-layouts  1.39 us (1%)
    pallas_call x1, Pallas kernels, local(): pl.pallas_call(blend_kernel, out_shape=jax.ShapeDtypeStruct((OWNERS, 8, 1...  33 us
    all_to_all x1, blocking collectives, exchange(): lax.all_to_all(values, 'dev', split_axis=0, concat_axis=0, tiled=True)  19.1 us
    all_to_all x1, starting transfers between devices, exchange(): lax.all_to_all(values, 'dev', split_axis=0, concat_axis=0, tiled=True)  11.5 us
    pallas_call x1, Pallas kernels, local(): pl.pallas_call(offer_kernel, out_shape=(jax.ShapeDtypeStruct((OWNERS * 12...  11 us
    all_to_all x1, waiting for transfers between devices, exchange(): lax.all_to_all(values, 'dev', split_axis=0, concat_axis=0, tiled=True)  8.15 us
    pallas_call x1, Pallas kernels, local(): pl.pallas_call(plan_kernel, out_shape=(jax.ShapeDtypeStruct((BATCHES, 32,...  6.65 us
    pallas_call x1, Pallas kernels, local(): pl.pallas_call(grads_kernel, out_shape=(jax.ShapeDtypeStruct((PARAMS, 409...  5.48 us
  transfers between devices with their start and end apart: 1, of which 1 were waited for; matrix products, arithmetic and copies ran while one was open for 0% of the time, Pallas kernels for 7%

profile of v8, /device:TPU:1, one launch (start us, length us, event | category | flops | bytes accessed | tf_op | source)
XLA Modules:
  0.0 97.3 jit_solution(26468259713574396)
XLA Ops:
  0.6 11.0 %offer.1 = (f32[1536,128]{1,0:T(8,128)}, f32[136,128]{1,0:T(8,128)}, s32[2,16,256]{2,1,0:T(8,128)}) custom-call(f32[2,4,8]{2,1,0:T(4,128)} %camera_ref.1, f32[59,4096]{1,0:T(8,128)} %params_ref.3, s32[2,1,32,128]{3,2,1,0:T(8,128)} %bitcast.10), custom_call_target="tpu_custom_call" | custom-call | tf_op jit(solution)/shard_map/offer/pallas_call | solution.py:939
  11.7 0.0 copy-start.6
  11.7 11.5 %all-to-all-start = ((f32[128,1,1536]{2,1,0:T(1,128)}), f32[128,1,1536]{2,1,0:T(1,128)S(1)}, u32[]{:S(2)}, u32[]{:S(2)}) async-start(f32[128,1,1536]{2,1,0:T(1,128)} %bitcast.9), calls=%async_computation | async-start | bytes 1572864 | tf_op jit(solution)/shard_map/all_to_all | solution.py:917
  23.2 0.0 copy-done.6
  23.2 0.0 copy-start.2
  23.2 0.1 copy.13.target_ref
  23.4 0.0 copy-start.4
  23.4 0.7 copy-done.4
  24.1 0.2 convert_reduce_fusion
  24.3 0.0 copy-start.5
  24.3 0.1 select_reduce_fusion.order_ref
  24.4 0.0 copy-done.2
  24.4 0.6 copy-done.5
  24.9 0.0 copy-start.1
  24.9 6.7 %plan.1 = (f32[2,32,128]{2,1,0:T(8,128)S(1)}, s32[2,64,128]{2,1,0:T(8,128)S(1)}, f32[2,32,128]{2,1,0:T(8,128)S(1)}, f32[2,96,256]{2,1,0:T(8,128)S(1)}) custom-call(s32[2,32]{1,0:T(2,128)S(1)} %select_reduce_fusion.order_ref, s32[2,32]{1,0:T(2,128)S(1)} %copy-done.5, s32[2,32]{1,0:T(2,128)S(1)} %bitcast.7, s32[2,32,256]{2,1,0:T(8,128)S(1)} %copy-done.2, ...), custom_call_target="tpu_custom_call" | custom-call | tf_op jit(solution)/shard_map/plan/pallas_call | solution.py:959
  31.6 8.2 %all-to-all-done = f32[128,1,1536]{2,1,0:T(1,128)S(1)} async-done(((f32[128,1,1536]{2,1,0:T(1,128)}), f32[128,1,1536]{2,1,0:T(1,128)S(1)}, u32[]{:S(2)}, u32[]{:S(2)}) %all-to-all-start) | async-done | bytes 786464 | tf_op jit(solution)/shard_map/all_to_all | solution.py:917
  39.7 0.0 copy-done.1
  39.8 0.0 copy-start
  39.8 33.0 %blend.1 = f32[128,8,128]{2,1,0:T(8,128)S(1)} custom-call(s32[2,32]{1,0:T(2,128)S(1)} %select_reduce_fusion.order_ref, s32[2,32]{1,0:T(2,128)S(1)} %bitcast.8, f32[136,128]{1,0:T(8,128)S(1)} %copy-done.1, f32[1536,128]{1,0:T(8,128)S(1)} %bitcast.5, f32[2,32,128]{2,1,0:T(8,128)S(1)} %get-tuple-element.14.view_ref, ...), custom_call_target="tpu_custom_call" | custom-call | tf_op jit(solution)/shard_map/blend/pallas_call | solution.py:975
  72.7 0.0 copy-start.3
  72.7 19.1 %all_to_all.10.grad_ref = f32[128,8,128]{2,1,0:T(8,128)S(1)} all-to-all(f32[128,8,128]{2,1,0:T(8,128)S(1)} %blend.1), channel_id=1, replica_groups=mesh['dev'=128] {'dev'}, dimensions={0} | all-to-all | bytes 1048576 | tf_op jit(solution)/shard_map/all_to_all | solution.py:917
  91.8 0.0 copy-done
  91.8 0.0 copy-done.3
  91.8 5.5 %param_grads.1 = (f32[59,4096]{1,0:T(8,128)}, f32[1,1]{1,0:T(1,128)}) custom-call(f32[136,128]{1,0:T(8,128)S(1)} %copy-done.1, f32[59,4096]{1,0:T(8,128)S(1)} %copy-done, s32[2,16,256]{2,1,0:T(8,128)S(1)} %copy-done.3, f32[128,8,128]{2,1,0:T(8,128)S(1)} %all_to_all.10.grad_ref), custom_call_target="tpu_custom_call" | custom-call | tf_op jit(solution)/shard_map/param_grads/pallas_call | solution.py:1003
  (1 shorter events, 0.0 us)
Async XLA Ops:
  11.7 11.5 %copy-start.6 = (f32[2,32,3,256]{3,1,2,0:T(8,128)S(1)}, f32[2,32,3,256]{3,1,2,0:T(8,128)}, u32[]{:S(2)}) copy-start(f32[2,32,3,256]{3,1,2,0:T(8,128)} %param.13) | copy-start | bytes 589828
  11.7 28.1 %all-to-all-start = ((f32[128,1,1536]{2,1,0:T(1,128)}), f32[128,1,1536]{2,1,0:T(1,128)S(1)}, u32[]{:S(2)}, u32[]{:S(2)}) async-start(f32[128,1,1536]{2,1,0:T(1,128)} %bitcast.9), calls=%async_computation | async-start | bytes 1572864 | tf_op jit(solution)/shard_map/all_to_all | solution.py:917
  23.2 1.2 %copy-start.2 = (s32[2,32,256]{2,1,0:T(8,128)S(1)}, s32[2,32,256]{2,1,0:T(8,128)}, u32[]{:S(2)}) copy-start(s32[2,32,256]{2,1,0:T(8,128)} %slots_ref.1) | copy-start | bytes 196612
  23.4 0.7 copy-start.4
  24.3 0.7 copy-start.5
  24.9 14.8 %copy-start.1 = (f32[136,128]{1,0:T(8,128)S(1)}, f32[136,128]{1,0:T(8,128)}, u32[]{:S(2)}) copy-start(f32[136,128]{1,0:T(8,128)} %get-tuple-element.11.cam_ref) | copy-start | bytes 208900
  39.8 52.1 %copy-start = (f32[59,4096]{1,0:T(8,128)S(1)}, f32[59,4096]{1,0:T(8,128)}, u32[]{:S(2)}) copy-start(f32[59,4096]{1,0:T(8,128)} %params_ref.3) | copy-start | bytes 2899972
  72.7 19.1 %copy-start.3 = (s32[2,16,256]{2,1,0:T(8,128)S(1)}, s32[2,16,256]{2,1,0:T(8,128)}, u32[]{:S(2)}) copy-start(s32[2,16,256]{2,1,0:T(8,128)} %get-tuple-element.12.send_ref) | copy-start | bytes 98308
